TPU v7x, 512 devices: a whole 4x8x8 slice. The times are simulated.
512 devices in a mesh: slab: 128 (over z, y, core), sub: 4 (over x).
Axes of the slice: x: 4, y: 8, z: 8, core: 2. Of those that a mesh axis runs over, the one named last changes fastest.
Arguments:
- positions: float32 [3, 2097152], P(None, ('slab', 'sub')), may hold values from -5 to 5
- motion: float32 [6, 2097152], P(None, ('slab', 'sub')), may hold values from -3 to 3
- radius: float32 [2097152], P(('slab', 'sub')), may hold values from 0.4 to 0.8
- liquid: float32 [2097152], P(('slab', 'sub')), may hold values from 0.05 to 0.4
- new_owner: int32 [16384], P(('slab', 'sub')), may hold values from 0 to 4095, as said below
- ghost_rows: int32 [3, 262144], P(None, ('slab', 'sub')), may hold values from 0 to 4095
- partner_tiles: int32 [2, 16384], P(None, ('slab', 'sub')), may hold values from 0 to 55
- live_pairs: int32 [16384], P(('slab', 'sub')), may hold values from 0 to 2
Outputs:
- contact_force: float32 [3, 2097152], P(None, ('slab', 'sub'))
- contact_torque: float32 [3, 2097152], P(None, ('slab', 'sub'))
- motion_next: float32 [6, 2097152], P(None, ('slab', 'sub'))
Inputs may be any that keep to these rules, and one draw needn't show every extreme that they name: `new_owner`: within each sub column the entries form a permutation of the 32 * 128 block places; every block stays on its slab or moves to the slab just before or just after; at most 4 blocks of one device go to each neighbouring slab, and in every draw some device sends exactly 4 blocks to the next slab. `ghost_rows`: local particle indices after migration. `partner_tiles`: indices of candidate tiles of the same device.
All inputs are finite; a program needn't handle non-finite values.
Results may differ from a plain program's by a relative error of at most 0.0003.
Values sent between devices are 32-bit elements; how exact they have to be, the bound alone decides.
No kernel may reach another device: no remote copies, remote signals or barrier semaphores. Data moves between devices by JAX's collectives and lax.ppermute only.
A program may use at most 64 MiB of HBM per device.

v0:
```python
import jax
import jax.numpy as jnp
from jax import lax
from jax.sharding import PartitionSpec as P

min_distance = 0.2
stiffness = 1.0
normal_damp = 0.5
shear_damp = 0.3
surface_tension = 2.0
rupture_scale = 1.0
time_step = 0.005


def with_halo(block, sides, width):
    for axis, dim in sides:
        count = lax.axis_size(axis)
        forward = [(i, i + 1) for i in range(count - 1)]
        backward = [(target, source) for source, target in forward]
        low = lax.ppermute(
            lax.slice_in_dim(block, block.shape[dim] - width, None, axis=dim), axis, forward
        )
        high = lax.ppermute(lax.slice_in_dim(block, 0, width, axis=dim), axis, backward)
        block = jnp.concatenate([low, block, high], axis=dim)
    return block


def cross_product(first, second):
    return jnp.stack(
        [
            first[1] * second[2] - first[2] * second[1],
            first[2] * second[0] - first[0] * second[2],
            first[0] * second[1] - first[1] * second[0],
        ]
    )


def contact(center, others, live_mask):
    offset = others[0:3, None, :] - center[0:3, :, None]
    length = jnp.sqrt(jnp.sum(offset * offset, axis=0))
    normal = offset / jnp.maximum(length, min_distance)
    radius_own = center[9][:, None]
    radius_far = others[9][None, :]
    liquid_own = center[10][:, None]
    liquid_far = others[10][None, :]
    intersection = jnp.maximum(radius_own + radius_far - length, 0.0)
    reduced = radius_own * radius_far / (radius_own + radius_far)
    spread = jnp.sqrt(reduced * intersection)
    spins = radius_own[None] * center[6:9, :, None] + radius_far[None] * others[6:9, None, :]
    relative = others[3:6, None, :] - center[3:6, :, None] - cross_product(spins, normal)
    approach = jnp.sum(relative * normal, axis=0)
    sliding = relative - approach[None] * normal
    pressure = stiffness * spread * intersection - normal_damp * spread * approach
    separation = jnp.maximum(length - radius_own - radius_far, 0.0)
    bridge_fill = jnp.maximum(1.0 - separation / (rupture_scale * (liquid_own + liquid_far)), 0.0)
    bridge = (
        surface_tension * reduced * jnp.sqrt(liquid_own * liquid_far) * bridge_fill * bridge_fill
    )
    shear = shear_damp * spread[None] * sliding * live_mask[None, None, :]
    pair_force = ((bridge - pressure) * live_mask[None, :])[None] * normal + shear
    pair_turn = cross_product(normal, shear)
    on_center = jnp.concatenate(
        [jnp.sum(pair_force, axis=2), center[9][None, :] * jnp.sum(pair_turn, axis=2)], 0
    )
    on_others = jnp.concatenate(
        [-jnp.sum(pair_force, axis=1), others[9][None, :] * jnp.sum(pair_turn, axis=1)], 0
    )
    return (on_center, on_others)


def device_forces(candidates, tiles, live_count):
    width = candidates.shape[1]
    partners = tiles.shape[0]
    local_tiles = tiles.shape[1]
    tile_view = candidates.reshape(11, width // 128, 128)
    turns = min(local_tiles, 16)
    group = local_tiles // turns

    def one_turn(turn, carry):
        own_sum, react_sum = carry
        first = (turn * group).astype(jnp.int32)
        center = lax.dynamic_slice_in_dim(tile_view, first, group, 1)
        partner_ids = lax.dynamic_slice_in_dim(tiles, first, group, 1).T
        counts = lax.dynamic_slice_in_dim(live_count, first, group, 0)
        others = jnp.take(tile_view, partner_ids.reshape(-1), axis=1).reshape(
            11, group, partners * 128
        )
        live_mask = (jnp.arange(partners, dtype=jnp.int32)[None, :] < counts[:, None]).astype(
            jnp.float32
        )
        live_mask = jnp.repeat(live_mask, 128, axis=1)
        on_center, on_others = jax.vmap(contact, in_axes=(1, 1, 0))(center, others, live_mask)
        slots = first + jnp.arange(group, dtype=jnp.int32)
        own_sum = own_sum.at[:, slots].add(on_center.transpose(1, 0, 2))
        spread_back = (
            on_others.reshape(group, 6, partners, 128)
            .transpose(1, 0, 2, 3)
            .reshape(6, group * partners, 128)
        )
        react_sum = react_sum.at[:, partner_ids.reshape(-1)].add(spread_back)
        return (own_sum, react_sum)

    start = (
        jnp.zeros((6, local_tiles, 128), jnp.float32),
        jnp.zeros((6, width // 128, 128), jnp.float32),
    )
    own_sum, react_sum = lax.fori_loop(0, turns, one_turn, start)
    return (own_sum.reshape(6, local_tiles * 128), react_sum.reshape(6, width))


def body(positions, motion, radius, liquid, new_owner, ghost_rows, partner_tiles, live_pairs):
    states = jnp.concatenate([positions, motion, radius[None], liquid[None]], 0)
    per_dev = states.shape[1]
    blocks_dev = per_dev // 128
    ghost_len = ghost_rows.shape[1]
    here = lax.axis_index("slab")
    owner_tag = jnp.repeat((new_owner + 1).astype(jnp.float32), 128)
    tagged = jnp.concatenate([states, owner_tag[None]], 0)
    wanted = here * blocks_dev + jnp.arange(blocks_dev, dtype=jnp.int32) + 1
    border = with_halo(tagged, (("slab", 1),), per_dev)
    arrivals = border.reshape(12, 3 * blocks_dev, 128)
    arrival_tags = arrivals[11, :, 0].astype(jnp.int32)
    picked = jnp.argmax(arrival_tags[None, :] == wanted[:, None], axis=1)
    migrated = jnp.take(arrivals[:11], picked, axis=1).reshape(11, per_dev)
    ghosts = jnp.take(migrated, ghost_rows, axis=1)
    layers = with_halo(jnp.concatenate([ghosts[:, 0], ghosts[:, 1]], 1), (("slab", 1),), ghost_len)
    shared = lax.all_gather(ghosts[:, 2], "sub", axis=1, tiled=True)
    candidates = jnp.concatenate(
        [migrated, layers[:, :ghost_len], layers[:, 3 * ghost_len :], shared], 1
    )
    own_sum, react_sum = device_forces(candidates, partner_tiles, live_pairs)
    totals = own_sum + react_sum[:, :per_dev]
    returned = with_halo(react_sum[:, per_dev : per_dev + 2 * ghost_len], (("slab", 1),), ghost_len)
    returned_shared = lax.psum_scatter(
        react_sum[:, per_dev + 2 * ghost_len :], "sub", scatter_dimension=1, tiled=True
    )
    totals = totals.at[:, ghost_rows[0]].add(returned[:, :ghost_len])
    totals = totals.at[:, ghost_rows[1]].add(returned[:, 3 * ghost_len :])
    totals = totals.at[:, ghost_rows[2]].add(returned_shared)
    radii = migrated[9]
    mass = radii**3
    inertia = 0.4 * radii**5
    velocity = migrated[3:6] + time_step * totals[0:3] / mass[None, :]
    spin_next = migrated[6:9] + time_step * totals[3:6] / inertia[None, :]
    return (totals[0:3], totals[3:6], jnp.concatenate([velocity, spin_next], 0))


def solution(mesh):
    return jax.shard_map(
        body,
        mesh=mesh,
        in_specs=(
            P(None, ("slab", "sub")),
            P(None, ("slab", "sub")),
            P(("slab", "sub")),
            P(("slab", "sub")),
            P(("slab", "sub")),
            P(None, ("slab", "sub")),
            P(None, ("slab", "sub")),
            P(("slab", "sub")),
        ),
        out_specs=(P(None, ("slab", "sub")), P(None, ("slab", "sub")), P(None, ("slab", "sub"))),
        check_vma=False,
    )
```

profile of v0, /device:TPU:8, one launch (start us, length us, event | category | flops | bytes accessed | tf_op | source)
XLA Modules:
  0.0 194.3 jit_solution(17635807034207438304)
XLA Ops:
  7.2 0.7 add_convert_fusion
  7.9 2.7 %concatenate.26 = f32[12,4096]{1,0:T(8,128)S(1)} concatenate(f32[3,4096]{1,0:T(4,128)} %param.10, f32[6,4096]{1,0:T(8,128)} %param.11, f32[1,4096]{1,0:T(1,128)} %bitcast.185, f32[1,4096]{1,0:T(1,128)} %bitcast.186, f32[1,4096]{1,0:T(1,128)S(1)} %bitcast.182), dimensions={0} | concatenate | bytes 393216 | tf_op jit(solution)/shard_map/concatenate | solution.py:118
  10.7 1.9 collective-permute-start.1
  12.6 2.4 %collective-permute-start = (f32[12,4096]{1,0:T(8,128)S(1)}, f32[12,4096]{1,0:T(8,128)S(1)}, u32[]{:S(2)}, u32[]{:S(2)}) collective-permute-start(f32[12,4096]{1,0:T(8,128)S(1)} %concatenate.26), channel_id=1, source_target_pairs={{0,4},{4,8},{8,12},{12,16},{16,20},{20,24},{24,28},{28,32},{32,36}... | collective-permute-start | bytes 589832 | tf_op jit(solution)/shard_map/ppermute | solution.py:20
  15.0 0.8 compare_select_fusion.4
  15.9 0.7 compare_select_fusion.3
  16.6 0.7 compare_and_fusion.1
  17.3 7.2 %collective-permute-done = f32[12,4096]{1,0:T(8,128)S(1)} collective-permute-done((f32[12,4096]{1,0:T(8,128)S(1)}, f32[12,4096]{1,0:T(8,128)S(1)}, u32[]{:S(2)}, u32[]{:S(2)}) %collective-permute-start) | collective-permute-done | bytes 196640 | tf_op jit(solution)/shard_map/ppermute | solution.py:20
  24.8 0.7 iota_reduce_fusion
  26.9 2.0 %copy.179 = f32[11,32,128]{0,2,1:T(8,128)} copy(f32[11,32,128]{2,0,1:T(8,128)S(1)} %bitcast.165) | data formatting | bytes 360448 | tf_op jit(solution)/shard_map/jit(_take)/gather | solution.py:124
  28.9 3.6 %bitcast_select_fusion = f32[11,4096]{0,1:T(8,128)S(1)} fusion(f32[11,32,128]{0,2,1:T(8,128)} %copy.179, pred[4096]{0:T(1024)(128)(4,1)S(1)} %broadcast_bitcast_fusion.1), kind=kLoop, calls=%fused_computation.67 | loop fusion | flops 45056 | bytes 364544 | tf_op jit(solution)/shard_map/jit(_take)/select_n | solution.py:124
  32.6 0.6 copy.171
  33.2 2.6 %gather_fusion.2 = f32[1536,11]{1,0:T(8,128)S(1)} fusion(f32[11,4096]{0,1:T(8,128)S(1)} %bitcast_select_fusion, s32[2048]{0:T(1024)S(1)} %pad_clamp_fusion.1), kind=kCustom, calls=%fused_computation.2 | custom fusion | bytes 141312 | tf_op jit(solution)/shard_map/jit(_take)/gather | solution.py:125
  36.1 1.9 collective-permute-start.2
  38.0 3.6 %collective-permute-start.3 = (f32[11,512]{1,0:T(8,128)S(1)}, f32[11,512]{1,0:T(8,128)S(1)}, u32[]{:S(2)}, u32[]{:S(2)}) collective-permute-start(f32[11,512]{1,0:T(8,128)S(1)} %get-tuple-element.213), channel_id=1, source_target_pairs={{4,0},{8,4},{12,8},{16,12},{20,16},{24,20},{28,24},{32,28},{36,32}... | collective-permute-start | bytes 67592 | tf_op jit(solution)/shard_map/ppermute | solution.py:23
  41.7 12.0 %all-gather = f32[11,1,2048]{2,0,1:T(8,128)S(1)} all-gather(f32[11,1,512]{2,0,1:T(8,128)S(1)} %get-tuple-element.212), channel_id=2, replica_groups=mesh['slab'=128,'sub'=4] {'sub'}, dimensions={2}, use_global_device_ids=true | all-gather | bytes 112640 | tf_op jit(solution)/shard_map/all_gather | solution.py:127
  54.0 82.5 %while.15 = (s32[]{:T(128)}, f32[6,32,128]{2,0,1:T(8,128)S(1)}, f32[6,56,128]{2,0,1:T(8,128)S(1)}, f32[11,56,128]{2,0,1:T(8,128)S(1)}, s32[2,32]{1,0:T(2,128)S(1...) while((s32[]{:T(128)}, f32[6,32,128]{2,0,1:T(8,128)S(1)}, ...), condition=%wide.region_10.11_spmd, body=%wide.region_1.10_spmd.sunk | while | flops 9061440 | bytes 13678168 | solution.py:107
  57.9 0.6 scatter_fusion
  58.5 0.6 scatter_fusion.1
  63.0 0.6 scatter_fusion
  63.6 0.6 scatter_fusion.1
  68.2 0.6 scatter_fusion
  68.8 0.6 scatter_fusion.1
  73.3 0.6 scatter_fusion
  74.0 0.6 scatter_fusion.1
  78.5 0.6 scatter_fusion
  79.1 0.6 scatter_fusion.1
  83.7 0.6 scatter_fusion
  84.3 0.6 scatter_fusion.1
  88.8 0.6 scatter_fusion
  89.4 0.6 scatter_fusion.1
  94.0 0.6 scatter_fusion
  94.6 0.6 scatter_fusion.1
  99.1 0.6 scatter_fusion
  99.7 0.6 scatter_fusion.1
  104.3 0.6 scatter_fusion
  104.9 0.6 scatter_fusion.1
  109.4 0.6 scatter_fusion
  110.0 0.6 scatter_fusion.1
  114.6 0.6 scatter_fusion
  115.2 0.6 scatter_fusion.1
  119.7 0.6 scatter_fusion
  120.3 0.6 scatter_fusion.1
  124.9 0.6 scatter_fusion
  125.5 0.6 scatter_fusion.1
  130.0 0.6 scatter_fusion
  130.7 0.6 scatter_fusion.1
  135.8 0.6 scatter_fusion.1
  136.5 2.4 %copy.175 = f32[6,56,128]{0,2,1:T(8,128)} copy(f32[6,56,128]{2,0,1:T(8,128)S(1)} %get-tuple-element.116) | data formatting | bytes 344064 | tf_op jit(solution)/shard_map/while | solution.py:107
  138.9 1.1 fusion.24
  140.0 2.3 %slice.275 = f32[6,2048]{0,1:T(8,128)} slice(f32[6,7168]{0,1:T(8,128)} %bitcast.155), slice={[0:6], [5120:7168]} | slice | bytes 98304 | tf_op jit(solution)/shard_map/slice | solution.py:135
  142.3 2.0 %copy.174 = f32[6,32,128]{0,2,1:T(8,128)} copy(f32[6,32,128]{2,0,1:T(8,128)S(1)} %get-tuple-element.115) | data formatting | bytes 196608 | tf_op jit(solution)/shard_map/while | solution.py:107
  144.3 1.9 collective-permute-start.5
  146.2 2.4 %collective-permute-start.4 = (f32[6,512]{0,1:T(8,128)S(1)}, f32[6,512]{0,1:T(8,128)S(1)}, u32[]{:S(2)}, u32[]{:S(2)}) collective-permute-start(f32[6,512]{0,1:T(8,128)S(1)} %get-tuple-element.206), channel_id=1, source_target_pairs={{0,4},{4,8},{8,12},{12,16},{16,20},{20,24},{24,28},{28,32},{32,36}... | collective-permute-start | bytes 36872 | tf_op jit(solution)/shard_map/ppermute | solution.py:20
  148.6 2.4 %slice_add_fusion = f32[6,4096]{0,1:T(8,128)S(1)} fusion(f32[6,7168]{0,1:T(8,128)} %bitcast.156, f32[6,32,128]{0,2,1:T(8,128)} %copy.174), kind=kLoop, calls=%fused_computation.66 | loop fusion | flops 24576 | bytes 294912 | tf_op jit(solution)/shard_map/add | solution.py:132
  151.0 2.8 %collective-permute-done.4 = f32[6,512]{0,1:T(8,128)S(1)} collective-permute-done((f32[6,512]{0,1:T(8,128)S(1)}, f32[6,512]{0,1:T(8,128)S(1)}, u32[]{:S(2)}, u32[]{:S(2)}) %collective-permute-start.4) | collective-permute-done | bytes 12320 | tf_op jit(solution)/shard_map/ppermute | solution.py:20
  153.9 4.1 %scatter_custom_fusion.2 = f32[6,4096]{0,1:T(8,128)S(1)} fusion(f32[6,4096]{0,1:T(8,128)S(1)} %slice_add_fusion, s32[512]{0:T(512)S(1)} %bitcast.190, f32[6,512]{0,1:T(8,128)S(1)} %collective-permute-done.4), kind=kCustom, calls=%fused_computation.74 | custom fusion | flops 3072 | bytes 360448 | tf_op jit(solution)/shard_map/scatter-add | solution.py:137
  158.0 4.3 %scatter_custom_fusion.3 = f32[6,4096]{0,1:T(8,128)S(1)} fusion(f32[6,4096]{0,1:T(8,128)S(1)} %scatter_custom_fusion.2, s32[512]{0:T(512)S(1)} %bitcast.189, f32[6,512]{0,1:T(8,128)S(1)} %collective-permute-done.5), kind=kCustom, calls=%fused_computation.72 | custom fusion | flops 3072 | bytes 360448 | tf_op jit(solution)/shard_map/scatter-add | solution.py:138
  162.2 14.5 %reduce-scatter.2.cloned.1.call-done = f32[6,512]{0,1:T(8,128)} async-done(((f32[6,2048]{0,1:T(8,128)}), f32[6,512]{0,1:T(8,128)}) %reduce-scatter.2.cloned.1.call-update) | async-done | bytes 12304 | tf_op jit(solution)/shard_map/reduce_scatter | solution.py:134
  176.7 4.5 %scatter_custom_fusion.4 = f32[6,4096]{0,1:T(8,128)S(1)} fusion(f32[6,4096]{0,1:T(8,128)S(1)} %scatter_custom_fusion.3, s32[512]{0:T(512)S(1)} %bitcast.188, f32[6,512]{0,1:T(8,128)} %reduce-scatter.2.cloned.1.call-done), kind=kCustom, calls=%fused_computation.70 | custom fusion | flops 3072 | bytes 110592 | tf_op jit(solution)/shard_map/scatter-add | solution.py:139
  181.2 2.6 %fusion.25 = (f32[3,4096]{0,1:T(8,128)}, f32[3,4096]{0,1:T(8,128)}) fusion(f32[6,4096]{0,1:T(8,128)S(1)} %scatter_custom_fusion.4), kind=kLoop, calls=%fused_computation.105 | loop fusion | bytes 196608 | tf_op jit(solution)/shard_map/slice | solution.py:145
  183.7 2.4 %copy.187 = f32[3,4096]{1,0:T(4,128)S(1)} copy(f32[3,4096]{0,1:T(8,128)} %get-tuple-element.207) | data formatting | bytes 98304
  186.1 0.6 copy.186
  186.8 0.7 pad_maximum_fusion.5
  (799 shorter events, 61.6 us)
Async XLA Ops:
  7.2 169.5 %reduce-scatter.2.cloned.1.call-start = ((), (), s32[]{:S(2)}) async-start(), calls=%async_computation.1 | async-start | bytes 1310720 | tf_op jit(solution)/shard_map/reduce_scatter | solution.py:134
  10.7 6.6 %collective-permute-start.1 = (f32[12,4096]{1,0:T(8,128)S(1)}, f32[12,4096]{1,0:T(8,128)S(1)}, u32[]{:S(2)}, u32[]{:S(2)}) collective-permute-start(f32[12,4096]{1,0:T(8,128)S(1)} %concatenate.26), channel_id=1, source_target_pairs={{4,0},{8,4},{12,8},{16,12},{20,16},{24,20},{28,24},{32,28},{36,32}... | collective-permute-start | bytes 589832 | tf_op jit(solution)/shard_map/ppermute | solution.py:23
  12.6 11.9 %collective-permute-start = (f32[12,4096]{1,0:T(8,128)S(1)}, f32[12,4096]{1,0:T(8,128)S(1)}, u32[]{:S(2)}, u32[]{:S(2)}) collective-permute-start(f32[12,4096]{1,0:T(8,128)S(1)} %concatenate.26), channel_id=1, source_target_pairs={{0,4},{4,8},{8,12},{12,16},{16,20},{20,24},{24,28},{28,32},{32,36}... | collective-permute-start | bytes 589832 | tf_op jit(solution)/shard_map/ppermute | solution.py:20
  36.0 17.9 %copy-start.3 = (s32[2,32]{1,0:T(2,128)S(1)}, s32[2,32]{1,0:T(2,128)}, u32[]{:S(2)}) copy-start(s32[2,32]{1,0:T(2,128)} %param.16) | copy-start | bytes 772
  36.0 17.9 %copy-start.4 = (s32[32]{0:T(128)S(1)}, s32[32]{0:T(128)}, u32[]{:S(2)}) copy-start(s32[32]{0:T(128)} %param.17) | copy-start | bytes 388
  36.1 17.6 %collective-permute-start.2 = (f32[11,512]{1,0:T(8,128)S(1)}, f32[11,512]{1,0:T(8,128)S(1)}, u32[]{:S(2)}, u32[]{:S(2)}) collective-permute-start(f32[11,512]{1,0:T(8,128)S(1)} %get-tuple-element.211), channel_id=1, source_target_pairs={{0,4},{4,8},{8,12},{12,16},{16,20},{20,24},{24,28},{28,32},{32,36}... | collective-permute-start | bytes 67592 | tf_op jit(solution)/shard_map/ppermute | solution.py:20
  38.0 15.7 %collective-permute-start.3 = (f32[11,512]{1,0:T(8,128)S(1)}, f32[11,512]{1,0:T(8,128)S(1)}, u32[]{:S(2)}, u32[]{:S(2)}) collective-permute-start(f32[11,512]{1,0:T(8,128)S(1)} %get-tuple-element.213), channel_id=1, source_target_pairs={{4,0},{8,4},{12,8},{16,12},{20,16},{24,20},{28,24},{32,28},{36,32}... | collective-permute-start | bytes 67592 | tf_op jit(solution)/shard_map/ppermute | solution.py:23
  144.3 13.7 %collective-permute-start.5 = (f32[6,512]{0,1:T(8,128)S(1)}, f32[6,512]{0,1:T(8,128)S(1)}, u32[]{:S(2)}, u32[]{:S(2)}) collective-permute-start(f32[6,512]{0,1:T(8,128)S(1)} %get-tuple-element.205), channel_id=1, source_target_pairs={{4,0},{8,4},{12,8},{16,12},{20,16},{24,20},{28,24},{32,28},{36,32}... | collective-permute-start | bytes 36872 | tf_op jit(solution)/shard_map/ppermute | solution.py:23
  146.2 7.7 %collective-permute-start.4 = (f32[6,512]{0,1:T(8,128)S(1)}, f32[6,512]{0,1:T(8,128)S(1)}, u32[]{:S(2)}, u32[]{:S(2)}) collective-permute-start(f32[6,512]{0,1:T(8,128)S(1)} %get-tuple-element.206), channel_id=1, source_target_pairs={{0,4},{4,8},{8,12},{12,16},{16,20},{20,24},{24,28},{28,32},{32,36}... | collective-permute-start | bytes 36872 | tf_op jit(solution)/shard_map/ppermute | solution.py:20
  183.7 2.4 %copy-start = (f32[3,4096]{0,1:T(8,128)S(1)}, f32[3,4096]{0,1:T(8,128)}, u32[]{:S(2)}) copy-start(f32[3,4096]{0,1:T(8,128)} %get-tuple-element.208) | copy-start | bytes 147460
  186.1 1.4 copy-start.1
  186.7 0.8 copy-start.2
Sparse Core Ops, SparseCore 0:
  144.4 32.2 reduce-scatter.1
where the time goes:
time: 195 us; the launch traced here: 194 us
  other arithmetic  83 us (43%)
  local copies, waits for them, and re-layouts  42.3 us (22%)
  waiting for transfers between devices  24.5 us (13%)
  starting transfers between devices  14.3 us (7%)
  between operations  14.3 us (7%)
  blocking collectives  12 us (6%)
  loops' own time  4.01 us (2%)
    reduce_scatter x1, waiting for transfers between devices, body(): lax.psum_scatter(react_sum[:, per_dev + 2 * ghost_len:], 'sub', scatter_d...  14.5 us
    all_gather x1, blocking collectives, body(): shared = lax.all_gather(ghosts[:, 2], 'sub', axis=1, tiled=True)  12 us
    scatter-add x16, other arithmetic, one_turn(): react_sum = react_sum.at[:, partner_ids.reshape(-1)].add(spread_back)  10.3 us
    ppermute x3, waiting for transfers between devices, with_halo(): lax.ppermute(lax.slice_in_dim(block, block.shape[dim] - width, None, axis...  10 us
    scatter-add x16, other arithmetic, one_turn(): own_sum = own_sum.at[:, slots].add(on_center.transpose(1, 0, 2))  9.64 us
    gather x16, local copies, waits for them, and re-layouts, one_turn(): jnp.take(tile_view, partner_ids.reshape(-1), axis=1)  8.81 us
    reduce_sum x16, other arithmetic, contact(): jnp.sum(pair_force, axis=1)  8.56 us
    mul x16, other arithmetic, contact(): shear = shear_damp * spread[None] * sliding * live_mask[None, None, :]  7.68 us
  transfers between devices with their start and end apart: 7, of which 3 were waited for; matrix products, arithmetic and copies ran while one was open for 7% of the time, Pallas kernels for 0%

commit v1 on v0

v1 whole, which is shorter than its diff:
```python
import functools

import jax
import jax.numpy as jnp
from jax import lax
from jax.experimental import pallas as pl
from jax.experimental.pallas import tpu as pltpu
from jax.sharding import PartitionSpec as P

min_distance = 0.2
stiffness = 1.0
normal_damp = 0.5
shear_damp = 0.3
surface_tension = 2.0
rupture_scale = 1.0
time_step = 0.005

LANES = 128
ROWS = 16
CAP = 4
FEATS = 16
MATS = 5

f32 = jnp.float32
bf16 = jnp.bfloat16
VMEM = pl.BlockSpec(memory_space=pltpu.VMEM)
SMEM = pl.BlockSpec(memory_space=pltpu.SMEM)
PARAMS = pltpu.CompilerParams(vmem_limit_bytes=40 * 1024 * 1024)


def split(value, parts):
    out = []
    for _ in range(parts - 1):
        high = value.astype(bf16)
        out.append(high)
        value = value - high.astype(f32)
    out.append(value.astype(bf16))
    return out


def dot_nn(left, right):
    return lax.dot_general(left, right, (((1,), (0,)), ((), ())), preferred_element_type=f32)


def dot_nt(left, right):
    return lax.dot_general(left, right, (((1,), (1,)), ((), ())), preferred_element_type=f32)


def pack_kernel(owner, positions, motion, radius, liquid, state, ahead, behind):
    here = lax.axis_index("slab")
    blocks = state.shape[0]
    ahead[...] = jnp.zeros_like(ahead)
    behind[...] = jnp.zeros_like(behind)
    count_ahead = jnp.int32(0)
    count_behind = jnp.int32(0)
    for block in range(blocks):
        columns = slice(block * LANES, (block + 1) * LANES)
        place = owner[block]
        state[block, 0:3, :] = positions[:, columns]
        state[block, 3:9, :] = motion[:, columns]
        state[block, 9:10, :] = radius[block : block + 1, :]
        state[block, 10:11, :] = liquid[block : block + 1, :]
        state[block, 11:16, :] = jnp.full((5, LANES), (place + 1).astype(f32), f32)
        slab = place // blocks
        goes_ahead = slab == here + 1
        goes_behind = slab == here - 1

        @pl.when(goes_ahead)
        def _():
            ahead[count_ahead] = state[block]

        @pl.when(goes_behind)
        def _():
            behind[count_behind] = state[block]

        count_ahead = jnp.minimum(count_ahead + goes_ahead.astype(jnp.int32), CAP - 1)
        count_behind = jnp.minimum(count_behind + goes_behind.astype(jnp.int32), CAP - 1)


def place_kernel(owner, state, low, high, rows, migrated, ghosts0, ghosts1, ghosts2):
    here = lax.axis_index("slab")
    blocks = state.shape[0]
    for block in range(blocks):
        place = owner[block]

        @pl.when(place // blocks == here)
        def _():
            migrated[place % blocks] = state[block]

    base = (here * blocks + 1).astype(f32)
    arrived = [low[slot] for slot in range(CAP)] + [high[slot] for slot in range(CAP)]
    tags = [jnp.broadcast_to(block[11:12, :], (ROWS, LANES)) - base for block in arrived]
    for slot in range(blocks):
        current = migrated[slot]
        for block, tag in zip(arrived, tags):
            current = jnp.where(tag == float(slot), block, current)
        migrated[slot] = current

    flat = migrated[...].reshape(blocks * ROWS, LANES)
    left = jnp.concatenate(split(flat, 3), axis=1)
    lane_ids = lax.broadcasted_iota(jnp.int32, (LANES, LANES), 0)
    for which, ghosts in enumerate((ghosts0, ghosts1, ghosts2)):
        for tile in range(ghosts.shape[0]):
            index = rows[which : which + 1, tile * LANES : (tile + 1) * LANES]
            hot = jnp.where(lane_ids == index % LANES, 1.0, 0.0).astype(bf16)
            picked = dot_nn(left, jnp.concatenate([hot, hot, hot], axis=0))
            source = jnp.broadcast_to(index // LANES, (ROWS, LANES))
            total = jnp.zeros((ROWS, LANES), f32)
            for block in range(blocks):
                total = jnp.where(source == block, picked[block * ROWS : (block + 1) * ROWS], total)
            ghosts[tile] = total


def cross(first, second):
    return [
        first[1] * second[2] - first[2] * second[1],
        first[2] * second[0] - first[0] * second[2],
        first[0] * second[1] - first[1] * second[0],
    ]


def recip(value):
    guess = pl.reciprocal(value, approx=True)
    return guess * (2.0 - value * guess)


def prepare(tile, scaled, feats, slot):
    rows = [tile[row : row + 1, :] for row in range(11)]
    place, velocity, spin = rows[0:3], rows[3:6], rows[6:9]
    radius, liquid = rows[9], rows[10]
    turn = [radius * part for part in spin]
    bond = radius * jnp.sqrt(surface_tension * liquid)
    one = jnp.ones((1, LANES), f32)
    zero = jnp.zeros((1, LANES), f32)
    scaled[slot] = jnp.concatenate(
        place + velocity + turn + [radius, liquid, bond, zero, zero, zero, zero], axis=0
    )
    features = jnp.concatenate(
        place + [one] + velocity + turn + cross(turn, place) + cross(place, velocity), axis=0
    )
    feats[slot] = jnp.concatenate(split(features, 3), axis=0)


def add_pair(first, second, scaled, feats, sums, coefs):
    near = scaled[first].T
    far = scaled[second]
    far_rows = [far[row : row + 1, :] for row in range(12)]
    step = 16
    for start in range(0, LANES, step):
        center = near[start : start + step]
        col = [center[:, row : row + 1] for row in range(12)]
        offset = [far_rows[row] - col[row] for row in range(3)]
        moving = [far_rows[row] - col[row] for row in range(3, 6)]
        turning = [far_rows[row] + col[row] for row in range(6, 9)]
        square = offset[0] * offset[0] + offset[1] * offset[1] + offset[2] * offset[2]
        along = offset[0] * moving[0] + offset[1] * moving[1] + offset[2] * moving[2]
        twist = offset[0] * turning[0] + offset[1] * turning[1] + offset[2] * turning[2]
        root = lax.rsqrt(jnp.maximum(square, 1e-30))
        length = square * root
        inverse = jnp.minimum(root, 1.0 / min_distance)
        radii = far_rows[9] + col[9]
        gap = length - radii
        overlap = jnp.maximum(-gap, 0.0)
        apart = jnp.maximum(gap, 0.0)
        over_radii = recip(radii)
        inner = far_rows[9] * col[9] * over_radii * overlap
        spread = inner * lax.rsqrt(jnp.maximum(inner, 1e-30))
        fill = jnp.maximum(1.0 - apart * recip(rupture_scale * (far_rows[10] + col[10])), 0.0)
        bridge = far_rows[11] * col[11] * over_radii * (fill * fill)
        approach = along * inverse
        shear = shear_damp * spread
        push = stiffness * overlap - (normal_damp - shear_damp) * approach
        shear_inv = shear * inverse
        shear_inv2 = shear_inv * inverse
        mats = [
            (bridge - spread * push) * inverse,
            shear,
            shear_inv,
            shear_inv2 * square,
            shear_inv2 * twist,
        ]
        for index, mat in enumerate(mats):
            high, low = split(mat, 2)
            coefs[index * LANES + start : index * LANES + start + step, 0:LANES] = high
            coefs[index * LANES + start : index * LANES + start + step, LANES:] = low
    far_feats = feats[second]
    own = dot_nt(jnp.concatenate([far_feats, far_feats], axis=1), coefs[...])
    own = own[0:FEATS] + own[FEATS : 2 * FEATS] + own[2 * FEATS :]
    near_feats = feats[first]
    own_base = pl.multiple_of(first * (MATS * FEATS), 16)
    far_base = pl.multiple_of(second * (MATS * FEATS), 16)
    for index in range(MATS):
        sums[pl.ds(own_base + index * FEATS, FEATS), :] += own[:, index * LANES : (index + 1) * LANES]
    for index in range(MATS):
        back = dot_nn(near_feats, coefs[index * LANES : (index + 1) * LANES, :])
        back = back[:, 0:LANES] + back[:, LANES:]
        back = back[0:FEATS] + back[FEATS : 2 * FEATS] + back[2 * FEATS :]
        if index == MATS - 1:
            back = -back
        sums[pl.ds(far_base + index * FEATS, FEATS), :] += back


def finish(group, sums, scaled):
    span = MATS * FEATS

    def total(mat, feat):
        return sums[pl.ds(group * 8 * span + mat * FEATS + feat, 8, stride=span), :]

    def own(row):
        return scaled[pl.ds(group * 8, 8), row, :]

    place = [own(row) for row in range(3)]
    velocity = [own(row) for row in range(3, 6)]
    turn = [own(row) for row in range(6, 9)]
    radius = own(9)
    s_place = [total(0, feat) for feat in range(3)]
    s_one = total(0, 3)
    c_one = total(1, 3)
    c_velocity = [total(1, feat) for feat in range(4, 7)]
    n_place = [total(2, feat) for feat in range(3)]
    n_one = total(2, 3)
    n_velocity = [total(2, feat) for feat in range(4, 7)]
    n_turn = [total(2, feat) for feat in range(7, 10)]
    n_turn_place = [total(2, feat) for feat in range(10, 13)]
    n_place_velocity = [total(2, feat) for feat in range(13, 16)]
    k_one = total(3, 3)
    k_turn = [total(3, feat) for feat in range(7, 10)]
    g_place = [total(4, feat) for feat in range(3)]
    g_one = total(4, 3)
    turn_place = cross(turn, place)
    place_velocity = cross(place, velocity)
    first = cross(turn, n_place)
    second = cross(n_turn, place)
    third = cross(n_place, velocity)
    fourth = cross(place, n_velocity)
    force = [
        (s_place[x] - place[x] * s_one)
        + (c_velocity[x] - velocity[x] * c_one)
        - (first[x] - turn_place[x] * n_one + n_turn_place[x] - second[x])
        for x in range(3)
    ]
    torque = [
        radius
        * (
            (n_place_velocity[x] - third[x] - fourth[x] + place_velocity[x] * n_one)
            - (turn[x] * k_one + k_turn[x])
            + (g_place[x] - place[x] * g_one)
        )
        for x in range(3)
    ]
    return force + torque


def pair_kernel(remote, partners, live, state, *rest):
    blocks = state.shape[0]
    if remote:
        buffers, rest = rest[:6], rest[6:]
        totals, returns = rest[0], rest[1:7]
        scaled, feats, sums, coefs, todo = rest[7:]
    else:
        totals, scaled, feats, sums, coefs, todo = rest
    tiles = scaled.shape[0]
    sums[...] = jnp.zeros_like(sums)
    for tile in range(blocks):
        prepare(state[tile], scaled, feats, tile)
    if remote:
        size = buffers[0].shape[0]
        for which, buffer in enumerate(buffers):
            for tile in range(size):
                prepare(buffer[tile], scaled, feats, blocks + which * size + tile)
        sub = lax.axis_index("sub")
        subs = lax.axis_size("sub")
    count = jnp.int32(0)
    for tile in range(blocks):
        for which in range(partners.shape[0]):
            partner = partners[which, tile]
            slot = partner
            if remote:
                shared = (partner - blocks) // size - 2
                shift = lax.rem(sub - shared + 2 * subs, subs)
                slot = jnp.where(shared >= 0, partner + (shift - shared) * size, partner)
                wanted = (which < live[tile]) & (partner >= blocks)
            else:
                wanted = (which < live[tile]) & (partner < blocks)
            todo[count] = tile * 64 + slot
            count = count + wanted.astype(jnp.int32)

    def one_pair(index, carry):
        entry = todo[index]
        add_pair(entry // 64, entry % 64, scaled, feats, sums, coefs)
        return carry

    lax.fori_loop(0, count, one_pair, 0)
    for group in range(tiles // 8):
        for row, value in enumerate(finish(group, sums, scaled)):
            if group < blocks // 8:
                totals[pl.ds(group * 64 + row, 8, stride=8), :] = value
            else:
                which = (group - blocks // 8) * 2
                for part in range(2):
                    returns[which + part][:, row, :] = value[part * size : (part + 1) * size]


def final_kernel(
    state, totals_near, totals_far, rows, ret0, ret1, sub0, sub1, sub2, sub3, force, torque, kicked
):
    blocks = state.shape[0]
    size = ret0.shape[0]
    lane_ids = lax.broadcasted_iota(jnp.int32, (LANES, LANES), 0)
    hots = []
    lefts = []
    for which in range(3):
        for tile in range(size):
            index = rows[which : which + 1, tile * LANES : (tile + 1) * LANES]
            hots.append(jnp.where(lane_ids == index % LANES, 1.0, 0.0).astype(bf16))
            if which == 0:
                value = ret0[tile]
            elif which == 1:
                value = ret1[tile]
            else:
                value = sub0[tile] + sub1[tile] + sub2[tile] + sub3[tile]
            high = value.astype(bf16).astype(f32)
            both = jnp.concatenate([high, value - high], axis=0)
            source = jnp.broadcast_to(index // LANES, (ROWS, LANES))
            lefts.append(
                jnp.concatenate(
                    [
                        jnp.where(source == block, both, 0.0).astype(bf16)
                        for block in range(blocks)
                    ],
                    axis=0,
                )
            )
    added = dot_nt(jnp.concatenate(lefts, axis=1), jnp.concatenate(hots, axis=1))
    row_ids = lax.broadcasted_iota(jnp.int32, (8, LANES), 0)
    for block in range(blocks):
        columns = slice(block * LANES, (block + 1) * LANES)
        extra = added[block * ROWS : block * ROWS + 8] + added[block * ROWS + 8 : block * ROWS + 16]
        part = slice(block * 8, block * 8 + 8)
        total = totals_near[part, :] + totals_far[part, :] + extra
        radius = state[block, 9:10, :]
        mass = radius * radius * radius
        inertia = 0.4 * mass * radius * radius
        weight = jnp.where(row_ids < 3, time_step / mass, time_step / inertia)
        force[:, columns] = total[0:3]
        torque[:, columns] = total[3:6]
        kicked[:, columns] = state[block, 3:9, :] + (total * weight)[0:6]


def shape(*dims, dtype=f32):
    return jax.ShapeDtypeStruct(dims, dtype)


def pair_scratch(tiles, pairs):
    return [
        pltpu.VMEM((tiles, ROWS, LANES), f32),
        pltpu.VMEM((tiles, 3 * FEATS, LANES), bf16),
        pltpu.VMEM((tiles * MATS * FEATS, LANES), f32),
        pltpu.VMEM((MATS * LANES, 2 * LANES), bf16),
        pltpu.SMEM((pairs + 1,), jnp.int32),
    ]


def body(positions, motion, radius, liquid, new_owner, ghost_rows, partner_tiles, live_pairs):
    per_dev = positions.shape[1]
    blocks = per_dev // LANES
    size = ghost_rows.shape[1] // LANES
    pairs = partner_tiles.shape[0] * blocks
    slabs = lax.axis_size("slab")
    subs = lax.axis_size("sub")
    up = [(i, i + 1) for i in range(slabs - 1)]
    down = [(i + 1, i) for i in range(slabs - 1)]
    around = [[(i, (i + d) % subs) for i in range(subs)] for d in range(subs)]
    against = [[(i, (i - d) % subs) for i in range(subs)] for d in range(subs)]

    state, ahead, behind = pl.pallas_call(
        pack_kernel,
        out_shape=(
            shape(blocks, ROWS, LANES),
            shape(CAP, ROWS, LANES),
            shape(CAP, ROWS, LANES),
        ),
        in_specs=[SMEM] + [VMEM] * 4,
        out_specs=(VMEM,) * 3,
        compiler_params=PARAMS,
        name="pack",
    )(
        new_owner,
        positions,
        motion,
        radius.reshape(blocks, LANES),
        liquid.reshape(blocks, LANES),
    )
    low = lax.ppermute(ahead, "slab", up)
    high = lax.ppermute(behind, "slab", down)
    migrated, ghosts0, ghosts1, ghosts2 = pl.pallas_call(
        place_kernel,
        out_shape=(shape(blocks, ROWS, LANES),) + (shape(size, ROWS, LANES),) * 3,
        in_specs=[SMEM] + [VMEM] * 4,
        out_specs=(VMEM,) * 4,
        compiler_params=PARAMS,
        name="place",
    )(new_owner, state, low, high, ghost_rows)
    before = lax.ppermute(ghosts1, "slab", up)
    after = lax.ppermute(ghosts0, "slab", down)
    shared = [ghosts2] + [lax.ppermute(ghosts2, "sub", around[d]) for d in range(1, subs)]
    totals_near = pl.pallas_call(
        functools.partial(pair_kernel, False),
        out_shape=shape(blocks * 8, LANES),
        in_specs=[SMEM, SMEM, VMEM],
        out_specs=VMEM,
        scratch_shapes=pair_scratch(blocks, pairs),
        compiler_params=PARAMS,
        cost_estimate=pl.CostEstimate(flops=60000000, bytes_accessed=400000, transcendentals=0),
        name="near_pairs",
    )(partner_tiles, live_pairs, migrated)
    far = pl.pallas_call(
        functools.partial(pair_kernel, True),
        out_shape=(shape(blocks * 8, LANES),) + (shape(size, 8, LANES),) * 6,
        in_specs=[SMEM, SMEM] + [VMEM] * 7,
        out_specs=(VMEM,) * 7,
        scratch_shapes=pair_scratch(blocks + 6 * size, pairs),
        compiler_params=PARAMS,
        cost_estimate=pl.CostEstimate(flops=60000000, bytes_accessed=400000, transcendentals=0),
        name="far_pairs",
    )(partner_tiles, live_pairs, migrated, before, after, *shared)
    totals_far, back_before, back_after = far[0], far[1], far[2]
    back_shared = far[3:]
    return0 = lax.ppermute(back_after, "slab", up)
    return1 = lax.ppermute(back_before, "slab", down)
    returned = [back_shared[0]] + [
        lax.ppermute(back_shared[d], "sub", against[d]) for d in range(1, subs)
    ]
    return tuple(
        pl.pallas_call(
            final_kernel,
            out_shape=(shape(3, per_dev), shape(3, per_dev), shape(6, per_dev)),
            in_specs=[VMEM] * 10,
            out_specs=(VMEM,) * 3,
            compiler_params=PARAMS,
            name="final",
        )(migrated, totals_near, totals_far, ghost_rows, return0, return1, *returned)
    )


def solution(mesh):
    return jax.shard_map(
        body,
        mesh=mesh,
        in_specs=(
            P(None, ("slab", "sub")),
            P(None, ("slab", "sub")),
            P(("slab", "sub")),
            P(("slab", "sub")),
            P(("slab", "sub")),
            P(None, ("slab", "sub")),
            P(None, ("slab", "sub")),
            P(("slab", "sub")),
        ),
        out_specs=(P(None, ("slab", "sub")), P(None, ("slab", "sub")), P(None, ("slab", "sub"))),
        check_vma=False,
    )
```

time: 195 us -> 90.1 us (0.46)
  the two profiles are of different devices: /device:TPU:8 before, /device:TPU:223 now
where the time goes in v1:
time: 90.1 us; the launch traced here: 89.4 us
  starting transfers between devices  40.3 us (45%)
  Pallas kernels  38.6 us (43%)
  waiting for transfers between devices  5.84 us (6%)
  local copies, waits for them, and re-layouts  3.84 us (4%)
    pallas_call x1, Pallas kernels, body(): pl.pallas_call(functools.partial(pair_kernel, False), out_shape=shape(blo...  20.4 us
    ppermute x3, starting transfers between devices, body(): lax.ppermute(back_shared[d], 'sub', against[d])  14.9 us
    pallas_call x1, Pallas kernels, body(): pl.pallas_call(functools.partial(pair_kernel, True), out_shape=(shape(blo...  13.2 us
    ppermute x3, starting transfers between devices, body(): lax.ppermute(ghosts2, 'sub', around[d])  8.92 us
    ppermute x1, starting transfers between devices, body(): low = lax.ppermute(ahead, 'slab', up)  4.97 us
    ppermute x1, waiting for transfers between devices, body(): high = lax.ppermute(behind, 'slab', down)  4.51 us
    unnamed x16, local copies, waits for them, and re-layouts  3.84 us
    ppermute x1, starting transfers between devices, body(): return1 = lax.ppermute(back_before, 'slab', down)  3.37 us
  transfers between devices with their start and end apart: 12, of which 2 were waited for; matrix products, arithmetic and copies ran while one was open for 0% of the time, Pallas kernels for 23%

profile of v1, /device:TPU:223, one launch (start us, length us, event | category | flops | bytes accessed | tf_op | source)
XLA Modules:
  0.0 89.4 jit_solution(10971227512731742249)
XLA Ops:
  0.6 0.0 copy-start.6
  0.6 0.6 copy-done.6
  1.3 0.0 copy-start
  1.3 0.9 %copy-done = f32[6,4096]{1,0:T(8,128)S(1)} copy-done((f32[6,4096]{1,0:T(8,128)S(1)}, f32[6,4096]{1,0:T(8,128)}, u32[]{:S(2)}) %copy-start) | copy-done | bytes 98328
  2.2 0.0 copy-start.1
  2.2 0.8 copy-done.1
  3.0 0.0 copy-start.3
  3.0 0.7 copy-done.3
  3.8 0.0 copy-start.4
  3.8 0.7 copy-done.4
  4.5 0.0 copy-start.2
  4.5 1.2 %pack.1 = (f32[32,16,128]{2,1,0:T(8,128)S(1)}, f32[4,16,128]{2,1,0:T(8,128)S(1)}, f32[4,16,128]{2,1,0:T(8,128)S(1)}) custom-call(s32[32]{0:T(128)S(1)} %copy-done.6, f32[3,4096]{1,0:T(4,128)S(1)} %copy-done.1, f32[6,4096]{1,0:T(8,128)S(1)} %copy-done, f32[32,128]{1,0:T(8,128)S(1)} %bitcast.2, f32[32,128]{1,0:T(8,128)S(1)} %bitcast.3), custom_call_target="tpu_custom_call" | custom-call | tf_op jit(solution)/shard_map/pack/pallas_call | solution.py:376
  5.7 5.0 %collective-permute-start = (f32[4,16,128]{2,1,0:T(8,128)S(1)}, f32[4,16,128]{2,1,0:T(8,128)S(1)}, u32[]{:S(2)}, u32[]{:S(2)}) collective-permute-start(f32[4,16,128]{2,1,0:T(8,128)S(1)} %get-tuple-element.18), channel_id=1, source_target_pairs={{0,4},{4,8},{8,12},{12,16},{16,20},{20,24},{24,28},{28,32},{32,36}... | collective-permute-start | bytes 98312 | tf_op jit(solution)/shard_map/ppermute | solution.py:394
  10.7 1.9 %collective-permute-start.1 = (f32[4,16,128]{2,1,0:T(8,128)S(1)}, f32[4,16,128]{2,1,0:T(8,128)S(1)}, u32[]{:S(2)}, u32[]{:S(2)}) collective-permute-start(f32[4,16,128]{2,1,0:T(8,128)S(1)} %get-tuple-element.19), channel_id=1, source_target_pairs={{4,0},{8,4},{12,8},{16,12},{20,16},{24,20},{28,24},{32,28},{36,32}... | collective-permute-start | bytes 98312 | tf_op jit(solution)/shard_map/ppermute | solution.py:395
  12.6 0.0 collective-permute-done.low
  12.6 4.5 %collective-permute-done.1.high = f32[4,16,128]{2,1,0:T(8,128)S(1)} collective-permute-done((f32[4,16,128]{2,1,0:T(8,128)S(1)}, f32[4,16,128]{2,1,0:T(8,128)S(1)}, u32[]{:S(2)}, u32[]{:S(2)}) %collective-permute-start.1) | collective-permute-done | bytes 32800 | tf_op jit(solution)/shard_map/ppermute | solution.py:395
  17.1 0.0 copy-done.2
  17.1 2.4 %place.1 = (f32[32,16,128]{2,1,0:T(8,128)S(1)}, f32[4,16,128]{2,1,0:T(8,128)S(1)}, f32[4,16,128]{2,1,0:T(8,128)S(1)}, f32[4,16,128]{2,1,0:T(8,128)S(1)}) custom-call(s32[32]{0:T(128)S(1)} %copy-done.6, f32[32,16,128]{2,1,0:T(8,128)S(1)} %get-tuple-element.17.state, f32[4,16,128]{2,1,0:T(8,128)S(1)} %collective-permute-done.low, ...), custom_call_target="tpu_custom_call" | custom-call | tf_op jit(solution)/shard_map/place/pallas_call | solution.py:396
  19.6 1.9 %collective-permute-start.2 = (f32[4,16,128]{2,1,0:T(8,128)S(1)}, f32[4,16,128]{2,1,0:T(8,128)S(1)}, u32[]{:S(2)}, u32[]{:S(2)}) collective-permute-start(f32[4,16,128]{2,1,0:T(8,128)S(1)} %get-tuple-element.21), channel_id=1, source_target_pairs={{0,4},{4,8},{8,12},{12,16},{16,20},{20,24},{24,28},{28,32},{32,36}... | collective-permute-start | bytes 98312 | tf_op jit(solution)/shard_map/ppermute | solution.py:404
  21.5 2.4 %collective-permute-start.3 = (f32[4,16,128]{2,1,0:T(8,128)S(1)}, f32[4,16,128]{2,1,0:T(8,128)S(1)}, u32[]{:S(2)}, u32[]{:S(2)}) collective-permute-start(f32[4,16,128]{2,1,0:T(8,128)S(1)} %get-tuple-element.22), channel_id=1, source_target_pairs={{4,0},{8,4},{12,8},{16,12},{20,16},{24,20},{28,24},{32,28},{36,32}... | collective-permute-start | bytes 98312 | tf_op jit(solution)/shard_map/ppermute | solution.py:405
  23.9 0.0 copy-start.5
  23.9 0.0 copy-start.7
  23.9 2.5 %collective-permute-start.6 = (f32[4,16,128]{2,1,0:T(8,128)S(1)}, f32[4,16,128]{2,1,0:T(8,128)S(1)}, u32[]{:S(2)}, u32[]{:S(2)}) collective-permute-start(f32[4,16,128]{2,1,0:T(8,128)S(1)} %get-tuple-element.23.rest_2_), channel_id=1, source_target_pairs={{0,3},{1,0},{2,1},{3,2},{4,7},{5,4},{6,5},{7,6},{8,11},{9,8},{10,9... | collective-permute-start | bytes 98312 | tf_op jit(solution)/shard_map/ppermute | solution.py:406
  26.4 2.7 %collective-permute-start.5 = (f32[4,16,128]{2,1,0:T(8,128)S(1)}, f32[4,16,128]{2,1,0:T(8,128)S(1)}, u32[]{:S(2)}, u32[]{:S(2)}) collective-permute-start(f32[4,16,128]{2,1,0:T(8,128)S(1)} %get-tuple-element.23.rest_2_), channel_id=1, source_target_pairs={{0,2},{1,3},{2,0},{3,1},{4,6},{5,7},{6,4},{7,5},{8,10},{9,11},{10,... | collective-permute-start | bytes 98312 | tf_op jit(solution)/shard_map/ppermute | solution.py:406
  29.2 3.7 %collective-permute-start.4 = (f32[4,16,128]{2,1,0:T(8,128)S(1)}, f32[4,16,128]{2,1,0:T(8,128)S(1)}, u32[]{:S(2)}, u32[]{:S(2)}) collective-permute-start(f32[4,16,128]{2,1,0:T(8,128)S(1)} %get-tuple-element.23.rest_2_), channel_id=1, source_target_pairs={{0,1},{1,2},{2,3},{3,0},{4,5},{5,6},{6,7},{7,4},{8,9},{9,10},{10,1... | collective-permute-start | bytes 98312 | tf_op jit(solution)/shard_map/ppermute | solution.py:406
  32.9 0.0 collective-permute-done.2.rest_0_
  32.9 0.0 collective-permute-done.3.rest_1_
  32.9 0.0 collective-permute-done.6.rest_5_
  32.9 0.0 collective-permute-done.5.rest_4_
  32.9 1.3 %collective-permute-done.4.rest_3_ = f32[4,16,128]{2,1,0:T(8,128)S(1)} collective-permute-done((f32[4,16,128]{2,1,0:T(8,128)S(1)}, f32[4,16,128]{2,1,0:T(8,128)S(1)}, u32[]{:S(2)}, u32[]{:S(2)}) %collective-permute-start.4) | collective-permute-done | bytes 32800 | tf_op jit(solution)/shard_map/ppermute | solution.py:406
  34.2 0.0 copy-done.5
  34.2 0.0 copy-done.7
  34.2 13.2 %far_pairs.1 = (f32[256,128]{1,0:T(8,128)S(1)}, f32[4,8,128]{2,1,0:T(8,128)S(1)}, f32[4,8,128]{2,1,0:T(8,128)S(1)}, f32[4,8,128]{2,1,0:T(8,128)S(1)}, f32[4,8,12...) custom-call(s32[2,32]{1,0:T(2,128)S(1)} %copy-done.5, s32[32]{0:T(128)S(1)} %copy-done.7, ...), custom_call_target="tpu_custom_call" | custom-call | flops 60000000 | bytes 400000 | tf_op jit(solution)/shard_map/far_pairs/pallas_call | solution.py:417
  47.5 1.9 %collective-permute-start.7 = (f32[4,8,128]{2,1,0:T(8,128)S(1)}, f32[4,8,128]{2,1,0:T(8,128)S(1)}, u32[]{:S(2)}, u32[]{:S(2)}) collective-permute-start(f32[4,8,128]{2,1,0:T(8,128)S(1)} %get-tuple-element.25), channel_id=1, source_target_pairs={{0,4},{4,8},{8,12},{12,16},{16,20},{20,24},{24,28},{28,32},{32,36}... | collective-permute-start | bytes 49160 | tf_op jit(solution)/shard_map/ppermute | solution.py:429
  49.4 3.4 %collective-permute-start.8 = (f32[4,8,128]{2,1,0:T(8,128)S(1)}, f32[4,8,128]{2,1,0:T(8,128)S(1)}, u32[]{:S(2)}, u32[]{:S(2)}) collective-permute-start(f32[4,8,128]{2,1,0:T(8,128)S(1)} %get-tuple-element.26), channel_id=1, source_target_pairs={{4,0},{8,4},{12,8},{16,12},{20,16},{24,20},{28,24},{32,28},{36,32}... | collective-permute-start | bytes 49160 | tf_op jit(solution)/shard_map/ppermute | solution.py:430
  52.8 2.8 %collective-permute-start.9 = (f32[4,8,128]{2,1,0:T(8,128)S(1)}, f32[4,8,128]{2,1,0:T(8,128)S(1)}, u32[]{:S(2)}, u32[]{:S(2)}) collective-permute-start(f32[4,8,128]{2,1,0:T(8,128)S(1)} %get-tuple-element.28), channel_id=1, source_target_pairs={{0,3},{1,0},{2,1},{3,2},{4,7},{5,4},{6,5},{7,6},{8,11},{9,8},{10,9... | collective-permute-start | bytes 49160 | tf_op jit(solution)/shard_map/ppermute | solution.py:432
  55.6 8.1 %collective-permute-start.10 = (f32[4,8,128]{2,1,0:T(8,128)S(1)}, f32[4,8,128]{2,1,0:T(8,128)S(1)}, u32[]{:S(2)}, u32[]{:S(2)}) collective-permute-start(f32[4,8,128]{2,1,0:T(8,128)S(1)} %get-tuple-element.29), channel_id=1, source_target_pairs={{0,2},{1,3},{2,0},{3,1},{4,6},{5,7},{6,4},{7,5},{8,10},{9,11},{10,... | collective-permute-start | bytes 49160 | tf_op jit(solution)/shard_map/ppermute | solution.py:432
  63.7 4.0 %collective-permute-start.11 = (f32[4,8,128]{2,1,0:T(8,128)S(1)}, f32[4,8,128]{2,1,0:T(8,128)S(1)}, u32[]{:S(2)}, u32[]{:S(2)}) collective-permute-start(f32[4,8,128]{2,1,0:T(8,128)S(1)} %get-tuple-element.30), channel_id=1, source_target_pairs={{0,1},{1,2},{2,3},{3,0},{4,5},{5,6},{6,7},{7,4},{8,9},{9,10},{10,1... | collective-permute-start | bytes 49160 | tf_op jit(solution)/shard_map/ppermute | solution.py:432
  67.7 20.4 %near_pairs.1.totals_near = f32[256,128]{1,0:T(8,128)S(1)} custom-call(s32[2,32]{1,0:T(2,128)S(1)} %copy-done.5, s32[32]{0:T(128)S(1)} %copy-done.7, f32[32,16,128]{2,1,0:T(8,128)S(1)} %get-tuple-element.20.state), custom_call_target="tpu_custom_call" | custom-call | flops 60000000 | bytes 400000 | tf_op jit(solution)/shard_map/near_pairs/pallas_call | solution.py:407
  88.1 0.0 collective-permute-done.7.ret0
  88.1 0.0 collective-permute-done.8.ret1
  88.1 0.0 collective-permute-done.9.sub1
  88.1 0.0 collective-permute-done.10.sub2
  88.1 0.0 collective-permute-done.11.sub3
  88.1 1.3 %final.1 = (f32[3,4096]{1,0:T(4,128)}, f32[3,4096]{1,0:T(4,128)}, f32[6,4096]{1,0:T(8,128)}) custom-call(f32[32,16,128]{2,1,0:T(8,128)S(1)} %get-tuple-element.20.state, f32[256,128]{1,0:T(8,128)S(1)} %near_pairs.1.totals_near, f32[256,128]{1,0:T(8,128)S(1)} %get-tuple-element.24.totals_far, s32[3,512]{1,0:T(4,128)S(1)} %copy-done.2, ...), custom_call_target="tpu_custom_call" | custom-call | tf_op jit(solution)/shard_map/final/pallas_call | solution.py:435
Async XLA Ops:
  0.6 0.7 copy-start.6
  1.3 0.9 %copy-start = (f32[6,4096]{1,0:T(8,128)S(1)}, f32[6,4096]{1,0:T(8,128)}, u32[]{:S(2)}) copy-start(f32[6,4096]{1,0:T(8,128)} %motion.1) | copy-start | bytes 294916
  2.2 0.8 copy-start.1
  3.0 0.7 copy-start.3
  3.8 0.7 copy-start.4
  4.5 12.7 %copy-start.2 = (s32[3,512]{1,0:T(4,128)S(1)}, s32[3,512]{1,0:T(4,128)}, u32[]{:S(2)}) copy-start(s32[3,512]{1,0:T(4,128)} %rows.3) | copy-start | bytes 18436
  5.7 6.9 %collective-permute-start = (f32[4,16,128]{2,1,0:T(8,128)S(1)}, f32[4,16,128]{2,1,0:T(8,128)S(1)}, u32[]{:S(2)}, u32[]{:S(2)}) collective-permute-start(f32[4,16,128]{2,1,0:T(8,128)S(1)} %get-tuple-element.18), channel_id=1, source_target_pairs={{0,4},{4,8},{8,12},{12,16},{16,20},{20,24},{24,28},{28,32},{32,36}... | collective-permute-start | bytes 98312 | tf_op jit(solution)/shard_map/ppermute | solution.py:394
  10.7 6.4 %collective-permute-start.1 = (f32[4,16,128]{2,1,0:T(8,128)S(1)}, f32[4,16,128]{2,1,0:T(8,128)S(1)}, u32[]{:S(2)}, u32[]{:S(2)}) collective-permute-start(f32[4,16,128]{2,1,0:T(8,128)S(1)} %get-tuple-element.19), channel_id=1, source_target_pairs={{4,0},{8,4},{12,8},{16,12},{20,16},{24,20},{28,24},{32,28},{36,32}... | collective-permute-start | bytes 98312 | tf_op jit(solution)/shard_map/ppermute | solution.py:395
  19.6 13.3 %collective-permute-start.2 = (f32[4,16,128]{2,1,0:T(8,128)S(1)}, f32[4,16,128]{2,1,0:T(8,128)S(1)}, u32[]{:S(2)}, u32[]{:S(2)}) collective-permute-start(f32[4,16,128]{2,1,0:T(8,128)S(1)} %get-tuple-element.21), channel_id=1, source_target_pairs={{0,4},{4,8},{8,12},{12,16},{16,20},{20,24},{24,28},{28,32},{32,36}... | collective-permute-start | bytes 98312 | tf_op jit(solution)/shard_map/ppermute | solution.py:404
  21.5 11.4 %collective-permute-start.3 = (f32[4,16,128]{2,1,0:T(8,128)S(1)}, f32[4,16,128]{2,1,0:T(8,128)S(1)}, u32[]{:S(2)}, u32[]{:S(2)}) collective-permute-start(f32[4,16,128]{2,1,0:T(8,128)S(1)} %get-tuple-element.22), channel_id=1, source_target_pairs={{4,0},{8,4},{12,8},{16,12},{20,16},{24,20},{28,24},{32,28},{36,32}... | collective-permute-start | bytes 98312 | tf_op jit(solution)/shard_map/ppermute | solution.py:405
  23.9 10.3 %copy-start.5 = (s32[2,32]{1,0:T(2,128)S(1)}, s32[2,32]{1,0:T(2,128)}, u32[]{:S(2)}) copy-start(s32[2,32]{1,0:T(2,128)} %partners.3) | copy-start | bytes 772
  23.9 10.3 %copy-start.7 = (s32[32]{0:T(128)S(1)}, s32[32]{0:T(128)}, u32[]{:S(2)}) copy-start(s32[32]{0:T(128)} %live.3) | copy-start | bytes 388
  23.9 9.0 %collective-permute-start.6 = (f32[4,16,128]{2,1,0:T(8,128)S(1)}, f32[4,16,128]{2,1,0:T(8,128)S(1)}, u32[]{:S(2)}, u32[]{:S(2)}) collective-permute-start(f32[4,16,128]{2,1,0:T(8,128)S(1)} %get-tuple-element.23.rest_2_), channel_id=1, source_target_pairs={{0,3},{1,0},{2,1},{3,2},{4,7},{5,4},{6,5},{7,6},{8,11},{9,8},{10,9... | collective-permute-start | bytes 98312 | tf_op jit(solution)/shard_map/ppermute | solution.py:406
  26.4 6.5 %collective-permute-start.5 = (f32[4,16,128]{2,1,0:T(8,128)S(1)}, f32[4,16,128]{2,1,0:T(8,128)S(1)}, u32[]{:S(2)}, u32[]{:S(2)}) collective-permute-start(f32[4,16,128]{2,1,0:T(8,128)S(1)} %get-tuple-element.23.rest_2_), channel_id=1, source_target_pairs={{0,2},{1,3},{2,0},{3,1},{4,6},{5,7},{6,4},{7,5},{8,10},{9,11},{10,... | collective-permute-start | bytes 98312 | tf_op jit(solution)/shard_map/ppermute | solution.py:406
  29.2 5.1 %collective-permute-start.4 = (f32[4,16,128]{2,1,0:T(8,128)S(1)}, f32[4,16,128]{2,1,0:T(8,128)S(1)}, u32[]{:S(2)}, u32[]{:S(2)}) collective-permute-start(f32[4,16,128]{2,1,0:T(8,128)S(1)} %get-tuple-element.23.rest_2_), channel_id=1, source_target_pairs={{0,1},{1,2},{2,3},{3,0},{4,5},{5,6},{6,7},{7,4},{8,9},{9,10},{10,1... | collective-permute-start | bytes 98312 | tf_op jit(solution)/shard_map/ppermute | solution.py:406
  47.5 40.6 %collective-permute-start.7 = (f32[4,8,128]{2,1,0:T(8,128)S(1)}, f32[4,8,128]{2,1,0:T(8,128)S(1)}, u32[]{:S(2)}, u32[]{:S(2)}) collective-permute-start(f32[4,8,128]{2,1,0:T(8,128)S(1)} %get-tuple-element.25), channel_id=1, source_target_pairs={{0,4},{4,8},{8,12},{12,16},{16,20},{20,24},{24,28},{28,32},{32,36}... | collective-permute-start | bytes 49160 | tf_op jit(solution)/shard_map/ppermute | solution.py:429
  49.4 38.7 %collective-permute-start.8 = (f32[4,8,128]{2,1,0:T(8,128)S(1)}, f32[4,8,128]{2,1,0:T(8,128)S(1)}, u32[]{:S(2)}, u32[]{:S(2)}) collective-permute-start(f32[4,8,128]{2,1,0:T(8,128)S(1)} %get-tuple-element.26), channel_id=1, source_target_pairs={{4,0},{8,4},{12,8},{16,12},{20,16},{24,20},{28,24},{32,28},{36,32}... | collective-permute-start | bytes 49160 | tf_op jit(solution)/shard_map/ppermute | solution.py:430
  52.8 35.3 %collective-permute-start.9 = (f32[4,8,128]{2,1,0:T(8,128)S(1)}, f32[4,8,128]{2,1,0:T(8,128)S(1)}, u32[]{:S(2)}, u32[]{:S(2)}) collective-permute-start(f32[4,8,128]{2,1,0:T(8,128)S(1)} %get-tuple-element.28), channel_id=1, source_target_pairs={{0,3},{1,0},{2,1},{3,2},{4,7},{5,4},{6,5},{7,6},{8,11},{9,8},{10,9... | collective-permute-start | bytes 49160 | tf_op jit(solution)/shard_map/ppermute | solution.py:432
  55.6 32.5 %collective-permute-start.10 = (f32[4,8,128]{2,1,0:T(8,128)S(1)}, f32[4,8,128]{2,1,0:T(8,128)S(1)}, u32[]{:S(2)}, u32[]{:S(2)}) collective-permute-start(f32[4,8,128]{2,1,0:T(8,128)S(1)} %get-tuple-element.29), channel_id=1, source_target_pairs={{0,2},{1,3},{2,0},{3,1},{4,6},{5,7},{6,4},{7,5},{8,10},{9,11},{10,... | collective-permute-start | bytes 49160 | tf_op jit(solution)/shard_map/ppermute | solution.py:432
  63.7 24.4 %collective-permute-start.11 = (f32[4,8,128]{2,1,0:T(8,128)S(1)}, f32[4,8,128]{2,1,0:T(8,128)S(1)}, u32[]{:S(2)}, u32[]{:S(2)}) collective-permute-start(f32[4,8,128]{2,1,0:T(8,128)S(1)} %get-tuple-element.30), channel_id=1, source_target_pairs={{0,1},{1,2},{2,3},{3,0},{4,5},{5,6},{6,7},{7,4},{8,9},{9,10},{10,1... | collective-permute-start | bytes 49160 | tf_op jit(solution)/shard_map/ppermute | solution.py:432

commit v2 on v1

v2 whole, which is shorter than its diff:
```python
import functools

import jax
import jax.numpy as jnp
from jax import lax
from jax.experimental import pallas as pl
from jax.experimental.pallas import tpu as pltpu
from jax.sharding import PartitionSpec as P

min_distance = 0.2
stiffness = 1.0
normal_damp = 0.5
shear_damp = 0.3
surface_tension = 2.0
rupture_scale = 1.0
time_step = 0.005

LANES = 128
ROWS = 16
CAP = 4
FEATS = 16
MATS = 5
PAIR_ROWS = 12
GROUP = 4

f32 = jnp.float32
bf16 = jnp.bfloat16
VMEM = pl.BlockSpec(memory_space=pltpu.VMEM)
SMEM = pl.BlockSpec(memory_space=pltpu.SMEM)
HBM = pl.BlockSpec(memory_space=pltpu.HBM)
PARAMS = pltpu.CompilerParams(vmem_limit_bytes=40 * 1024 * 1024)


def split(value, parts):
    out = []
    for _ in range(parts - 1):
        high = value.astype(bf16)
        out.append(high)
        value = value - high.astype(f32)
    out.append(value.astype(bf16))
    return out


def dot_nn(left, right):
    return lax.dot_general(left, right, (((1,), (0,)), ((), ())), preferred_element_type=f32)


def dot_nt(left, right):
    return lax.dot_general(left, right, (((1,), (1,)), ((), ())), preferred_element_type=f32)


def pack_kernel(
    owner, positions, motion, radius, liquid, state, ahead, behind, place, speed, size, wet, sems
):
    copies = [
        pltpu.make_async_copy(source, target, sems.at[index])
        for index, (source, target) in enumerate(
            [(positions, place), (motion, speed), (radius, size), (liquid, wet)]
        )
    ]
    for copy in copies:
        copy.start()
    here = lax.axis_index("slab")
    blocks = state.shape[0]
    ahead[...] = jnp.zeros_like(ahead)
    behind[...] = jnp.zeros_like(behind)
    for copy in copies:
        copy.wait()
    count_ahead = jnp.int32(0)
    count_behind = jnp.int32(0)
    for block in range(blocks):
        columns = slice(block * LANES, (block + 1) * LANES)
        target = owner[block]
        state[block, 0:3, :] = place[:, columns]
        state[block, 3:9, :] = speed[:, columns]
        state[block, 9:10, :] = size[block : block + 1, :]
        state[block, 10:11, :] = wet[block : block + 1, :]
        state[block, 11:16, :] = jnp.full((5, LANES), (target + 1).astype(f32), f32)
        slab = target // blocks
        goes_ahead = slab == here + 1
        goes_behind = slab == here - 1

        @pl.when(goes_ahead)
        def _():
            ahead[count_ahead] = state[block]

        @pl.when(goes_behind)
        def _():
            behind[count_behind] = state[block]

        count_ahead = jnp.minimum(count_ahead + goes_ahead.astype(jnp.int32), CAP - 1)
        count_behind = jnp.minimum(count_behind + goes_behind.astype(jnp.int32), CAP - 1)


def place_kernel(owner, state, low, high, rows, partners, live, to_prev, to_next, to_sub):
    here = lax.axis_index("slab")
    blocks = state.shape[0]
    for block in range(blocks):
        target = owner[block]

        @pl.when(target // blocks == here)
        def _():
            to_sub[target % blocks] = state[block]

    base = (here * blocks + 1).astype(f32)
    arrived = [low[slot] for slot in range(CAP)] + [high[slot] for slot in range(CAP)]
    tags = [jnp.broadcast_to(block[11:12, :], (ROWS, LANES)) - base for block in arrived]
    for slot in range(blocks):
        current = to_sub[slot]
        for block, tag in zip(arrived, tags):
            current = jnp.where(tag == float(slot), block, current)
        to_sub[slot] = current
        to_prev[slot] = current
        to_next[slot] = current

    flat = to_sub[0:blocks].reshape(blocks * ROWS, LANES)
    left = jnp.concatenate(split(flat, 3), axis=1)
    lane_ids = lax.broadcasted_iota(jnp.int32, (LANES, LANES), 0)
    code = jnp.concatenate(
        [
            jnp.where(live[...] > which, partners[which : which + 1, :], -1).astype(f32)
            for which in range(partners.shape[0])
        ],
        axis=0,
    )
    for which, message in enumerate((to_prev, to_next, to_sub)):
        for tile in range(message.shape[0] - blocks):
            index = rows[which : which + 1, tile * LANES : (tile + 1) * LANES]
            hot = jnp.where(lane_ids == index % LANES, 1.0, 0.0).astype(bf16)
            picked = dot_nn(left, jnp.concatenate([hot, hot, hot], axis=0))
            source = jnp.broadcast_to(index // LANES, (ROWS, LANES))
            total = jnp.zeros((ROWS, LANES), f32)
            for block in range(blocks):
                total = jnp.where(source == block, picked[block * ROWS : (block + 1) * ROWS], total)
            message[blocks + tile] = total
        message[blocks, 11 : 11 + partners.shape[0], 0:blocks] = code


def cross(first, second):
    return [
        first[1] * second[2] - first[2] * second[1],
        first[2] * second[0] - first[0] * second[2],
        first[0] * second[1] - first[1] * second[0],
    ]


def recip(value):
    guess = pl.reciprocal(value, approx=True)
    return guess * (2.0 - value * guess)


def scale(tile):
    radius, liquid = tile[9:10, :], tile[10:11, :]
    bond = radius * jnp.sqrt(surface_tension * liquid)
    zero = jnp.zeros((4, LANES), f32)
    return jnp.concatenate([tile[0:6, :], radius * tile[6:9, :], radius, liquid, bond, zero], axis=0)


def features(scaled):
    rows = [scaled[row : row + 1, :] for row in range(9)]
    place, velocity, turn = rows[0:3], rows[3:6], rows[6:9]
    one = jnp.ones((1, LANES), f32)
    values = jnp.concatenate(
        place + [one] + velocity + turn + cross(turn, place) + cross(place, velocity), axis=0
    )
    return jnp.concatenate(split(values, 3), axis=0)


def fill_spread(spread):
    rows = lax.broadcasted_iota(jnp.int32, (3 * ROWS, LANES), 0) % ROWS
    for row in range(PAIR_ROWS):
        spread[:, row * LANES : (row + 1) * LANES] = jnp.where(rows == row, 1.0, 0.0).astype(bf16)


def pair_scalars(near, far, spread, coefs):
    parts = jnp.concatenate(split(near, 3), axis=0)
    columns = lax.dot_general(
        parts, spread[...], (((0,), (0,)), ((), ())), preferred_element_type=f32
    )
    far_rows = [far[row : row + 1, :] for row in range(PAIR_ROWS)]
    step = 16
    for start in range(0, LANES, step):
        col = [
            columns[start : start + step, row * LANES : (row + 1) * LANES]
            for row in range(PAIR_ROWS)
        ]
        offset = [far_rows[row] - col[row] for row in range(3)]
        moving = [far_rows[row] - col[row] for row in range(3, 6)]
        turning = [far_rows[row] + col[row] for row in range(6, 9)]
        square = offset[0] * offset[0] + offset[1] * offset[1] + offset[2] * offset[2]
        along = offset[0] * moving[0] + offset[1] * moving[1] + offset[2] * moving[2]
        twist = offset[0] * turning[0] + offset[1] * turning[1] + offset[2] * turning[2]
        root = lax.rsqrt(jnp.maximum(square, 1e-30))
        length = square * root
        inverse = jnp.minimum(root, 1.0 / min_distance)
        radii = far_rows[9] + col[9]
        gap = length - radii
        overlap = jnp.maximum(-gap, 0.0)
        apart = jnp.maximum(gap, 0.0)
        over_radii = recip(radii)
        inner = far_rows[9] * col[9] * over_radii * overlap
        spread = inner * lax.rsqrt(jnp.maximum(inner, 1e-30))
        fill = jnp.maximum(1.0 - apart * recip(rupture_scale * (far_rows[10] + col[10])), 0.0)
        bridge = far_rows[11] * col[11] * over_radii * (fill * fill)
        approach = along * inverse
        shear = shear_damp * spread
        push = stiffness * overlap - (normal_damp - shear_damp) * approach
        shear_inv = shear * inverse
        shear_inv2 = shear_inv * inverse
        mats = [
            (bridge - spread * push) * inverse,
            shear,
            shear_inv,
            shear_inv2 * square,
            shear_inv2 * twist,
        ]
        for index, mat in enumerate(mats):
            high, low = split(mat, 2)
            coefs[index * LANES + start : index * LANES + start + step, 0:LANES] = high
            coefs[index * LANES + start : index * LANES + start + step, LANES:] = low


def add_own(first, far_feats, sums, coefs):
    own = dot_nt(jnp.concatenate([far_feats, far_feats], axis=1), coefs[...])
    own = own[0:FEATS] + own[FEATS : 2 * FEATS] + own[2 * FEATS :]
    base = pl.multiple_of(first * (MATS * FEATS), 16)
    for index in range(MATS):
        sums[pl.ds(base + index * FEATS, FEATS), :] += own[:, index * LANES : (index + 1) * LANES]


def add_back(second, near_feats, sums, coefs):
    base = pl.multiple_of(second * (MATS * FEATS), 16)
    for index in range(MATS):
        back = dot_nn(near_feats, coefs[index * LANES : (index + 1) * LANES, :])
        back = back[:, 0:LANES] + back[:, LANES:]
        back = back[0:FEATS] + back[FEATS : 2 * FEATS] + back[2 * FEATS :]
        if index == MATS - 1:
            back = -back
        sums[pl.ds(base + index * FEATS, FEATS), :] += back


def finish(group, sums, scaled):
    span = MATS * FEATS

    def total(mat, feat):
        return sums[pl.ds(group * 8 * span + mat * FEATS + feat, 8, stride=span), :]

    def own(row):
        return scaled[pl.ds(group * 8, 8), row, :]

    place = [own(row) for row in range(3)]
    velocity = [own(row) for row in range(3, 6)]
    turn = [own(row) for row in range(6, 9)]
    radius = own(9)
    s_place = [total(0, feat) for feat in range(3)]
    s_one = total(0, 3)
    c_one = total(1, 3)
    c_velocity = [total(1, feat) for feat in range(4, 7)]
    n_place = [total(2, feat) for feat in range(3)]
    n_one = total(2, 3)
    n_velocity = [total(2, feat) for feat in range(4, 7)]
    n_turn = [total(2, feat) for feat in range(7, 10)]
    n_turn_place = [total(2, feat) for feat in range(10, 13)]
    n_place_velocity = [total(2, feat) for feat in range(13, 16)]
    k_one = total(3, 3)
    k_turn = [total(3, feat) for feat in range(7, 10)]
    g_place = [total(4, feat) for feat in range(3)]
    g_one = total(4, 3)
    turn_place = cross(turn, place)
    place_velocity = cross(place, velocity)
    first = cross(turn, n_place)
    second = cross(n_turn, place)
    third = cross(n_place, velocity)
    fourth = cross(place, n_velocity)
    force = [
        (s_place[x] - place[x] * s_one)
        + (c_velocity[x] - velocity[x] * c_one)
        - (first[x] - turn_place[x] * n_one + n_turn_place[x] - second[x])
        for x in range(3)
    ]
    torque = [
        radius
        * (
            (n_place_velocity[x] - third[x] - fourth[x] + place_velocity[x] * n_one)
            - (turn[x] * k_one + k_turn[x])
            + (g_place[x] - place[x] * g_one)
        )
        for x in range(3)
    ]
    return force + torque


def near_kernel(
    partners, live, to_prev, to_next, to_sub, totals, scaled, feats, sums, spread, todo, *coefs
):
    own_tiles = to_sub.shape[0]
    size = own_tiles - partners.shape[1]
    blocks = own_tiles - size
    fill_spread(spread)
    sums[...] = jnp.zeros_like(sums)
    for tile in range(own_tiles):
        scaled[tile] = scale(to_sub[tile])
        feats[tile] = features(scaled[tile])
    for tile in range(size):
        scaled[own_tiles + tile] = scale(to_prev[blocks + tile])
        scaled[own_tiles + size + tile] = scale(to_next[blocks + tile])
    spare = scaled.shape[0] - 1
    for tile in range(own_tiles + 2 * size, spare + 1):
        scaled[tile] = jnp.ones((ROWS, LANES), f32)
    feats[spare] = features(scaled[spare])
    shared = blocks + (2 + lax.axis_index("sub")) * size
    count = jnp.int32(0)
    for tile in range(blocks):
        for which in range(partners.shape[0]):
            partner = partners[which, tile]
            mine = (partner >= shared) & (partner < shared + size)
            wanted = (which < live[tile]) & ((partner < blocks) | mine)
            slot = jnp.where(mine, partner - shared + blocks, partner)
            todo[count] = tile * 64 + slot
            count = count + wanted.astype(jnp.int32)

    for extra in range(GROUP):
        todo[count + extra] = spare * 64 + spare

    def some_pairs(index, carry):
        entries = [todo[index * GROUP + lane] for lane in range(GROUP)]
        entries = [(entry // 64, entry % 64) for entry in entries]
        for (first, second), coef in zip(entries, coefs):
            pair_scalars(scaled[first], scaled[second], spread, coef)
        for (first, second), coef in zip(entries, coefs):
            add_own(first, feats[second], sums, coef)
            add_back(second, feats[first], sums, coef)
        return carry

    lax.fori_loop(0, (count + GROUP - 1) // GROUP, some_pairs, 0)
    for group in range(scaled.shape[0] // 8):
        for row, value in enumerate(finish(group, sums, scaled)):
            totals[pl.ds(group * 64 + row, 8, stride=8), :] = value


def far_kernel(shared, partners, live, before, scaled, *rest):
    messages, rest = rest[:-8 - GROUP], rest[-8 - GROUP :]
    totals, sums, spread, picked, codes, heard, todo, sem = rest[:8]
    coefs = rest[8:]
    spare = scaled.shape[0] - 1
    fill_spread(spread)
    blocks = partners.shape[1]
    choices = partners.shape[0]
    size = messages[0].shape[0] - blocks
    for number, message in enumerate(messages):
        codes[number * choices : (number + 1) * choices, :] = message[
            blocks, 11 : 11 + choices, :
        ].astype(jnp.int32)
    copy = pltpu.make_async_copy(codes, heard, sem)
    copy.start()
    sums[...] = jnp.zeros_like(sums)
    copy.wait()
    sub = lax.axis_index("sub")
    subs = lax.axis_size("sub")
    count = jnp.int32(0)
    for number, message in enumerate(messages):
        if shared:
            sender = lax.rem(sub + subs - 1 - number, subs)
            theirs = blocks + (2 + sender) * size
            ours = blocks + (2 + sub) * size
            ghost = blocks
        else:
            theirs = blocks + number * size
            ours = blocks + (1 - number) * size
            ghost = blocks + (1 + number) * size

        start = count
        for tile in range(blocks):
            for which in range(choices):
                shift = partners[which, tile] - theirs
                wanted = (which < live[tile]) & (shift >= 0) & (shift < size)
                todo[count] = tile * 64 + blocks + shift
                count = count + wanted.astype(jnp.int32)
                shift = heard[number * choices + which, tile] - ours
                wanted = (shift >= 0) & (shift < size)
                todo[count] = (ghost + shift) * 64 + tile
                count = count + wanted.astype(jnp.int32)

        def pick(index, carry):
            picked[index] = scale(message[todo[index] % 64])
            return carry

        lax.fori_loop(start, count, pick, 0)
    for extra in range(GROUP):
        todo[count + extra] = spare * 64
        picked[count + extra] = scaled[spare]

    def some_pairs(index, carry):
        first = index * GROUP
        mine = [todo[first + lane] // 64 for lane in range(GROUP)]
        near = [picked[first + lane] for lane in range(GROUP)]
        for lane, coef in enumerate(coefs):
            pair_scalars(near[lane], scaled[mine[lane]], spread, coef)
        for lane, coef in enumerate(coefs):
            add_back(mine[lane], features(near[lane]), sums, coef)
        return carry

    lax.fori_loop(0, (count + GROUP - 1) // GROUP, some_pairs, 0)
    for group in range(scaled.shape[0] // 8):
        for row, value in enumerate(finish(group, sums, scaled)):
            part = pl.ds(group * 64 + row, 8, stride=8)
            totals[part, :] = before[part, :] + value


def final_kernel(state, totals, rows, force, torque, kicked):
    size = rows.shape[1] // LANES
    blocks = state.shape[0] - size
    lane_ids = lax.broadcasted_iota(jnp.int32, (LANES, LANES), 0)
    hots = []
    lefts = []
    for which in range(3):
        for tile in range(size):
            index = rows[which : which + 1, tile * LANES : (tile + 1) * LANES]
            hots.append(jnp.where(lane_ids == index % LANES, 1.0, 0.0).astype(bf16))
            ghost = blocks + (which + 1) % 3 * size + tile
            value = totals[ghost * 8 : ghost * 8 + 8, :]
            high = value.astype(bf16).astype(f32)
            both = jnp.concatenate([high, value - high], axis=0)
            source = jnp.broadcast_to(index // LANES, (ROWS, LANES))
            lefts.append(
                jnp.concatenate(
                    [
                        jnp.where(source == block, both, 0.0).astype(bf16)
                        for block in range(blocks)
                    ],
                    axis=0,
                )
            )
    added = dot_nt(jnp.concatenate(lefts, axis=1), jnp.concatenate(hots, axis=1))
    row_ids = lax.broadcasted_iota(jnp.int32, (8, LANES), 0)
    for block in range(blocks):
        columns = slice(block * LANES, (block + 1) * LANES)
        extra = added[block * ROWS : block * ROWS + 8] + added[block * ROWS + 8 : block * ROWS + 16]
        total = totals[block * 8 : block * 8 + 8, :] + extra
        radius = state[block, 9:10, :]
        mass = radius * radius * radius
        inertia = 0.4 * mass * radius * radius
        weight = jnp.where(row_ids < 3, time_step / mass, time_step / inertia)
        force[:, columns] = total[0:3]
        torque[:, columns] = total[3:6]
        kicked[:, columns] = state[block, 3:9, :] + (total * weight)[0:6]


def shape(*dims, dtype=f32):
    return jax.ShapeDtypeStruct(dims, dtype)


def body(positions, motion, radius, liquid, new_owner, ghost_rows, partner_tiles, live_pairs):
    per_dev = positions.shape[1]
    blocks = per_dev // LANES
    size = ghost_rows.shape[1] // LANES
    choices = partner_tiles.shape[0]
    tiles = -(-(blocks + 3 * size) // 8) * 8
    slabs = lax.axis_size("slab")
    subs = lax.axis_size("sub")
    up = [(i, i + 1) for i in range(slabs - 1)]
    down = [(i + 1, i) for i in range(slabs - 1)]
    around = [[(i, (i + d) % subs) for i in range(subs)] for d in range(subs)]
    sums = pltpu.VMEM((tiles * MATS * FEATS, LANES), f32)
    spread = pltpu.VMEM((3 * ROWS, PAIR_ROWS * LANES), bf16)
    coefs = [pltpu.VMEM((MATS * LANES, 2 * LANES), bf16)] * GROUP
    cost = pl.CostEstimate(flops=60000000, bytes_accessed=400000, transcendentals=0)

    state, ahead, behind = pl.pallas_call(
        pack_kernel,
        out_shape=(
            shape(blocks, ROWS, LANES),
            shape(CAP, ROWS, LANES),
            shape(CAP, ROWS, LANES),
        ),
        in_specs=[SMEM] + [HBM] * 4,
        out_specs=(VMEM,) * 3,
        scratch_shapes=[
            pltpu.VMEM((3, per_dev), f32),
            pltpu.VMEM((6, per_dev), f32),
            pltpu.VMEM((blocks, LANES), f32),
            pltpu.VMEM((blocks, LANES), f32),
            pltpu.SemaphoreType.DMA((4,)),
        ],
        compiler_params=PARAMS,
        name="pack",
    )(
        new_owner,
        positions,
        motion,
        radius.reshape(blocks, LANES),
        liquid.reshape(blocks, LANES),
    )
    low = lax.ppermute(ahead, "slab", up)
    high = lax.ppermute(behind, "slab", down)
    to_prev, to_next, to_sub = pl.pallas_call(
        place_kernel,
        out_shape=(shape(blocks + size, ROWS, LANES),) * 3,
        in_specs=[SMEM] + [VMEM] * 6,
        out_specs=(VMEM,) * 3,
        compiler_params=PARAMS,
        name="place",
    )(new_owner, state, low, high, ghost_rows, partner_tiles, live_pairs.reshape(1, blocks))
    around_sub = [lax.ppermute(to_sub, "sub", around[d]) for d in range(1, subs)]
    from_prev = lax.ppermute(to_next, "slab", up)
    from_next = lax.ppermute(to_prev, "slab", down)
    totals, scaled = pl.pallas_call(
        near_kernel,
        out_shape=(shape(tiles * 8, LANES), shape(tiles, ROWS, LANES)),
        in_specs=[SMEM, SMEM] + [VMEM] * 3,
        out_specs=(VMEM, VMEM),
        scratch_shapes=[
            pltpu.VMEM((tiles, 3 * FEATS, LANES), bf16),
            sums,
            spread,
            pltpu.SMEM((choices * blocks + GROUP,), jnp.int32),
        ]
        + coefs,
        compiler_params=PARAMS,
        cost_estimate=cost,
        name="near_pairs",
    )(partner_tiles, live_pairs, to_prev, to_next, to_sub)
    for shared, messages in ((False, [from_prev, from_next]), (True, around_sub)):
        room = choices * blocks * (1 + len(messages))
        totals = pl.pallas_call(
            functools.partial(far_kernel, shared),
            out_shape=shape(tiles * 8, LANES),
            in_specs=[SMEM, SMEM] + [VMEM] * (2 + len(messages)),
            out_specs=VMEM,
            scratch_shapes=[
                sums,
                spread,
                pltpu.VMEM((room + GROUP, ROWS, LANES), f32),
                pltpu.VMEM((8, LANES), jnp.int32),
                pltpu.SMEM((8, LANES), jnp.int32),
                pltpu.SMEM((room + GROUP,), jnp.int32),
                pltpu.SemaphoreType.DMA(()),
            ]
            + coefs,
            compiler_params=PARAMS,
            cost_estimate=cost,
            name="sub_pairs" if shared else "slab_pairs",
        )(partner_tiles, live_pairs, totals, scaled, *messages)
    return tuple(
        pl.pallas_call(
            final_kernel,
            out_shape=(shape(3, per_dev), shape(3, per_dev), shape(6, per_dev)),
            in_specs=[VMEM] * 3,
            out_specs=(VMEM,) * 3,
            compiler_params=PARAMS,
            name="final",
        )(to_sub, totals, ghost_rows)
    )


def solution(mesh):
    return jax.shard_map(
        body,
        mesh=mesh,
        in_specs=(
            P(None, ("slab", "sub")),
            P(None, ("slab", "sub")),
            P(("slab", "sub")),
            P(("slab", "sub")),
            P(("slab", "sub")),
            P(None, ("slab", "sub")),
            P(None, ("slab", "sub")),
            P(("slab", "sub")),
        ),
        out_specs=(P(None, ("slab", "sub")), P(None, ("slab", "sub")), P(None, ("slab", "sub"))),
        check_vma=False,
    )
```

time: 90.1 us -> 66.1 us (0.73)
  the two profiles are of different devices: /device:TPU:223 before, /device:TPU:248 now
where the time goes in v2:
time: 66.1 us; the launch traced here: 65.7 us
  Pallas kernels  31.8 us (48%)
  starting transfers between devices  26.7 us (40%)
  local copies, waits for them, and re-layouts  4.51 us (7%)
  waiting for transfers between devices  1.84 us (3%)
  between operations  0.79 us (1%)
    pallas_call x2, Pallas kernels, body(): pl.pallas_call(functools.partial(far_kernel, shared), out_shape=shape(til...  16.2 us
    ppermute x3, starting transfers between devices, body(): lax.ppermute(to_sub, 'sub', around[d])  11.4 us
    pallas_call x1, Pallas kernels, body(): pl.pallas_call(near_kernel, out_shape=(shape(tiles * 8, LANES), shape(til...  10.3 us
    ppermute x1, starting transfers between devices, body(): from_prev = lax.ppermute(to_next, 'slab', up)  7.86 us
    unnamed x16, local copies, waits for them, and re-layouts  4.51 us
    ppermute x1, starting transfers between devices, body(): high = lax.ppermute(behind, 'slab', down)  3.64 us
    pallas_call x1, Pallas kernels, body(): pl.pallas_call(place_kernel, out_shape=(shape(blocks + size, ROWS, LANES)...  2.44 us
    ppermute x1, starting transfers between devices, body(): from_next = lax.ppermute(to_prev, 'slab', down)  1.92 us
  transfers between devices with their start and end apart: 7, of which 1 were waited for; matrix products, arithmetic and copies ran while one was open for 0% of the time, Pallas kernels for 26%

profile of v2, /device:TPU:248, one launch (start us, length us, event | category | flops | bytes accessed | tf_op | source)
XLA Modules:
  0.0 65.7 jit_solution(233114117353092673)
XLA Ops:
  0.6 0.0 copy-start.7
  0.6 0.6 copy-done.7
  1.3 0.0 copy-start
  1.3 0.9 %copy-done = f32[6,4096]{1,0:T(8,128)S(1)} copy-done((f32[6,4096]{1,0:T(8,128)S(1)}, f32[6,4096]{1,0:T(8,128)}, u32[]{:S(2)}) %copy-start) | copy-done | bytes 98328
  2.2 0.0 copy-start.1
  2.2 0.8 %copy-done.1 = f32[3,4096]{1,0:T(4,128)S(1)} copy-done((f32[3,4096]{1,0:T(4,128)S(1)}, f32[3,4096]{1,0:T(4,128)}, u32[]{:S(2)}) %copy-start.1) | copy-done | bytes 49176
  3.0 0.0 copy-start.3
  3.0 0.7 %copy-done.3 = f32[4096]{0:T(1024)S(1)} copy-done((f32[4096]{0:T(1024)S(1)}, f32[4096]{0:T(1024)}, u32[]{:S(2)}) %copy-start.3) | copy-done | bytes 16408
  3.8 0.0 copy-start.4
  3.8 0.7 %copy-done.4 = f32[4096]{0:T(1024)S(1)} copy-done((f32[4096]{0:T(1024)S(1)}, f32[4096]{0:T(1024)}, u32[]{:S(2)}) %copy-start.4) | copy-done | bytes 16408
  4.5 0.0 copy-start.2
  4.5 1.6 %pack.1 = (f32[32,16,128]{2,1,0:T(8,128)S(1)}, f32[4,16,128]{2,1,0:T(8,128)S(1)}, f32[4,16,128]{2,1,0:T(8,128)S(1)}) custom-call(s32[32]{0:T(128)S(1)} %copy-done.7, f32[3,4096]{1,0:T(4,128)S(1)} %copy-done.1, f32[6,4096]{1,0:T(8,128)S(1)} %copy-done, f32[32,128]{1,0:T(8,128)S(1)} %bitcast.3, f32[32,128]{1,0:T(8,128)S(1)} %bitcast.4), custom_call_target="tpu_custom_call" | custom-call | tf_op jit(solution)/shard_map/pack/pallas_call | solution.py:469
  6.0 1.9 %collective-permute-start = (f32[4,16,128]{2,1,0:T(8,128)S(1)}, f32[4,16,128]{2,1,0:T(8,128)S(1)}, u32[]{:S(2)}, u32[]{:S(2)}) collective-permute-start(f32[4,16,128]{2,1,0:T(8,128)S(1)} %get-tuple-element.12), channel_id=1, source_target_pairs={{0,4},{4,8},{8,12},{12,16},{16,20},{20,24},{24,28},{28,32},{32,36}... | collective-permute-start | bytes 98312 | tf_op jit(solution)/shard_map/ppermute | solution.py:494
  8.0 3.6 %collective-permute-start.1 = (f32[4,16,128]{2,1,0:T(8,128)S(1)}, f32[4,16,128]{2,1,0:T(8,128)S(1)}, u32[]{:S(2)}, u32[]{:S(2)}) collective-permute-start(f32[4,16,128]{2,1,0:T(8,128)S(1)} %get-tuple-element.13), channel_id=1, source_target_pairs={{4,0},{8,4},{12,8},{16,12},{20,16},{24,20},{28,24},{32,28},{36,32}... | collective-permute-start | bytes 98312 | tf_op jit(solution)/shard_map/ppermute | solution.py:495
  11.6 0.0 collective-permute-done.low
  11.6 1.8 %collective-permute-done.1.high = f32[4,16,128]{2,1,0:T(8,128)S(1)} collective-permute-done((f32[4,16,128]{2,1,0:T(8,128)S(1)}, f32[4,16,128]{2,1,0:T(8,128)S(1)}, u32[]{:S(2)}, u32[]{:S(2)}) %collective-permute-start.1) | collective-permute-done | bytes 32800 | tf_op jit(solution)/shard_map/ppermute | solution.py:495
  13.5 0.0 copy-start.5
  13.5 0.0 copy-start.6
  13.5 0.0 copy-done.2
  13.5 0.7 %copy-done.5 = s32[2,32]{1,0:T(2,128)S(1)} copy-done((s32[2,32]{1,0:T(2,128)S(1)}, s32[2,32]{1,0:T(2,128)}, u32[]{:S(2)}) %copy-start.5) | copy-done | bytes 280
  14.1 0.0 copy-done.6
  14.1 2.4 %place.1 = (f32[36,16,128]{2,1,0:T(8,128)S(1)}, f32[36,16,128]{2,1,0:T(8,128)S(1)}, f32[36,16,128]{2,1,0:T(8,128)S(1)}) custom-call(s32[32]{0:T(128)S(1)} %copy-done.7, f32[32,16,128]{2,1,0:T(8,128)S(1)} %get-tuple-element.11.state, f32[4,16,128]{2,1,0:T(8,128)S(1)} %collective-permute-done.low, f32[4,16,128]{2,1,0:T(8,128)S(1)} %collective-permute-done.1.high, ...), custom_call_target="tpu_custom_call" | custom-call | tf_op jit(solution)/shard_map/place/pallas_call | solution.py:496
  16.6 7.9 %collective-permute-start.2 = (f32[36,16,128]{2,1,0:T(8,128)S(1)}, f32[36,16,128]{2,1,0:T(8,128)S(1)}, u32[]{:S(2)}, u32[]{:S(2)}) collective-permute-start(f32[36,16,128]{2,1,0:T(8,128)S(1)} %get-tuple-element.16.to_next), channel_id=1, source_target_pairs={{0,4},{4,8},{8,12},{12,16},{16,20},{20,24},{24,28},{28,32},{32,36}... | collective-permute-start | bytes 884744 | tf_op jit(solution)/shard_map/ppermute | solution.py:505
  24.5 1.9 %collective-permute-start.3 = (f32[36,16,128]{2,1,0:T(8,128)S(1)}, f32[36,16,128]{2,1,0:T(8,128)S(1)}, u32[]{:S(2)}, u32[]{:S(2)}) collective-permute-start(f32[36,16,128]{2,1,0:T(8,128)S(1)} %get-tuple-element.15.to_prev), channel_id=1, source_target_pairs={{4,0},{8,4},{12,8},{16,12},{20,16},{24,20},{28,24},{32,28},{36,32}... | collective-permute-start | bytes 884744 | tf_op jit(solution)/shard_map/ppermute | solution.py:506
  26.4 3.4 %collective-permute-start.4 = (f32[36,16,128]{2,1,0:T(8,128)S(1)}, f32[36,16,128]{2,1,0:T(8,128)S(1)}, u32[]{:S(2)}, u32[]{:S(2)}) collective-permute-start(f32[36,16,128]{2,1,0:T(8,128)S(1)} %get-tuple-element.14.to_sub.state), channel_id=1, source_target_pairs={{0,1},{1,2},{2,3},{3,0},{4,5},{5,6},{6,7},{7,4},{8,9},{9,10},{10,1... | collective-permute-start | bytes 884744 | tf_op jit(solution)/shard_map/ppermute | solution.py:504
  29.8 4.6 %collective-permute-start.5 = (f32[36,16,128]{2,1,0:T(8,128)S(1)}, f32[36,16,128]{2,1,0:T(8,128)S(1)}, u32[]{:S(2)}, u32[]{:S(2)}) collective-permute-start(f32[36,16,128]{2,1,0:T(8,128)S(1)} %get-tuple-element.14.to_sub.state), channel_id=1, source_target_pairs={{0,2},{1,3},{2,0},{3,1},{4,6},{5,7},{6,4},{7,5},{8,10},{9,11},{10,... | collective-permute-start | bytes 884744 | tf_op jit(solution)/shard_map/ppermute | solution.py:504
  34.4 3.3 %collective-permute-start.6 = (f32[36,16,128]{2,1,0:T(8,128)S(1)}, f32[36,16,128]{2,1,0:T(8,128)S(1)}, u32[]{:S(2)}, u32[]{:S(2)}) collective-permute-start(f32[36,16,128]{2,1,0:T(8,128)S(1)} %get-tuple-element.14.to_sub.state), channel_id=1, source_target_pairs={{0,3},{1,0},{2,1},{3,2},{4,7},{5,4},{6,5},{7,6},{8,11},{9,8},{10,9... | collective-permute-start | bytes 884744 | tf_op jit(solution)/shard_map/ppermute | solution.py:504
  37.8 10.3 %near_pairs.1 = (f32[384,128]{1,0:T(8,128)S(1)}, f32[48,16,128]{2,1,0:T(8,128)S(1)}) custom-call(s32[2,32]{1,0:T(2,128)S(1)} %copy-done.5, s32[32]{0:T(128)S(1)} %copy-done.6, f32[36,16,128]{2,1,0:T(8,128)S(1)} %get-tuple-element.15.to_prev, f32[36,16,128]{2,1,0:T(8,128)S(1)} %get-tuple-element.16.to_next, f32[36,16,128]{2,1,0:T(8,128)S(1)} %get-tuple-element.14.to_sub.state), custom_call_target="tpu_custom_call" | custom-call | flops 60000000 | bytes 400000 | tf_op jit(solution)/shard_map/near_pairs/pallas_call | solution.py:507
  48.1 0.0 collective-permute-done.2.rest_0_
  48.1 0.0 collective-permute-done.3.rest_1_
  48.1 6.6 %slab_pairs.1.before = f32[384,128]{1,0:T(8,128)S(1)} custom-call(s32[2,32]{1,0:T(2,128)S(1)} %copy-done.5, s32[32]{0:T(128)S(1)} %copy-done.6, f32[384,128]{1,0:T(8,128)S(1)} %get-tuple-element.17.before, f32[48,16,128]{2,1,0:T(8,128)S(1)} %get-tuple-element.18.scaled, f32[36,16,128]{2,1,0:T(8,128)S(1)} %collective-permute-done.2.rest_0_, ...), custom_call_target="tpu_custom_call" | custom-call | flops 60000000 | bytes 400000 | tf_op jit(solution)/shard_map/slab_pairs/pallas_call | solution.py:525
  54.7 0.0 collective-permute-done.4.rest_0_
  54.7 0.0 collective-permute-done.5.rest_1_
  54.7 0.0 collective-permute-done.6.rest_2_
  54.7 9.6 %sub_pairs.1.totals = f32[384,128]{1,0:T(8,128)S(1)} custom-call(s32[2,32]{1,0:T(2,128)S(1)} %copy-done.5, s32[32]{0:T(128)S(1)} %copy-done.6, f32[384,128]{1,0:T(8,128)S(1)} %slab_pairs.1.before, f32[48,16,128]{2,1,0:T(8,128)S(1)} %get-tuple-element.18.scaled, f32[36,16,128]{2,1,0:T(8,128)S(1)} %collective-permute-done.4.rest_0_, ...), custom_call_target="tpu_custom_call" | custom-call | flops 60000000 | bytes 400000 | tf_op jit(solution)/shard_map/sub_pairs/pallas_call | solution.py:525
  64.4 1.3 %final.1 = (f32[3,4096]{1,0:T(4,128)}, f32[3,4096]{1,0:T(4,128)}, f32[6,4096]{1,0:T(8,128)}) custom-call(f32[36,16,128]{2,1,0:T(8,128)S(1)} %get-tuple-element.14.to_sub.state, f32[384,128]{1,0:T(8,128)S(1)} %sub_pairs.1.totals, s32[3,512]{1,0:T(4,128)S(1)} %copy-done.2), custom_call_target="tpu_custom_call" | custom-call | tf_op jit(solution)/shard_map/final/pallas_call | solution.py:545
Async XLA Ops:
  0.6 0.7 copy-start.7
  1.3 0.9 %copy-start = (f32[6,4096]{1,0:T(8,128)S(1)}, f32[6,4096]{1,0:T(8,128)}, u32[]{:S(2)}) copy-start(f32[6,4096]{1,0:T(8,128)} %motion.1) | copy-start | bytes 294916
  2.2 0.8 %copy-start.1 = (f32[3,4096]{1,0:T(4,128)S(1)}, f32[3,4096]{1,0:T(4,128)}, u32[]{:S(2)}) copy-start(f32[3,4096]{1,0:T(4,128)} %positions.1) | copy-start | bytes 147460
  3.0 0.7 %copy-start.3 = (f32[4096]{0:T(1024)S(1)}, f32[4096]{0:T(1024)}, u32[]{:S(2)}) copy-start(f32[4096]{0:T(1024)} %param.10) | copy-start | bytes 49156
  3.8 0.7 %copy-start.4 = (f32[4096]{0:T(1024)S(1)}, f32[4096]{0:T(1024)}, u32[]{:S(2)}) copy-start(f32[4096]{0:T(1024)} %param.11) | copy-start | bytes 49156
  4.5 9.0 %copy-start.2 = (s32[3,512]{1,0:T(4,128)S(1)}, s32[3,512]{1,0:T(4,128)}, u32[]{:S(2)}) copy-start(s32[3,512]{1,0:T(4,128)} %rows.3) | copy-start | bytes 18436
  6.0 5.6 %collective-permute-start = (f32[4,16,128]{2,1,0:T(8,128)S(1)}, f32[4,16,128]{2,1,0:T(8,128)S(1)}, u32[]{:S(2)}, u32[]{:S(2)}) collective-permute-start(f32[4,16,128]{2,1,0:T(8,128)S(1)} %get-tuple-element.12), channel_id=1, source_target_pairs={{0,4},{4,8},{8,12},{12,16},{16,20},{20,24},{24,28},{28,32},{32,36}... | collective-permute-start | bytes 98312 | tf_op jit(solution)/shard_map/ppermute | solution.py:494
  8.0 5.5 %collective-permute-start.1 = (f32[4,16,128]{2,1,0:T(8,128)S(1)}, f32[4,16,128]{2,1,0:T(8,128)S(1)}, u32[]{:S(2)}, u32[]{:S(2)}) collective-permute-start(f32[4,16,128]{2,1,0:T(8,128)S(1)} %get-tuple-element.13), channel_id=1, source_target_pairs={{4,0},{8,4},{12,8},{16,12},{20,16},{24,20},{28,24},{32,28},{36,32}... | collective-permute-start | bytes 98312 | tf_op jit(solution)/shard_map/ppermute | solution.py:495
  13.5 0.7 %copy-start.5 = (s32[2,32]{1,0:T(2,128)S(1)}, s32[2,32]{1,0:T(2,128)}, u32[]{:S(2)}) copy-start(s32[2,32]{1,0:T(2,128)} %partners.7) | copy-start | bytes 772
  13.5 0.7 %copy-start.6 = (s32[32]{0:T(128)S(1)}, s32[32]{0:T(128)}, u32[]{:S(2)}) copy-start(s32[32]{0:T(128)} %live.5) | copy-start | bytes 388
  16.6 31.5 %collective-permute-start.2 = (f32[36,16,128]{2,1,0:T(8,128)S(1)}, f32[36,16,128]{2,1,0:T(8,128)S(1)}, u32[]{:S(2)}, u32[]{:S(2)}) collective-permute-start(f32[36,16,128]{2,1,0:T(8,128)S(1)} %get-tuple-element.16.to_next), channel_id=1, source_target_pairs={{0,4},{4,8},{8,12},{12,16},{16,20},{20,24},{24,28},{28,32},{32,36}... | collective-permute-start | bytes 884744 | tf_op jit(solution)/shard_map/ppermute | solution.py:505
  24.5 23.6 %collective-permute-start.3 = (f32[36,16,128]{2,1,0:T(8,128)S(1)}, f32[36,16,128]{2,1,0:T(8,128)S(1)}, u32[]{:S(2)}, u32[]{:S(2)}) collective-permute-start(f32[36,16,128]{2,1,0:T(8,128)S(1)} %get-tuple-element.15.to_prev), channel_id=1, source_target_pairs={{4,0},{8,4},{12,8},{16,12},{20,16},{24,20},{28,24},{32,28},{36,32}... | collective-permute-start | bytes 884744 | tf_op jit(solution)/shard_map/ppermute | solution.py:506
  26.4 28.3 %collective-permute-start.4 = (f32[36,16,128]{2,1,0:T(8,128)S(1)}, f32[36,16,128]{2,1,0:T(8,128)S(1)}, u32[]{:S(2)}, u32[]{:S(2)}) collective-permute-start(f32[36,16,128]{2,1,0:T(8,128)S(1)} %get-tuple-element.14.to_sub.state), channel_id=1, source_target_pairs={{0,1},{1,2},{2,3},{3,0},{4,5},{5,6},{6,7},{7,4},{8,9},{9,10},{10,1... | collective-permute-start | bytes 884744 | tf_op jit(solution)/shard_map/ppermute | solution.py:504
  29.8 24.9 %collective-permute-start.5 = (f32[36,16,128]{2,1,0:T(8,128)S(1)}, f32[36,16,128]{2,1,0:T(8,128)S(1)}, u32[]{:S(2)}, u32[]{:S(2)}) collective-permute-start(f32[36,16,128]{2,1,0:T(8,128)S(1)} %get-tuple-element.14.to_sub.state), channel_id=1, source_target_pairs={{0,2},{1,3},{2,0},{3,1},{4,6},{5,7},{6,4},{7,5},{8,10},{9,11},{10,... | collective-permute-start | bytes 884744 | tf_op jit(solution)/shard_map/ppermute | solution.py:504
  34.4 20.3 %collective-permute-start.6 = (f32[36,16,128]{2,1,0:T(8,128)S(1)}, f32[36,16,128]{2,1,0:T(8,128)S(1)}, u32[]{:S(2)}, u32[]{:S(2)}) collective-permute-start(f32[36,16,128]{2,1,0:T(8,128)S(1)} %get-tuple-element.14.to_sub.state), channel_id=1, source_target_pairs={{0,3},{1,0},{2,1},{3,2},{4,7},{5,4},{6,5},{7,6},{8,11},{9,8},{10,9... | collective-permute-start | bytes 884744 | tf_op jit(solution)/shard_map/ppermute | solution.py:504

commit v3 on v2

v3 whole, which is shorter than its diff:
```python
import jax
import jax.numpy as jnp
from jax import lax
from jax.experimental import pallas as pl
from jax.experimental.pallas import tpu as pltpu
from jax.sharding import PartitionSpec as P

min_distance = 0.2
stiffness = 1.0
normal_damp = 0.5
shear_damp = 0.3
surface_tension = 2.0
rupture_scale = 1.0
time_step = 0.005

LANES = 128
ROWS = 16
CAP = 4
FEATS = 16
MATS = 5
WIDE_ROWS = (0, 1, 2, 9, 10, 11)
GROUP = 4
CHOICES = 2
GHOST_TILES = 4

f32 = jnp.float32
bf16 = jnp.bfloat16
VMEM = pl.BlockSpec(memory_space=pltpu.VMEM)
HBM = pl.BlockSpec(memory_space=pltpu.HBM)
PARAMS = pltpu.CompilerParams(vmem_limit_bytes=40 * 1024 * 1024)


def split(value, parts):
    out = []
    for _ in range(parts - 1):
        high = value.astype(bf16)
        out.append(high)
        value = value - high.astype(f32)
    out.append(value.astype(bf16))
    return out


def dot_nn(left, right):
    return lax.dot_general(left, right, (((1,), (0,)), ((), ())), preferred_element_type=f32)


def dot_nt(left, right):
    return lax.dot_general(left, right, (((1,), (1,)), ((), ())), preferred_element_type=f32)


def partners_of(here):
    odd = lax.rem(here, 2)
    return odd, here + 1 - 2 * odd, here - 1 + 2 * odd


def pack_kernel(*refs):
    sources, (state, swap_a, swap_b), (moving, sems) = refs[:8], refs[8:11], refs[-2:]
    goal, place, speed, size, wet, rows, partners, live = refs[11:-2]
    copies = [
        pltpu.make_async_copy(source, target, sems.at[index])
        for index, (source, target) in enumerate(zip(sources, refs[11:-2]))
    ]
    for copy in copies:
        copy.start()
    here = lax.axis_index("slab")
    _, slab_a, slab_b = partners_of(here)
    blocks = state.shape[0] - 1
    swap_a[...] = jnp.zeros_like(swap_a)
    swap_b[...] = jnp.zeros_like(swap_b)
    for copy in copies:
        copy.wait()
    count_a = jnp.int32(0)
    count_b = jnp.int32(0)
    for block in range(blocks):
        columns = slice(block * LANES, (block + 1) * LANES)
        target = goal[block]
        moving[block, 0:3, :] = place[:, columns]
        moving[block, 3:9, :] = speed[:, columns]
        moving[block, 9:10, :] = size[block : block + 1, :]
        moving[block, 10:11, :] = wet[block : block + 1, :]
        moving[block, 11:16, :] = jnp.full((5, LANES), (target + 1).astype(f32), f32)
        slab = target // blocks
        goes_a = slab == slab_a
        goes_b = slab == slab_b

        @pl.when(slab == here)
        def _():
            state[target % blocks] = moving[block]

        @pl.when(goes_a)
        def _():
            swap_a[count_a] = moving[block]

        @pl.when(goes_b)
        def _():
            swap_b[count_b] = moving[block]

        count_a = jnp.minimum(count_a + goes_a.astype(jnp.int32), CAP - 1)
        count_b = jnp.minimum(count_b + goes_b.astype(jnp.int32), CAP - 1)
    state[blocks] = jnp.zeros((ROWS, LANES), f32)
    tiles = rows.shape[1] // LANES
    for which in range(3):
        for tile in range(tiles):
            state[blocks, which * tiles + tile : which * tiles + tile + 1, :] = rows[
                which : which + 1, tile * LANES : (tile + 1) * LANES
            ].astype(f32)
    for which in range(partners.shape[0]):
        state[blocks, 12 + which : 13 + which, 0:blocks] = jnp.where(
            live[...] > which, partners[which : which + 1, :], -1
        ).astype(f32)


def ghost_index(extra, which, tile, tiles, odd):
    rows = [extra[other * tiles + tile : other * tiles + tile + 1, :] for other in range(3)]
    row = rows[2] if which == 2 else jnp.where(odd == which, rows[1], rows[0])
    return row.astype(jnp.int32)


def place_kernel(state, low, high, to_a, to_b, to_sub):
    here = lax.axis_index("slab")
    odd, _, _ = partners_of(here)
    blocks = state.shape[0] - 1
    size = to_sub.shape[0] - blocks
    extra = state[blocks]
    base = (here * blocks + 1).astype(f32)
    arrived = [low[slot] for slot in range(CAP)] + [high[slot] for slot in range(CAP)]
    tags = [jnp.broadcast_to(block[11:12, :], (ROWS, LANES)) - base for block in arrived]
    for slot in range(blocks):
        current = state[slot]
        for block, tag in zip(arrived, tags):
            current = jnp.where(tag == float(slot), block, current)
        to_sub[slot] = current
        to_a[slot] = current
        to_b[slot] = current

    flat = to_sub[0:blocks].reshape(blocks * ROWS, LANES)
    left = jnp.concatenate(split(flat, 3), axis=1)
    lane_ids = lax.broadcasted_iota(jnp.int32, (LANES, LANES), 0)
    for which, message in enumerate((to_a, to_b, to_sub)):
        for tile in range(message.shape[0] - blocks):
            index = ghost_index(extra, which, tile, size, odd)
            hot = jnp.where(lane_ids == index % LANES, 1.0, 0.0).astype(bf16)
            picked = dot_nn(left, jnp.concatenate([hot, hot, hot], axis=0))
            source = jnp.broadcast_to(index // LANES, (ROWS, LANES))
            total = jnp.zeros((ROWS, LANES), f32)
            for block in range(blocks):
                total = jnp.where(source == block, picked[block * ROWS : (block + 1) * ROWS], total)
            message[blocks + tile] = total
        message[blocks, 11:13, :] = extra[12:14, :]


def cross(first, second):
    return [
        first[1] * second[2] - first[2] * second[1],
        first[2] * second[0] - first[0] * second[2],
        first[0] * second[1] - first[1] * second[0],
    ]


def recip(value):
    guess = pl.reciprocal(value, approx=True)
    return guess * (2.0 - value * guess)


def dot_rows(first, second):
    return first[0] * second[0] + first[1] * second[1] + first[2] * second[2]


def scale(tile):
    radius, liquid = tile[9:10, :], tile[10:11, :]
    turn = radius * tile[6:9, :]
    bond = radius * jnp.sqrt(surface_tension * liquid)
    place = [tile[row : row + 1, :] for row in range(3)]
    along = dot_rows(place, [tile[row : row + 1, :] for row in range(3, 6)])
    twist = dot_rows(place, [turn[row : row + 1, :] for row in range(3)])
    one = jnp.ones((1, LANES), f32)
    return jnp.concatenate(
        [tile[0:6, :], turn, radius, rupture_scale * liquid, bond, along, one, twist, 0.0 * one],
        axis=0,
    )


def mirror(scaled):
    place, velocity, turn = scaled[0:3, :], scaled[3:6, :], scaled[6:9, :]
    along, one, twist, zero = [scaled[row : row + 1, :] for row in range(12, 16)]
    blank = jnp.broadcast_to(zero, (6, LANES))
    damp = normal_damp - shear_damp
    moving = jnp.concatenate([-velocity, -place, blank, one, along, zero, zero], axis=0)
    turning = jnp.concatenate(
        [-turn, blank[0:3], place, blank[0:3], zero, twist, -one, zero], axis=0
    )
    return jnp.concatenate([damp * moving, turning], axis=0)


def six(value, order):
    parts = split(value, 3)
    return jnp.concatenate([parts[index] for index in order], axis=0)


def features(scaled):
    rows = [scaled[row : row + 1, :] for row in range(9)]
    place, velocity, turn = rows[0:3], rows[3:6], rows[6:9]
    one = jnp.ones((1, LANES), f32)
    values = jnp.concatenate(
        place + [one] + velocity + turn + cross(turn, place) + cross(place, velocity), axis=0
    )
    return jnp.concatenate(split(values, 3), axis=0)


def fill_spread(spread):
    rows = lax.broadcasted_iota(jnp.int32, (6 * ROWS, LANES), 0)
    part = rows // ROWS
    first = (part == 0) | (part == 3) | (part == 5)
    for block, row in enumerate(WIDE_ROWS):
        hot = first & (rows % ROWS == row)
        spread[:, block * LANES : (block + 1) * LANES] = jnp.where(hot, 1.0, 0.0).astype(bf16)


def pair_scalars(near, far, far_mirror, spread, coefs):
    moving = six(far_mirror[0:ROWS], (0, 1, 2, 0, 1, 0))
    turning = six(far_mirror[ROWS:], (0, 1, 2, 0, 1, 0))
    columns = lax.dot_general(
        six(near, (0, 0, 0, 1, 1, 2)),
        jnp.concatenate([spread[...], moving, turning], axis=1),
        (((0,), (0,)), ((), ())),
        preferred_element_type=f32,
    )
    far_rows = [far[row : row + 1, :] for row in WIDE_ROWS]
    step = 16
    for start in range(0, LANES, step):
        col = [
            columns[start : start + step, block * LANES : (block + 1) * LANES] for block in range(8)
        ]
        offset = [far_rows[row] - col[row] for row in range(3)]
        along, twist = col[6], col[7]
        square = dot_rows(offset, offset)
        root = lax.rsqrt(jnp.maximum(square, 1e-30))
        inverse = jnp.minimum(root, 1.0 / min_distance)
        gap = square * root - (far_rows[3] + col[3])
        apart = jnp.maximum(gap, 0.0)
        overlap = apart - gap
        over_radii = recip(far_rows[3] + col[3])
        inner = far_rows[3] * col[3] * over_radii * overlap
        spread_pair = inner * lax.rsqrt(jnp.maximum(inner, 1e-30))
        fill = jnp.maximum(1.0 - apart * recip(far_rows[4] + col[4]), 0.0)
        bridge = far_rows[5] * col[5] * over_radii * (fill * fill)
        inverse1 = spread_pair * inverse
        inverse2 = inverse1 * inverse
        mats = [
            (bridge - spread_pair * (overlap - along * inverse)) * inverse,
            spread_pair,
            inverse1,
            inverse2 * square,
            inverse2 * twist,
        ]
        for index, mat in enumerate(mats):
            high, low = split(mat, 2)
            coefs[index * LANES + start : index * LANES + start + step, 0:LANES] = high
            coefs[index * LANES + start : index * LANES + start + step, LANES:] = low


def add_own(first, far_feats, sums, coefs):
    own = dot_nt(jnp.concatenate([far_feats, far_feats], axis=1), coefs[...])
    own = own[0:FEATS] + own[FEATS : 2 * FEATS] + own[2 * FEATS :]
    base = pl.multiple_of(first * (MATS * FEATS), 16)
    for index in range(MATS):
        sums[pl.ds(base + index * FEATS, FEATS), :] += own[:, index * LANES : (index + 1) * LANES]


def add_back(second, near_feats, sums, coefs):
    base = pl.multiple_of(second * (MATS * FEATS), 16)
    for index in range(MATS):
        back = dot_nn(near_feats, coefs[index * LANES : (index + 1) * LANES, :])
        back = back[:, 0:LANES] + back[:, LANES:]
        back = back[0:FEATS] + back[FEATS : 2 * FEATS] + back[2 * FEATS :]
        if index == MATS - 1:
            back = -back
        sums[pl.ds(base + index * FEATS, FEATS), :] += back


def finish(group, sums, scaled):
    span = MATS * FEATS

    def total(mat, feat):
        return sums[pl.ds(group * 8 * span + mat * FEATS + feat, 8, stride=span), :]

    def own(row):
        return scaled[pl.ds(group * 8, 8), row, :]

    place = [own(row) for row in range(3)]
    velocity = [own(row) for row in range(3, 6)]
    turn = [own(row) for row in range(6, 9)]
    radius = own(9)
    s_place = [total(0, feat) for feat in range(3)]
    s_one = total(0, 3)
    c_one = total(1, 3)
    c_velocity = [total(1, feat) for feat in range(4, 7)]
    n_place = [total(2, feat) for feat in range(3)]
    n_one = total(2, 3)
    n_velocity = [total(2, feat) for feat in range(4, 7)]
    n_turn = [total(2, feat) for feat in range(7, 10)]
    n_turn_place = [total(2, feat) for feat in range(10, 13)]
    n_place_velocity = [total(2, feat) for feat in range(13, 16)]
    k_one = total(3, 3)
    k_turn = [total(3, feat) for feat in range(7, 10)]
    g_place = [total(4, feat) for feat in range(3)]
    g_one = total(4, 3)
    turn_place = cross(turn, place)
    place_velocity = cross(place, velocity)
    first = cross(turn, n_place)
    second = cross(n_turn, place)
    third = cross(n_place, velocity)
    fourth = cross(place, n_velocity)
    force = [
        (s_place[x] - place[x] * s_one)
        + shear_damp
        * (
            (c_velocity[x] - velocity[x] * c_one)
            - (first[x] - turn_place[x] * n_one + n_turn_place[x] - second[x])
        )
        for x in range(3)
    ]
    torque = [
        shear_damp
        * radius
        * (
            (n_place_velocity[x] - third[x] - fourth[x] + place_velocity[x] * n_one)
            - (turn[x] * k_one + k_turn[x])
            + (g_place[x] - place[x] * g_one)
        )
        for x in range(3)
    ]
    return force + torque


def run_pairs(count, todo, coefs, load, scalars, add):
    def some_pairs(index, carry):
        items = [load(index * GROUP + lane) for lane in range(GROUP)]
        for lane in range(GROUP + 1):
            if lane < GROUP:
                scalars(items[lane], coefs[lane])
            if lane > 0:
                add(items[lane - 1], coefs[lane - 1])
        return carry

    lax.fori_loop(0, (count + GROUP - 1) // GROUP, some_pairs, 0)


def list_far(count, message, heard, number, theirs, ours, ghost, blocks, picked, todo):
    size = message.shape[0] - blocks
    start = count
    for tile in range(blocks):
        for which in range(CHOICES):
            shift = heard[which, tile] - theirs
            wanted = (shift >= 0) & (shift < size)
            todo[count] = tile * 64 + blocks + shift
            count = count + wanted.astype(jnp.int32)
            shift = heard[(number + 1) * CHOICES + which, tile] - ours
            wanted = (shift >= 0) & (shift < size)
            todo[count] = (ghost + shift) * 64 + tile
            count = count + wanted.astype(jnp.int32)

    def pick(index, carry):
        picked[index] = scale(message[todo[index] % 64])
        return carry

    lax.fori_loop(start, count, pick, 0)
    return count


def hear(messages, blocks, codes, heard, sem):
    for number, message in enumerate(messages):
        codes[number * CHOICES : (number + 1) * CHOICES, :] = message[
            blocks, 11 : 11 + CHOICES, :
        ].astype(jnp.int32)
    copy = pltpu.make_async_copy(codes, heard, sem)
    copy.start()
    return copy


def far_pairs(messages, places, tiles, sums, spread, picked, heard, todo, coefs):
    spare = tiles.shape[0] - 1
    blocks = messages[0].shape[0] - GHOST_TILES
    count = jnp.int32(0)
    for number, (message, (theirs, ours, ghost)) in enumerate(zip(messages, places)):
        count = list_far(count, message, heard, number, theirs, ours, ghost, blocks, picked, todo)
    for extra in range(GROUP):
        todo[count + extra] = spare * 64
        picked[count + extra] = tiles[spare, 0:ROWS]

    def load(index):
        return todo[index] // 64, picked[index]

    def scalars(item, coef):
        mine, near = item
        pair_scalars(near, tiles[mine, 0:ROWS], tiles[mine, ROWS:], spread, coef)

    def add(item, coef):
        add_back(item[0], features(item[1]), sums, coef)

    run_pairs(count, todo, coefs, load, scalars, add)


def slab_kernel(to_a, to_b, to_sub, from_a, from_b, totals, tiles, feats, sums, spread, *rest):
    picked, codes, heard, todo, sem = rest[:5]
    coefs = rest[5:]
    own_tiles = to_sub.shape[0]
    size = GHOST_TILES
    blocks = own_tiles - size
    copy = hear([to_sub, from_a, from_b], blocks, codes, heard, sem)
    spare = tiles.shape[0] - 1

    def enter(slot, tile):
        rows = scale(tile)
        tiles[slot, 0:ROWS] = rows
        tiles[slot, ROWS:] = mirror(rows)
        return rows

    fill_spread(spread)
    sums[...] = jnp.zeros_like(sums)
    for tile in range(own_tiles):
        feats[tile] = features(enter(tile, to_sub[tile]))
    for tile in range(size):
        enter(own_tiles + tile, to_a[blocks + tile])
        enter(own_tiles + size + tile, to_b[blocks + tile])
    for tile in range(own_tiles + 2 * size, spare + 1):
        feats[spare] = features(enter(tile, jnp.ones((ROWS, LANES), f32)))
    copy.wait()
    shared = blocks + (2 + lax.axis_index("sub")) * size
    count = jnp.int32(0)
    for tile in range(blocks):
        for which in range(CHOICES):
            partner = heard[which, tile]
            mine = (partner >= shared) & (partner < shared + size)
            wanted = ((partner >= 0) & (partner < blocks)) | mine
            slot = jnp.where(mine, partner - shared + blocks, partner)
            todo[count] = tile * 64 + slot
            count = count + wanted.astype(jnp.int32)
    for extra in range(GROUP):
        todo[count + extra] = spare * 64 + spare

    def load(index):
        return todo[index] // 64, todo[index] % 64

    def scalars(item, coef):
        first, second = item
        pair_scalars(tiles[first, 0:ROWS], tiles[second, 0:ROWS], tiles[second, ROWS:], spread, coef)

    def add(item, coef):
        first, second = item
        add_own(first, feats[second], sums, coef)
        add_back(second, feats[first], sums, coef)

    run_pairs(count, todo, coefs, load, scalars, add)
    odd, _, _ = partners_of(lax.axis_index("slab"))
    low, high = blocks + odd * size, blocks + (1 - odd) * size
    places = [(high, low, own_tiles), (low, high, own_tiles + size)]
    far_pairs([from_a, from_b], places, tiles, sums, spread, picked, heard, todo, coefs)
    for group in range(tiles.shape[0] // 8):
        for row, value in enumerate(finish(group, sums, tiles)):
            totals[pl.ds(group * 64 + row, 8, stride=8), :] = value


def sub_kernel(before, tiles, state, extra, *rest):
    messages = rest[: -11 - GROUP]
    force, torque, kicked, totals, sums, spread, picked, codes, heard, todo, sem = rest[
        -11 - GROUP : -GROUP
    ]
    coefs = rest[-GROUP:]
    size = GHOST_TILES
    blocks = state.shape[0] - size
    copy = hear([state, *messages], blocks, codes, heard, sem)
    fill_spread(spread)
    sums[...] = jnp.zeros_like(sums)
    copy.wait()
    sub = lax.axis_index("sub")
    ours = blocks + (2 + sub) * size
    places = [
        (blocks + (2 + lax.bitwise_xor(sub, number + 1)) * size, ours, blocks)
        for number in range(len(messages))
    ]
    far_pairs(messages, places, tiles, sums, spread, picked, heard, todo, coefs)
    for group in range(tiles.shape[0] // 8):
        for row, value in enumerate(finish(group, sums, tiles)):
            part = pl.ds(group * 64 + row, 8, stride=8)
            totals[part, :] = before[part, :] + value
    settle(state, totals, extra[blocks], force, torque, kicked)


def settle(state, totals, extra, force, torque, kicked):
    odd, _, _ = partners_of(lax.axis_index("slab"))
    size = GHOST_TILES
    blocks = state.shape[0] - size
    lane_ids = lax.broadcasted_iota(jnp.int32, (LANES, LANES), 0)
    hots = []
    lefts = []
    for which in range(3):
        for tile in range(size):
            index = ghost_index(extra, which, tile, size, odd)
            hots.append(jnp.where(lane_ids == index % LANES, 1.0, 0.0).astype(bf16))
            ghost = blocks + (which + 1) % 3 * size + tile
            value = totals[ghost * 8 : ghost * 8 + 8, :]
            high = value.astype(bf16).astype(f32)
            both = jnp.concatenate([high, value - high], axis=0)
            source = jnp.broadcast_to(index // LANES, (ROWS, LANES))
            lefts.append(
                jnp.concatenate(
                    [
                        jnp.where(source == block, both, 0.0).astype(bf16)
                        for block in range(blocks)
                    ],
                    axis=0,
                )
            )
    added = dot_nt(jnp.concatenate(lefts, axis=1), jnp.concatenate(hots, axis=1))
    row_ids = lax.broadcasted_iota(jnp.int32, (8, LANES), 0)
    for block in range(blocks):
        columns = slice(block * LANES, (block + 1) * LANES)
        extra = added[block * ROWS : block * ROWS + 8] + added[block * ROWS + 8 : block * ROWS + 16]
        total = totals[block * 8 : block * 8 + 8, :] + extra
        radius = state[block, 9:10, :]
        mass = radius * radius * radius
        inertia = 0.4 * mass * radius * radius
        weight = jnp.where(row_ids < 3, time_step / mass, time_step / inertia)
        force[:, columns] = total[0:3]
        torque[:, columns] = total[3:6]
        kicked[:, columns] = state[block, 3:9, :] + (total * weight)[0:6]


def shape(*dims, dtype=f32):
    return jax.ShapeDtypeStruct(dims, dtype)


def body(positions, motion, radius, liquid, new_owner, ghost_rows, partner_tiles, live_pairs):
    per_dev = positions.shape[1]
    blocks = per_dev // LANES
    size = ghost_rows.shape[1] // LANES
    choices = partner_tiles.shape[0]
    tiles = -(-(blocks + 3 * size + 1) // 8) * 8
    slabs = lax.axis_size("slab")
    subs = lax.axis_size("sub")
    inside = [(i, i ^ 1) for i in range(slabs) if i ^ 1 < slabs]
    across = [(i, (i - 1 ^ 1) + 1) for i in range(1, slabs) if (i - 1 ^ 1) + 1 < slabs]

    state, swap_a, swap_b = pl.pallas_call(
        pack_kernel,
        out_shape=(
            shape(blocks + 1, ROWS, LANES),
            shape(CAP, ROWS, LANES),
            shape(CAP, ROWS, LANES),
        ),
        in_specs=[HBM] * 8,
        out_specs=(VMEM,) * 3,
        scratch_shapes=[
            pltpu.SMEM((blocks,), jnp.int32),
            pltpu.VMEM((3, per_dev), f32),
            pltpu.VMEM((6, per_dev), f32),
            pltpu.VMEM((blocks, LANES), f32),
            pltpu.VMEM((blocks, LANES), f32),
            pltpu.VMEM(ghost_rows.shape, jnp.int32),
            pltpu.VMEM(partner_tiles.shape, jnp.int32),
            pltpu.VMEM((1, blocks), jnp.int32),
            pltpu.VMEM((blocks, ROWS, LANES), f32),
            pltpu.SemaphoreType.DMA((8,)),
        ],
        compiler_params=pltpu.CompilerParams(vmem_limit_bytes=60 * 1024 * 1024),
        name="pack",
    )(
        new_owner,
        positions,
        motion,
        radius.reshape(blocks, LANES),
        liquid.reshape(blocks, LANES),
        ghost_rows,
        partner_tiles,
        live_pairs.reshape(1, blocks),
    )
    low = lax.ppermute(swap_a, "slab", inside)
    high = lax.ppermute(swap_b, "slab", across)
    to_a, to_b, to_sub = pl.pallas_call(
        place_kernel,
        out_shape=(shape(blocks + size, ROWS, LANES),) * 3,
        in_specs=[VMEM] * 3,
        out_specs=(VMEM,) * 3,
        compiler_params=PARAMS,
        name="place",
    )(state, low, high)
    from_a = lax.ppermute(to_a, "slab", inside)
    from_b = lax.ppermute(to_b, "slab", across)
    from_sub = [
        lax.ppermute(to_sub, "sub", [(i, i ^ d) for i in range(subs)]) for d in range(1, subs)
    ]

    def work(messages):
        room = choices * blocks * (1 + messages) + GROUP
        return [
            pltpu.VMEM((tiles * MATS * FEATS, LANES), f32),
            pltpu.VMEM((6 * ROWS, len(WIDE_ROWS) * LANES), bf16),
            pltpu.VMEM((room, ROWS, LANES), f32),
            pltpu.VMEM((8, LANES), jnp.int32),
            pltpu.SMEM((8, LANES), jnp.int32),
            pltpu.SMEM((room,), jnp.int32),
            pltpu.SemaphoreType.DMA(()),
        ] + [pltpu.VMEM((MATS * LANES, 2 * LANES), bf16)] * GROUP

    totals, table = pl.pallas_call(
        slab_kernel,
        out_shape=(shape(tiles * 8, LANES), shape(tiles, 3 * ROWS, LANES)),
        in_specs=[VMEM] * 5,
        out_specs=(VMEM, VMEM),
        scratch_shapes=[pltpu.VMEM((tiles, 3 * FEATS, LANES), bf16)] + work(2),
        compiler_params=PARAMS,
        cost_estimate=pl.CostEstimate(flops=90000000, bytes_accessed=400000, transcendentals=0),
        name="slab_pairs",
    )(to_a, to_b, to_sub, from_a, from_b)
    return tuple(
        pl.pallas_call(
            sub_kernel,
            out_shape=(shape(3, per_dev), shape(3, per_dev), shape(6, per_dev)),
            in_specs=[VMEM] * (4 + len(from_sub)),
            out_specs=(VMEM,) * 3,
            scratch_shapes=[pltpu.VMEM((tiles * 8, LANES), f32)] + work(len(from_sub)),
            compiler_params=PARAMS,
            name="sub_pairs",
        )(totals, table, to_sub, state, *from_sub)
    )


def solution(mesh):
    return jax.shard_map(
        body,
        mesh=mesh,
        in_specs=(
            P(None, ("slab", "sub")),
            P(None, ("slab", "sub")),
            P(("slab", "sub")),
            P(("slab", "sub")),
            P(("slab", "sub")),
            P(None, ("slab", "sub")),
            P(None, ("slab", "sub")),
            P(("slab", "sub")),
        ),
        out_specs=(P(None, ("slab", "sub")), P(None, ("slab", "sub")), P(None, ("slab", "sub"))),
        check_vma=False,
    )
```

time: 66.1 us -> 56.7 us (0.86)
  the two profiles are of different devices: /device:TPU:248 before, /device:TPU:324 now
where the time goes in v3:
time: 56.7 us; the launch traced here: 56.4 us
  Pallas kernels  28 us (49%)
  starting transfers between devices  24.6 us (43%)
  waiting for transfers between devices  2.09 us (4%)
  local copies, waits for them, and re-layouts  0.96 us (2%)
  between operations  0.77 us (1%)
    pallas_call x1, Pallas kernels, body(): pl.pallas_call(slab_kernel, out_shape=(shape(tiles * 8, LANES), shape(til...  14.5 us
    ppermute x3, starting transfers between devices, body(): lax.ppermute(to_sub, 'sub', [(i, i ^ d) for i in range(subs)])  9.82 us
    pallas_call x1, Pallas kernels, body(): pl.pallas_call(sub_kernel, out_shape=(shape(3, per_dev), shape(3, per_dev...  9.41 us
    ppermute x1, starting transfers between devices, body(): from_b = lax.ppermute(to_b, 'slab', across)  5.46 us
    ppermute x1, starting transfers between devices, body(): high = lax.ppermute(swap_b, 'slab', across)  5.46 us
    pallas_call x1, Pallas kernels, body(): pl.pallas_call(pack_kernel, out_shape=(shape(blocks + 1, ROWS, LANES), sh...  2.57 us
    ppermute x1, waiting for transfers between devices, body(): high = lax.ppermute(swap_b, 'slab', across)  2.07 us
    ppermute x1, starting transfers between devices, body(): from_a = lax.ppermute(to_a, 'slab', inside)  1.92 us
  transfers between devices with their start and end apart: 7, of which 1 were waited for; matrix products, arithmetic and copies ran while one was open for 0% of the time, Pallas kernels for 26%

profile of v3, /device:TPU:324, one launch (start us, length us, event | category | flops | bytes accessed | tf_op | source)
XLA Modules:
  0.0 56.4 jit_solution(8714031402901687693)
XLA Ops:
  0.6 2.6 %pack.1 = (f32[33,16,128]{2,1,0:T(8,128)}, f32[4,16,128]{2,1,0:T(8,128)}, f32[4,16,128]{2,1,0:T(8,128)}) custom-call(s32[32]{0:T(128)} %refs_0_.1, f32[3,4096]{1,0:T(4,128)} %refs_1_.1, f32[6,4096]{1,0:T(8,128)} %refs_2_.1, f32[32,128]{1,0:T(8,128)} %bitcast.3, f32[32,128]{1,0:T(8,128)} %bitcast.4, s32[3,512]{1,0:T(4,128)} %refs_5_.1, s32[2,32]{1,0:T(2,128)} %refs_6_.1, ...), custom_call_target="tpu_custom_call" | custom-call | tf_op jit(solution)/shard_map/pack/pallas_call | solution.py:545
  3.2 1.9 %collective-permute-start = (f32[4,16,128]{2,1,0:T(8,128)}, f32[4,16,128]{2,1,0:T(8,128)S(1)}, u32[]{:S(2)}, u32[]{:S(2)}) collective-permute-start(f32[4,16,128]{2,1,0:T(8,128)} %get-tuple-element.12), channel_id=1, source_target_pairs={{0,4},{4,0},{8,12},{12,8},{16,20},{20,16},{24,28},{28,24},{32,36},... | collective-permute-start | bytes 98312 | tf_op jit(solution)/shard_map/ppermute | solution.py:578
  5.1 5.5 %collective-permute-start.1 = (f32[4,16,128]{2,1,0:T(8,128)}, f32[4,16,128]{2,1,0:T(8,128)S(1)}, u32[]{:S(2)}, u32[]{:S(2)}) collective-permute-start(f32[4,16,128]{2,1,0:T(8,128)} %get-tuple-element.13), channel_id=1, source_target_pairs={{4,8},{8,4},{12,16},{16,12},{20,24},{24,20},{28,32},{32,28},{36,40... | collective-permute-start | bytes 98312 | tf_op jit(solution)/shard_map/ppermute | solution.py:579
  10.6 0.0 collective-permute-done.low
  10.6 2.1 %collective-permute-done.1.high = f32[4,16,128]{2,1,0:T(8,128)S(1)} collective-permute-done((f32[4,16,128]{2,1,0:T(8,128)}, f32[4,16,128]{2,1,0:T(8,128)S(1)}, u32[]{:S(2)}, u32[]{:S(2)}) %collective-permute-start.1) | collective-permute-done | bytes 32800 | tf_op jit(solution)/shard_map/ppermute | solution.py:579
  12.7 0.0 copy-start
  12.7 1.0 %copy-done = f32[33,16,128]{2,1,0:T(8,128)S(1)} copy-done((f32[33,16,128]{2,1,0:T(8,128)S(1)}, f32[33,16,128]{2,1,0:T(8,128)}, u32[]{:S(2)}) %copy-start) | copy-done | bytes 270360
  13.6 0.0 copy-start.1
  13.6 1.5 %place.1 = (f32[36,16,128]{2,1,0:T(8,128)S(1)}, f32[36,16,128]{2,1,0:T(8,128)S(1)}, f32[36,16,128]{2,1,0:T(8,128)S(1)}) custom-call(f32[33,16,128]{2,1,0:T(8,128)S(1)} %copy-done, f32[4,16,128]{2,1,0:T(8,128)S(1)} %collective-permute-done.low, f32[4,16,128]{2,1,0:T(8,128)S(1)} %collective-permute-done.1.high), custom_call_target="tpu_custom_call" | custom-call | tf_op jit(solution)/shard_map/place/pallas_call | solution.py:580
  15.1 1.9 %collective-permute-start.2 = (f32[36,16,128]{2,1,0:T(8,128)S(1)}, f32[36,16,128]{2,1,0:T(8,128)S(1)}, u32[]{:S(2)}, u32[]{:S(2)}) collective-permute-start(f32[36,16,128]{2,1,0:T(8,128)S(1)} %get-tuple-element.14.to_a), channel_id=1, source_target_pairs={{0,4},{4,0},{8,12},{12,8},{16,20},{20,16},{24,28},{28,24},{32,36},... | collective-permute-start | bytes 884744 | tf_op jit(solution)/shard_map/ppermute | solution.py:588
  17.0 5.5 %collective-permute-start.3 = (f32[36,16,128]{2,1,0:T(8,128)S(1)}, f32[36,16,128]{2,1,0:T(8,128)S(1)}, u32[]{:S(2)}, u32[]{:S(2)}) collective-permute-start(f32[36,16,128]{2,1,0:T(8,128)S(1)} %get-tuple-element.15.to_b), channel_id=1, source_target_pairs={{4,8},{8,4},{12,16},{16,12},{20,24},{24,20},{28,32},{32,28},{36,40... | collective-permute-start | bytes 884744 | tf_op jit(solution)/shard_map/ppermute | solution.py:589
  22.5 2.4 %collective-permute-start.6 = (f32[36,16,128]{2,1,0:T(8,128)S(1)}, f32[36,16,128]{2,1,0:T(8,128)S(1)}, u32[]{:S(2)}, u32[]{:S(2)}) collective-permute-start(f32[36,16,128]{2,1,0:T(8,128)S(1)} %get-tuple-element.16.to_sub.state), channel_id=1, source_target_pairs={{0,3},{1,2},{2,1},{3,0},{4,7},{5,6},{6,5},{7,4},{8,11},{9,10},{10,... | collective-permute-start | bytes 884744 | tf_op jit(solution)/shard_map/ppermute | solution.py:591
  25.0 4.6 %collective-permute-start.5 = (f32[36,16,128]{2,1,0:T(8,128)S(1)}, f32[36,16,128]{2,1,0:T(8,128)S(1)}, u32[]{:S(2)}, u32[]{:S(2)}) collective-permute-start(f32[36,16,128]{2,1,0:T(8,128)S(1)} %get-tuple-element.16.to_sub.state), channel_id=1, source_target_pairs={{0,2},{1,3},{2,0},{3,1},{4,6},{5,7},{6,4},{7,5},{8,10},{9,11},{10,... | collective-permute-start | bytes 884744 | tf_op jit(solution)/shard_map/ppermute | solution.py:591
  29.6 2.7 %collective-permute-start.4 = (f32[36,16,128]{2,1,0:T(8,128)S(1)}, f32[36,16,128]{2,1,0:T(8,128)S(1)}, u32[]{:S(2)}, u32[]{:S(2)}) collective-permute-start(f32[36,16,128]{2,1,0:T(8,128)S(1)} %get-tuple-element.16.to_sub.state), channel_id=1, source_target_pairs={{0,1},{1,0},{2,3},{3,2},{4,5},{5,4},{6,7},{7,6},{8,9},{9,8},{10,11... | collective-permute-start | bytes 884744 | tf_op jit(solution)/shard_map/ppermute | solution.py:591
  32.4 0.0 collective-permute-done.2.from_a
  32.4 0.0 collective-permute-done.3.from_b
  32.4 14.5 %slab_pairs.1 = (f32[384,128]{1,0:T(8,128)S(1)}, f32[48,48,128]{2,1,0:T(8,128)S(1)}) custom-call(f32[36,16,128]{2,1,0:T(8,128)S(1)} %get-tuple-element.14.to_a, f32[36,16,128]{2,1,0:T(8,128)S(1)} %get-tuple-element.15.to_b, f32[36,16,128]{2,1,0:T(8,128)S(1)} %get-tuple-element.16.to_sub.state, f32[36,16,128]{2,1,0:T(8,128)S(1)} %collective-permute-done.2.from_a, ...), custom_call_target="tpu_custom_call" | custom-call | flops 90000000 | bytes 400000 | tf_op jit(solution)/shard_map/slab_pairs/pallas_call | solution.py:606
  46.9 0.0 collective-permute-done.6.rest_2_
  46.9 0.0 collective-permute-done.5.rest_1_
  46.9 0.0 collective-permute-done.4.rest_0_
  47.0 0.0 copy-done.1
  47.0 9.4 %sub_pairs.1 = (f32[3,4096]{1,0:T(4,128)}, f32[3,4096]{1,0:T(4,128)}, f32[6,4096]{1,0:T(8,128)}) custom-call(f32[384,128]{1,0:T(8,128)S(1)} %get-tuple-element.17.before, f32[48,48,128]{2,1,0:T(8,128)S(1)} %get-tuple-element.18.tiles, f32[36,16,128]{2,1,0:T(8,128)S(1)} %get-tuple-element.16.to_sub.state, f32[33,16,128]{2,1,0:T(8,128)S(1)} %copy-done.1, ...), custom_call_target="tpu_custom_call" | custom-call | tf_op jit(solution)/shard_map/sub_pairs/pallas_call | solution.py:617
Async XLA Ops:
  3.2 7.4 %collective-permute-start = (f32[4,16,128]{2,1,0:T(8,128)}, f32[4,16,128]{2,1,0:T(8,128)S(1)}, u32[]{:S(2)}, u32[]{:S(2)}) collective-permute-start(f32[4,16,128]{2,1,0:T(8,128)} %get-tuple-element.12), channel_id=1, source_target_pairs={{0,4},{4,0},{8,12},{12,8},{16,20},{20,16},{24,28},{28,24},{32,36},... | collective-permute-start | bytes 98312 | tf_op jit(solution)/shard_map/ppermute | solution.py:578
  5.1 7.6 %collective-permute-start.1 = (f32[4,16,128]{2,1,0:T(8,128)}, f32[4,16,128]{2,1,0:T(8,128)S(1)}, u32[]{:S(2)}, u32[]{:S(2)}) collective-permute-start(f32[4,16,128]{2,1,0:T(8,128)} %get-tuple-element.13), channel_id=1, source_target_pairs={{4,8},{8,4},{12,16},{16,12},{20,24},{24,20},{28,32},{32,28},{36,40... | collective-permute-start | bytes 98312 | tf_op jit(solution)/shard_map/ppermute | solution.py:579
  12.7 1.0 %copy-start = (f32[33,16,128]{2,1,0:T(8,128)S(1)}, f32[33,16,128]{2,1,0:T(8,128)}, u32[]{:S(2)}) copy-start(f32[33,16,128]{2,1,0:T(8,128)} %get-tuple-element.11.state.extra) | copy-start | bytes 811012
  13.6 33.3 %copy-start.1 = (f32[33,16,128]{2,1,0:T(8,128)S(1)}, f32[33,16,128]{2,1,0:T(8,128)}, u32[]{:S(2)}) copy-start(f32[33,16,128]{2,1,0:T(8,128)} %get-tuple-element.11.state.extra) | copy-start | bytes 811012
  15.1 17.2 %collective-permute-start.2 = (f32[36,16,128]{2,1,0:T(8,128)S(1)}, f32[36,16,128]{2,1,0:T(8,128)S(1)}, u32[]{:S(2)}, u32[]{:S(2)}) collective-permute-start(f32[36,16,128]{2,1,0:T(8,128)S(1)} %get-tuple-element.14.to_a), channel_id=1, source_target_pairs={{0,4},{4,0},{8,12},{12,8},{16,20},{20,16},{24,28},{28,24},{32,36},... | collective-permute-start | bytes 884744 | tf_op jit(solution)/shard_map/ppermute | solution.py:588
  17.0 15.3 %collective-permute-start.3 = (f32[36,16,128]{2,1,0:T(8,128)S(1)}, f32[36,16,128]{2,1,0:T(8,128)S(1)}, u32[]{:S(2)}, u32[]{:S(2)}) collective-permute-start(f32[36,16,128]{2,1,0:T(8,128)S(1)} %get-tuple-element.15.to_b), channel_id=1, source_target_pairs={{4,8},{8,4},{12,16},{16,12},{20,24},{24,20},{28,32},{32,28},{36,40... | collective-permute-start | bytes 884744 | tf_op jit(solution)/shard_map/ppermute | solution.py:589
  22.5 24.4 %collective-permute-start.6 = (f32[36,16,128]{2,1,0:T(8,128)S(1)}, f32[36,16,128]{2,1,0:T(8,128)S(1)}, u32[]{:S(2)}, u32[]{:S(2)}) collective-permute-start(f32[36,16,128]{2,1,0:T(8,128)S(1)} %get-tuple-element.16.to_sub.state), channel_id=1, source_target_pairs={{0,3},{1,2},{2,1},{3,0},{4,7},{5,6},{6,5},{7,4},{8,11},{9,10},{10,... | collective-permute-start | bytes 884744 | tf_op jit(solution)/shard_map/ppermute | solution.py:591
  25.0 22.0 %collective-permute-start.5 = (f32[36,16,128]{2,1,0:T(8,128)S(1)}, f32[36,16,128]{2,1,0:T(8,128)S(1)}, u32[]{:S(2)}, u32[]{:S(2)}) collective-permute-start(f32[36,16,128]{2,1,0:T(8,128)S(1)} %get-tuple-element.16.to_sub.state), channel_id=1, source_target_pairs={{0,2},{1,3},{2,0},{3,1},{4,6},{5,7},{6,4},{7,5},{8,10},{9,11},{10,... | collective-permute-start | bytes 884744 | tf_op jit(solution)/shard_map/ppermute | solution.py:591
  29.6 17.3 %collective-permute-start.4 = (f32[36,16,128]{2,1,0:T(8,128)S(1)}, f32[36,16,128]{2,1,0:T(8,128)S(1)}, u32[]{:S(2)}, u32[]{:S(2)}) collective-permute-start(f32[36,16,128]{2,1,0:T(8,128)S(1)} %get-tuple-element.16.to_sub.state), channel_id=1, source_target_pairs={{0,1},{1,0},{2,3},{3,2},{4,5},{5,4},{6,7},{7,6},{8,9},{9,8},{10,11... | collective-permute-start | bytes 884744 | tf_op jit(solution)/shard_map/ppermute | solution.py:591

commit v4 on v3

--- a/solution.py
+++ b/solution.py
@@ -462,7 +462,11 @@
 
 
 def sub_kernel(before, tiles, state, extra, *rest):
-    messages = rest[: -11 - GROUP]
+    sub = lax.axis_index("sub")
+    part = state.shape[0]
+    messages = [
+        rest[0].at[pl.ds(lax.bitwise_xor(sub, number + 1) * part, part)] for number in range(3)
+    ]
     force, torque, kicked, totals, sums, spread, picked, codes, heard, todo, sem = rest[
         -11 - GROUP : -GROUP
     ]
@@ -473,7 +477,6 @@
     fill_spread(spread)
     sums[...] = jnp.zeros_like(sums)
     copy.wait()
-    sub = lax.axis_index("sub")
     ours = blocks + (2 + sub) * size
     places = [
         (blocks + (2 + lax.bitwise_xor(sub, number + 1)) * size, ours, blocks)
@@ -587,9 +590,7 @@
     )(state, low, high)
     from_a = lax.ppermute(to_a, "slab", inside)
     from_b = lax.ppermute(to_b, "slab", across)
-    from_sub = [
-        lax.ppermute(to_sub, "sub", [(i, i ^ d) for i in range(subs)]) for d in range(1, subs)
-    ]
+    from_sub = [lax.all_gather(to_sub, "sub", axis=0, tiled=True)]
 
     def work(messages):
         room = choices * blocks * (1 + messages) + GROUP
@@ -619,7 +620,7 @@
             out_shape=(shape(3, per_dev), shape(3, per_dev), shape(6, per_dev)),
             in_specs=[VMEM] * (4 + len(from_sub)),
             out_specs=(VMEM,) * 3,
-            scratch_shapes=[pltpu.VMEM((tiles * 8, LANES), f32)] + work(len(from_sub)),
+            scratch_shapes=[pltpu.VMEM((tiles * 8, LANES), f32)] + work(subs - 1),
             compiler_params=PARAMS,
             name="sub_pairs",
         )(totals, table, to_sub, state, *from_sub)

time: 56.7 us -> 75.5 us (1.33)
  the two profiles are of different devices: /device:TPU:324 before, /device:TPU:152 now
where the time goes in v4:
time: 75.5 us; the launch traced here: 75.1 us
  Pallas kernels  31.5 us (42%)
  waiting for transfers between devices  17.3 us (23%)
  between operations  14.1 us (19%)
  starting transfers between devices  9.95 us (13%)
  local copies, waits for them, and re-layouts  2.23 us (3%)
    pallas_call x1, Pallas kernels, body(): pl.pallas_call(slab_kernel, out_shape=(shape(tiles * 8, LANES), shape(til...  14.2 us
    pallas_call x1, Pallas kernels, body(): pl.pallas_call(sub_kernel, out_shape=(shape(3, per_dev), shape(3, per_dev...  12.6 us
    all_gather x1, waiting for transfers between devices, body(): from_sub = [lax.all_gather(to_sub, 'sub', axis=0, tiled=True)]  8.23 us
    ppermute x1, waiting for transfers between devices, body(): from_b = lax.ppermute(to_b, 'slab', across)  6.1 us
    ppermute x1, starting transfers between devices, body(): from_a = lax.ppermute(to_a, 'slab', inside)  3.62 us
    ppermute x1, waiting for transfers between devices, body(): high = lax.ppermute(swap_b, 'slab', across)  2.97 us
    pallas_call x1, Pallas kernels, body(): pl.pallas_call(pack_kernel, out_shape=(shape(blocks + 1, ROWS, LANES), sh...  2.56 us
    ppermute x1, starting transfers between devices, body(): high = lax.ppermute(swap_b, 'slab', across)  2.46 us
  transfers between devices with their start and end apart: 5, of which 3 were waited for; matrix products, arithmetic and copies ran while one was open for 0% of the time, Pallas kernels for 19%

profile of v4, /device:TPU:152, one launch (start us, length us, event | category | flops | bytes accessed | tf_op | source)
XLA Modules:
  0.0 75.1 jit_solution(3144739259053626131)
XLA Ops:
  7.2 0.0 all-gather.2.cloned.1.call-start
  7.2 2.6 %pack.1 = (f32[33,16,128]{2,1,0:T(8,128)}, f32[4,16,128]{2,1,0:T(8,128)}, f32[4,16,128]{2,1,0:T(8,128)}) custom-call(s32[32]{0:T(128)} %refs_0_.1, f32[3,4096]{1,0:T(4,128)} %refs_1_.1, f32[6,4096]{1,0:T(8,128)} %refs_2_.1, f32[32,128]{1,0:T(8,128)} %bitcast.3, f32[32,128]{1,0:T(8,128)} %bitcast.4, s32[3,512]{1,0:T(4,128)} %refs_5_.1, s32[2,32]{1,0:T(2,128)} %refs_6_.1, ...), custom_call_target="tpu_custom_call" | custom-call | tf_op jit(solution)/shard_map/pack/pallas_call | solution.py:548
  9.8 1.9 %collective-permute-start = (f32[4,16,128]{2,1,0:T(8,128)}, f32[4,16,128]{2,1,0:T(8,128)S(1)}, u32[]{:S(2)}, u32[]{:S(2)}) collective-permute-start(f32[4,16,128]{2,1,0:T(8,128)} %get-tuple-element.12), channel_id=1, source_target_pairs={{0,4},{4,0},{8,12},{12,8},{16,20},{20,16},{24,28},{28,24},{32,36},... | collective-permute-start | bytes 98312 | tf_op jit(solution)/shard_map/ppermute | solution.py:581
  11.7 2.5 %collective-permute-start.1 = (f32[4,16,128]{2,1,0:T(8,128)}, f32[4,16,128]{2,1,0:T(8,128)S(1)}, u32[]{:S(2)}, u32[]{:S(2)}) collective-permute-start(f32[4,16,128]{2,1,0:T(8,128)} %get-tuple-element.13), channel_id=1, source_target_pairs={{4,8},{8,4},{12,16},{16,12},{20,24},{24,20},{28,32},{32,28},{36,40... | collective-permute-start | bytes 98312 | tf_op jit(solution)/shard_map/ppermute | solution.py:582
  14.2 0.0 collective-permute-done.low
  14.2 3.0 %collective-permute-done.1.high = f32[4,16,128]{2,1,0:T(8,128)S(1)} collective-permute-done((f32[4,16,128]{2,1,0:T(8,128)}, f32[4,16,128]{2,1,0:T(8,128)S(1)}, u32[]{:S(2)}, u32[]{:S(2)}) %collective-permute-start.1) | collective-permute-done | bytes 32800 | tf_op jit(solution)/shard_map/ppermute | solution.py:582
  17.2 0.0 copy-start.1
  17.2 1.0 %copy-done.1 = f32[33,16,128]{2,1,0:T(8,128)S(1)} copy-done((f32[33,16,128]{2,1,0:T(8,128)S(1)}, f32[33,16,128]{2,1,0:T(8,128)}, u32[]{:S(2)}) %copy-start.1) | copy-done | bytes 270360
  18.1 0.0 copy-start.2
  18.1 2.2 %place.1 = (f32[36,16,128]{2,1,0:T(8,128)S(1)}, f32[36,16,128]{2,1,0:T(8,128)S(1)}, f32[36,16,128]{2,1,0:T(8,128)}) custom-call(f32[33,16,128]{2,1,0:T(8,128)S(1)} %copy-done.1, f32[4,16,128]{2,1,0:T(8,128)S(1)} %collective-permute-done.low, f32[4,16,128]{2,1,0:T(8,128)S(1)} %collective-permute-done.1.high), custom_call_target="tpu_custom_call" | custom-call | tf_op jit(solution)/shard_map/place/pallas_call | solution.py:583
  20.3 0.0 all-gather.2.cloned.1.call-update
  20.3 3.6 %collective-permute-start.2 = (f32[36,16,128]{2,1,0:T(8,128)S(1)}, f32[36,16,128]{2,1,0:T(8,128)S(1)}, u32[]{:S(2)}, u32[]{:S(2)}) collective-permute-start(f32[36,16,128]{2,1,0:T(8,128)S(1)} %get-tuple-element.14.to_a), channel_id=1, source_target_pairs={{0,4},{4,0},{8,12},{12,8},{16,20},{20,16},{24,28},{28,24},{32,36},... | collective-permute-start | bytes 884744 | tf_op jit(solution)/shard_map/ppermute | solution.py:591
  23.9 1.9 %collective-permute-start.3 = (f32[36,16,128]{2,1,0:T(8,128)S(1)}, f32[36,16,128]{2,1,0:T(8,128)S(1)}, u32[]{:S(2)}, u32[]{:S(2)}) collective-permute-start(f32[36,16,128]{2,1,0:T(8,128)S(1)} %get-tuple-element.15.to_b), channel_id=1, source_target_pairs={{4,8},{8,4},{12,16},{16,12},{20,24},{24,20},{28,32},{32,28},{36,40... | collective-permute-start | bytes 884744 | tf_op jit(solution)/shard_map/ppermute | solution.py:592
  25.9 0.0 collective-permute-done.2.from_a
  25.9 6.1 %collective-permute-done.3.from_b = f32[36,16,128]{2,1,0:T(8,128)S(1)} collective-permute-done((f32[36,16,128]{2,1,0:T(8,128)S(1)}, f32[36,16,128]{2,1,0:T(8,128)S(1)}, u32[]{:S(2)}, u32[]{:S(2)}) %collective-permute-start.3) | collective-permute-done | bytes 294944 | tf_op jit(solution)/shard_map/ppermute | solution.py:592
  32.0 14.2 %slab_pairs.1 = (f32[384,128]{1,0:T(8,128)S(1)}, f32[48,48,128]{2,1,0:T(8,128)S(1)}) custom-call(f32[36,16,128]{2,1,0:T(8,128)S(1)} %get-tuple-element.14.to_a, f32[36,16,128]{2,1,0:T(8,128)S(1)} %get-tuple-element.15.to_b, f32[36,16,128]{2,1,0:T(8,128)} %get-tuple-element.16.to_sub.state, f32[36,16,128]{2,1,0:T(8,128)S(1)} %collective-permute-done.2.from_a, ...), custom_call_target="tpu_custom_call" | custom-call | flops 90000000 | bytes 400000 | tf_op jit(solution)/shard_map/slab_pairs/pallas_call | solution.py:607
  46.2 8.2 %all-gather.2.cloned.1.call-done.rest_0_ = f32[144,16,128]{2,1,0:T(8,128)} async-done(((f32[36,16,128]{2,1,0:T(8,128)}), f32[144,16,128]{2,1,0:T(8,128)}) %all-gather.2.cloned.1.call-update) | async-done | bytes 1179664 | tf_op jit(solution)/shard_map/all_gather | solution.py:593
  54.4 0.0 copy-done.2
  54.4 0.0 copy-start
  54.4 1.3 %copy-done = f32[144,16,128]{2,1,0:T(8,128)S(1)} copy-done((f32[144,16,128]{2,1,0:T(8,128)S(1)}, f32[144,16,128]{2,1,0:T(8,128)}, u32[]{:S(2)}) %copy-start) | copy-done | bytes 1179672
  55.7 12.6 %sub_pairs.1 = (f32[3,4096]{1,0:T(4,128)}, f32[3,4096]{1,0:T(4,128)}, f32[6,4096]{1,0:T(8,128)}) custom-call(f32[384,128]{1,0:T(8,128)S(1)} %get-tuple-element.17.before, f32[48,48,128]{2,1,0:T(8,128)S(1)} %get-tuple-element.18.tiles, f32[36,16,128]{2,1,0:T(8,128)} %get-tuple-element.16.to_sub.state, f32[33,16,128]{2,1,0:T(8,128)S(1)} %copy-done.2, ...), custom_call_target="tpu_custom_call" | custom-call | tf_op jit(solution)/shard_map/sub_pairs/pallas_call | solution.py:618
Async XLA Ops:
  7.2 47.3 %all-gather.2.cloned.1.call-start = ((), (), s32[]{:S(2)}) async-start(), calls=%async_computation | async-start | bytes 1474560 | tf_op jit(solution)/shard_map/all_gather | solution.py:593
  9.8 4.4 %collective-permute-start = (f32[4,16,128]{2,1,0:T(8,128)}, f32[4,16,128]{2,1,0:T(8,128)S(1)}, u32[]{:S(2)}, u32[]{:S(2)}) collective-permute-start(f32[4,16,128]{2,1,0:T(8,128)} %get-tuple-element.12), channel_id=1, source_target_pairs={{0,4},{4,0},{8,12},{12,8},{16,20},{20,16},{24,28},{28,24},{32,36},... | collective-permute-start | bytes 98312 | tf_op jit(solution)/shard_map/ppermute | solution.py:581
  11.7 5.4 %collective-permute-start.1 = (f32[4,16,128]{2,1,0:T(8,128)}, f32[4,16,128]{2,1,0:T(8,128)S(1)}, u32[]{:S(2)}, u32[]{:S(2)}) collective-permute-start(f32[4,16,128]{2,1,0:T(8,128)} %get-tuple-element.13), channel_id=1, source_target_pairs={{4,8},{8,4},{12,16},{16,12},{20,24},{24,20},{28,32},{32,28},{36,40... | collective-permute-start | bytes 98312 | tf_op jit(solution)/shard_map/ppermute | solution.py:582
  17.2 1.0 %copy-start.1 = (f32[33,16,128]{2,1,0:T(8,128)S(1)}, f32[33,16,128]{2,1,0:T(8,128)}, u32[]{:S(2)}) copy-start(f32[33,16,128]{2,1,0:T(8,128)} %get-tuple-element.11.state.extra) | copy-start | bytes 811012
  18.1 36.3 %copy-start.2 = (f32[33,16,128]{2,1,0:T(8,128)S(1)}, f32[33,16,128]{2,1,0:T(8,128)}, u32[]{:S(2)}) copy-start(f32[33,16,128]{2,1,0:T(8,128)} %get-tuple-element.11.state.extra) | copy-start | bytes 811012
  20.3 5.6 %collective-permute-start.2 = (f32[36,16,128]{2,1,0:T(8,128)S(1)}, f32[36,16,128]{2,1,0:T(8,128)S(1)}, u32[]{:S(2)}, u32[]{:S(2)}) collective-permute-start(f32[36,16,128]{2,1,0:T(8,128)S(1)} %get-tuple-element.14.to_a), channel_id=1, source_target_pairs={{0,4},{4,0},{8,12},{12,8},{16,20},{20,16},{24,28},{28,24},{32,36},... | collective-permute-start | bytes 884744 | tf_op jit(solution)/shard_map/ppermute | solution.py:591
  23.9 8.0 %collective-permute-start.3 = (f32[36,16,128]{2,1,0:T(8,128)S(1)}, f32[36,16,128]{2,1,0:T(8,128)S(1)}, u32[]{:S(2)}, u32[]{:S(2)}) collective-permute-start(f32[36,16,128]{2,1,0:T(8,128)S(1)} %get-tuple-element.15.to_b), channel_id=1, source_target_pairs={{4,8},{8,4},{12,16},{16,12},{20,24},{24,20},{28,32},{32,28},{36,40... | collective-permute-start | bytes 884744 | tf_op jit(solution)/shard_map/ppermute | solution.py:592
  54.4 1.3 %copy-start = (f32[144,16,128]{2,1,0:T(8,128)S(1)}, f32[144,16,128]{2,1,0:T(8,128)}, u32[]{:S(2)}) copy-start(f32[144,16,128]{2,1,0:T(8,128)} %all-gather.2.cloned.1.call-done.rest_0_) | copy-start | bytes 3538948
Sparse Core Ops, SparseCore 0:
  20.4 33.9 all-gather.1

commit v5 on v3

--- a/solution.py
+++ b/solution.py
@@ -54,11 +54,11 @@
 
 
 def pack_kernel(*refs):
-    sources, (state, swap_a, swap_b), (moving, sems) = refs[:8], refs[8:11], refs[-2:]
-    goal, place, speed, size, wet, rows, partners, live = refs[11:-2]
+    sources, (state, swap_a, swap_b), (moving, sems) = refs[:9], refs[9:12], refs[-2:]
+    goal, place, speed, size, wet, rows, partners, live, goals = refs[12:-2]
     copies = [
         pltpu.make_async_copy(source, target, sems.at[index])
-        for index, (source, target) in enumerate(zip(sources, refs[11:-2]))
+        for index, (source, target) in enumerate(zip(sources, refs[12:-2]))
     ]
     for copy in copies:
         copy.start()
@@ -108,6 +108,10 @@
         state[blocks, 12 + which : 13 + which, 0:blocks] = jnp.where(
             live[...] > which, partners[which : which + 1, :], -1
         ).astype(f32)
+    slots = lax.broadcasted_iota(jnp.int32, (LANES, blocks), 0)
+    filled = jnp.where((goals[...] - here * blocks == slots) & (slots < blocks), 1.0, 0.0)
+    counts = dot_nt(jnp.ones((8, blocks), bf16), filled.astype(bf16))
+    state[blocks, 14:15, :] = counts[0:1, :]
 
 
 def ghost_index(extra, which, tile, tiles, odd):
@@ -116,7 +120,7 @@
     return row.astype(jnp.int32)
 
 
-def place_kernel(state, low, high, to_a, to_b, to_sub):
+def place_kernel(state, low, high, _, to_a, to_b, to_sub):
     here = lax.axis_index("slab")
     odd, _, _ = partners_of(here)
     blocks = state.shape[0] - 1
@@ -146,7 +150,7 @@
             for block in range(blocks):
                 total = jnp.where(source == block, picked[block * ROWS : (block + 1) * ROWS], total)
             message[blocks + tile] = total
-        message[blocks, 11:13, :] = extra[12:14, :]
+        message[blocks, 11:14, :] = extra[12:15, :]
 
 
 def cross(first, second):
@@ -158,8 +162,7 @@
 
 
 def recip(value):
-    guess = pl.reciprocal(value, approx=True)
-    return guess * (2.0 - value * guess)
+    return pl.reciprocal(value, approx=True)
 
 
 def dot_rows(first, second):
@@ -346,25 +349,22 @@
     lax.fori_loop(0, (count + GROUP - 1) // GROUP, some_pairs, 0)
 
 
-def list_far(count, message, heard, number, theirs, ours, ghost, blocks, picked, todo):
+def within(shift, size):
+    return shift.astype(jnp.uint32) < jnp.uint32(size)
+
+
+def list_far(count, message, heard, number, theirs, ours, ghost, blocks, todo):
     size = message.shape[0] - blocks
-    start = count
     for tile in range(blocks):
         for which in range(CHOICES):
             shift = heard[which, tile] - theirs
-            wanted = (shift >= 0) & (shift < size)
+            wanted = within(shift, size)
             todo[count] = tile * 64 + blocks + shift
             count = count + wanted.astype(jnp.int32)
             shift = heard[(number + 1) * CHOICES + which, tile] - ours
-            wanted = (shift >= 0) & (shift < size)
+            wanted = within(shift, size)
             todo[count] = (ghost + shift) * 64 + tile
             count = count + wanted.astype(jnp.int32)
-
-    def pick(index, carry):
-        picked[index] = scale(message[todo[index] % 64])
-        return carry
-
-    lax.fori_loop(start, count, pick, 0)
     return count
 
 
@@ -378,12 +378,26 @@
     return copy
 
 
-def far_pairs(messages, places, tiles, sums, spread, picked, heard, todo, coefs):
-    spare = tiles.shape[0] - 1
+def list_all(messages, places, heard, todo):
     blocks = messages[0].shape[0] - GHOST_TILES
     count = jnp.int32(0)
+    ends = [count]
     for number, (message, (theirs, ours, ghost)) in enumerate(zip(messages, places)):
-        count = list_far(count, message, heard, number, theirs, ours, ghost, blocks, picked, todo)
+        count = list_far(count, message, heard, number, theirs, ours, ghost, blocks, todo)
+        ends.append(count)
+    return ends
+
+
+def far_pairs(messages, ends, tiles, sums, spread, picked, todo, coefs):
+    spare = tiles.shape[0] - 1
+    count = ends[-1]
+    for number, message in enumerate(messages):
+
+        def pick(index, carry, message=message):
+            picked[index] = scale(message[todo[index] % 64])
+            return carry
+
+        lax.fori_loop(ends[number], ends[number + 1], pick, 0)
     for extra in range(GROUP):
         todo[count + extra] = spare * 64
         picked[count + extra] = tiles[spare, 0:ROWS]
@@ -401,12 +415,23 @@
     run_pairs(count, todo, coefs, load, scalars, add)
 
 
-def slab_kernel(to_a, to_b, to_sub, from_a, from_b, totals, tiles, feats, sums, spread, *rest):
-    picked, codes, heard, todo, sem = rest[:5]
-    coefs = rest[5:]
+def early_kernel(state, table, feats):
+    for slot in range(table.shape[0]):
+        rows = scale(state[slot])
+        table[slot, 0:ROWS] = rows
+        table[slot, ROWS:] = mirror(rows)
+        feats[slot] = features(rows)
+
+
+def slab_kernel(
+    to_a, to_b, to_sub, from_a, from_b, table, early_feats, totals, tiles, feats, far_todo, new, sums, *rest
+):
+    spread, picked, codes, heard, todo, sem = rest[:6]
+    coefs = rest[6:]
     own_tiles = to_sub.shape[0]
     size = GHOST_TILES
     blocks = own_tiles - size
+    codes[7:8, :] = to_sub[blocks, 13:14, :].astype(jnp.int32)
     copy = hear([to_sub, from_a, from_b], blocks, codes, heard, sem)
     spare = tiles.shape[0] - 1
 
@@ -417,25 +442,43 @@
         return rows
 
     fill_spread(spread)
+    copy.wait()
+    shared = blocks + (2 + lax.axis_index("sub")) * size
+    count = jnp.int32(0)
+    for tile in range(blocks):
+        for which in range(CHOICES):
+            partner = heard[which, tile]
+            mine = within(partner - shared, size)
+            wanted = within(partner, blocks) | mine
+            slot = jnp.where(mine, partner - shared + blocks, partner)
+            todo[count] = tile * 64 + slot
+            count = count + wanted.astype(jnp.int32)
+    odd, _, _ = partners_of(lax.axis_index("slab"))
+    low, high = blocks + odd * size, blocks + (1 - odd) * size
+    places = [(high, low, own_tiles), (low, high, own_tiles + size)]
+    ends = list_all([from_a, from_b], places, heard, far_todo)
+    news = jnp.int32(0)
+    for slot in range(blocks):
+        new[news] = slot
+        news = news + (heard[7, slot] == 0).astype(jnp.int32)
     sums[...] = jnp.zeros_like(sums)
-    for tile in range(own_tiles):
+    for slot in range(blocks):
+        tiles[slot] = table[slot]
+        feats[slot] = early_feats[slot]
+    for tile in range(blocks, own_tiles):
         feats[tile] = features(enter(tile, to_sub[tile]))
     for tile in range(size):
         enter(own_tiles + tile, to_a[blocks + tile])
         enter(own_tiles + size + tile, to_b[blocks + tile])
     for tile in range(own_tiles + 2 * size, spare + 1):
         feats[spare] = features(enter(tile, jnp.ones((ROWS, LANES), f32)))
-    copy.wait()
-    shared = blocks + (2 + lax.axis_index("sub")) * size
-    count = jnp.int32(0)
-    for tile in range(blocks):
-        for which in range(CHOICES):
-            partner = heard[which, tile]
-            mine = (partner >= shared) & (partner < shared + size)
-            wanted = ((partner >= 0) & (partner < blocks)) | mine
-            slot = jnp.where(mine, partner - shared + blocks, partner)
-            todo[count] = tile * 64 + slot
-            count = count + wanted.astype(jnp.int32)
+
+    def enter_new(index, carry):
+        slot = new[index]
+        feats[slot] = features(enter(slot, to_sub[slot]))
+        return carry
+
+    lax.fori_loop(0, news, enter_new, 0)
     for extra in range(GROUP):
         todo[count + extra] = spare * 64 + spare
 
@@ -452,10 +495,7 @@
         add_back(second, feats[first], sums, coef)
 
     run_pairs(count, todo, coefs, load, scalars, add)
-    odd, _, _ = partners_of(lax.axis_index("slab"))
-    low, high = blocks + odd * size, blocks + (1 - odd) * size
-    places = [(high, low, own_tiles), (low, high, own_tiles + size)]
-    far_pairs([from_a, from_b], places, tiles, sums, spread, picked, heard, todo, coefs)
+    far_pairs([from_a, from_b], ends, tiles, sums, spread, picked, far_todo, coefs)
     for group in range(tiles.shape[0] // 8):
         for row, value in enumerate(finish(group, sums, tiles)):
             totals[pl.ds(group * 64 + row, 8, stride=8), :] = value
@@ -471,15 +511,16 @@
     blocks = state.shape[0] - size
     copy = hear([state, *messages], blocks, codes, heard, sem)
     fill_spread(spread)
+    copy.wait()
     sums[...] = jnp.zeros_like(sums)
-    copy.wait()
     sub = lax.axis_index("sub")
     ours = blocks + (2 + sub) * size
     places = [
         (blocks + (2 + lax.bitwise_xor(sub, number + 1)) * size, ours, blocks)
         for number in range(len(messages))
     ]
-    far_pairs(messages, places, tiles, sums, spread, picked, heard, todo, coefs)
+    ends = list_all(messages, places, heard, todo)
+    far_pairs(messages, ends, tiles, sums, spread, picked, todo, coefs)
     for group in range(tiles.shape[0] // 8):
         for row, value in enumerate(finish(group, sums, tiles)):
             part = pl.ds(group * 64 + row, 8, stride=8)
@@ -549,7 +590,7 @@
             shape(CAP, ROWS, LANES),
             shape(CAP, ROWS, LANES),
         ),
-        in_specs=[HBM] * 8,
+        in_specs=[HBM] * 9,
         out_specs=(VMEM,) * 3,
         scratch_shapes=[
             pltpu.SMEM((blocks,), jnp.int32),
@@ -560,8 +601,9 @@
             pltpu.VMEM(ghost_rows.shape, jnp.int32),
             pltpu.VMEM(partner_tiles.shape, jnp.int32),
             pltpu.VMEM((1, blocks), jnp.int32),
+            pltpu.VMEM((1, blocks), jnp.int32),
             pltpu.VMEM((blocks, ROWS, LANES), f32),
-            pltpu.SemaphoreType.DMA((8,)),
+            pltpu.SemaphoreType.DMA((9,)),
         ],
         compiler_params=pltpu.CompilerParams(vmem_limit_bytes=60 * 1024 * 1024),
         name="pack",
@@ -574,17 +616,30 @@
         ghost_rows,
         partner_tiles,
         live_pairs.reshape(1, blocks),
+        new_owner.reshape(1, blocks),
     )
     low = lax.ppermute(swap_a, "slab", inside)
     high = lax.ppermute(swap_b, "slab", across)
+    early = pl.pallas_call(
+        early_kernel,
+        out_shape=(
+            shape(blocks, 3 * ROWS, LANES),
+            shape(blocks, 3 * FEATS, LANES, dtype=bf16),
+        ),
+        in_specs=[VMEM],
+        out_specs=(VMEM, VMEM),
+        compiler_params=PARAMS,
+        cost_estimate=pl.CostEstimate(flops=4000000, bytes_accessed=1000000, transcendentals=0),
+        name="early",
+    )(state)
     to_a, to_b, to_sub = pl.pallas_call(
         place_kernel,
         out_shape=(shape(blocks + size, ROWS, LANES),) * 3,
-        in_specs=[VMEM] * 3,
+        in_specs=[VMEM] * 3 + [pl.BlockSpec(memory_space=pl.ANY)],
         out_specs=(VMEM,) * 3,
         compiler_params=PARAMS,
         name="place",
-    )(state, low, high)
+    )(state, low, high, early[0])
     from_a = lax.ppermute(to_a, "slab", inside)
     from_b = lax.ppermute(to_b, "slab", across)
     from_sub = [
@@ -606,13 +661,18 @@
     totals, table = pl.pallas_call(
         slab_kernel,
         out_shape=(shape(tiles * 8, LANES), shape(tiles, 3 * ROWS, LANES)),
-        in_specs=[VMEM] * 5,
+        in_specs=[VMEM] * 7,
         out_specs=(VMEM, VMEM),
-        scratch_shapes=[pltpu.VMEM((tiles, 3 * FEATS, LANES), bf16)] + work(2),
+        scratch_shapes=[
+            pltpu.VMEM((tiles, 3 * FEATS, LANES), bf16),
+            pltpu.SMEM((3 * choices * blocks + GROUP,), jnp.int32),
+            pltpu.SMEM((blocks + 1,), jnp.int32),
+        ]
+        + work(2),
         compiler_params=PARAMS,
         cost_estimate=pl.CostEstimate(flops=90000000, bytes_accessed=400000, transcendentals=0),
         name="slab_pairs",
-    )(to_a, to_b, to_sub, from_a, from_b)
+    )(to_a, to_b, to_sub, from_a, from_b, *early)
     return tuple(
         pl.pallas_call(
             sub_kernel,

time: 56.7 us -> 54.2 us (0.956)
  the two profiles are of different devices: /device:TPU:324 before, /device:TPU:202 now
where the time goes in v5:
time: 54.2 us; the launch traced here: 53.9 us
  Pallas kernels  30 us (55%)
  starting transfers between devices  20.7 us (38%)
  waiting for transfers between devices  1.53 us (3%)
  local copies, waits for them, and re-layouts  0.95 us (2%)
  between operations  0.77 us (1%)
    pallas_call x1, Pallas kernels, body(): pl.pallas_call(slab_kernel, out_shape=(shape(tiles * 8, LANES), shape(til...  18.7 us
    ppermute x3, starting transfers between devices, body(): lax.ppermute(to_sub, 'sub', [(i, i ^ d) for i in range(subs)])  9.82 us
    pallas_call x1, Pallas kernels, body(): pl.pallas_call(sub_kernel, out_shape=(shape(3, per_dev), shape(3, per_dev...  6.66 us
    ppermute x1, starting transfers between devices, body(): from_b = lax.ppermute(to_b, 'slab', across)  4.08 us
    pallas_call x1, Pallas kernels, body(): pl.pallas_call(pack_kernel, out_shape=(shape(blocks + 1, ROWS, LANES), sh...  2.69 us
    ppermute x1, starting transfers between devices, body(): high = lax.ppermute(swap_b, 'slab', across)  2.46 us
    ppermute x1, starting transfers between devices, body(): from_a = lax.ppermute(to_a, 'slab', inside)  2.41 us
    ppermute x1, starting transfers between devices, body(): low = lax.ppermute(swap_a, 'slab', inside)  1.92 us
  transfers between devices with their start and end apart: 7, of which 1 were waited for; matrix products, arithmetic and copies ran while one was open for 0% of the time, Pallas kernels for 36%

profile of v5, /device:TPU:202, one launch (start us, length us, event | category | flops | bytes accessed | tf_op | source)
XLA Modules:
  0.0 53.9 jit_solution(7381281564775279616)
XLA Ops:
  0.6 2.7 %pack.1 = (f32[33,16,128]{2,1,0:T(8,128)}, f32[4,16,128]{2,1,0:T(8,128)}, f32[4,16,128]{2,1,0:T(8,128)}) custom-call(s32[32]{0:T(128)} %refs_0_.1, f32[3,4096]{1,0:T(4,128)} %refs_1_.1, f32[6,4096]{1,0:T(8,128)} %refs_2_.1, f32[32,128]{1,0:T(8,128)} %bitcast.4, f32[32,128]{1,0:T(8,128)} %bitcast.5, s32[3,512]{1,0:T(4,128)} %refs_5_.1, s32[2,32]{1,0:T(2,128)} %refs_6_.1, ...), custom_call_target="tpu_custom_call" | custom-call | tf_op jit(solution)/shard_map/pack/pallas_call | solution.py:586
  3.3 1.9 %collective-permute-start = (f32[4,16,128]{2,1,0:T(8,128)}, f32[4,16,128]{2,1,0:T(8,128)S(1)}, u32[]{:S(2)}, u32[]{:S(2)}) collective-permute-start(f32[4,16,128]{2,1,0:T(8,128)} %get-tuple-element.14), channel_id=1, source_target_pairs={{0,4},{4,0},{8,12},{12,8},{16,20},{20,16},{24,28},{28,24},{32,36},... | collective-permute-start | bytes 98312 | tf_op jit(solution)/shard_map/ppermute | solution.py:621
  5.3 2.5 %collective-permute-start.1 = (f32[4,16,128]{2,1,0:T(8,128)}, f32[4,16,128]{2,1,0:T(8,128)S(1)}, u32[]{:S(2)}, u32[]{:S(2)}) collective-permute-start(f32[4,16,128]{2,1,0:T(8,128)} %get-tuple-element.15), channel_id=1, source_target_pairs={{4,8},{8,4},{12,16},{16,12},{20,24},{24,20},{28,32},{32,28},{36,40... | collective-permute-start | bytes 98312 | tf_op jit(solution)/shard_map/ppermute | solution.py:622
  7.7 0.0 copy-start
  7.7 0.9 %copy-done = f32[33,16,128]{2,1,0:T(8,128)S(1)} copy-done((f32[33,16,128]{2,1,0:T(8,128)S(1)}, f32[33,16,128]{2,1,0:T(8,128)}, u32[]{:S(2)}) %copy-start) | copy-done | bytes 270360
  8.7 0.5 early.1
  9.2 0.0 collective-permute-done.low
  9.2 1.5 %collective-permute-done.1.high = f32[4,16,128]{2,1,0:T(8,128)S(1)} collective-permute-done((f32[4,16,128]{2,1,0:T(8,128)}, f32[4,16,128]{2,1,0:T(8,128)S(1)}, u32[]{:S(2)}, u32[]{:S(2)}) %collective-permute-start.1) | collective-permute-done | bytes 32800 | tf_op jit(solution)/shard_map/ppermute | solution.py:622
  10.7 1.5 %place.1 = (f32[36,16,128]{2,1,0:T(8,128)S(1)}, f32[36,16,128]{2,1,0:T(8,128)S(1)}, f32[36,16,128]{2,1,0:T(8,128)S(1)}) custom-call(f32[33,16,128]{2,1,0:T(8,128)S(1)} %copy-done, f32[4,16,128]{2,1,0:T(8,128)S(1)} %collective-permute-done.low, f32[4,16,128]{2,1,0:T(8,128)S(1)} %collective-permute-done.1.high, f32[32,48,128]{2,1,0:T(8,128)S(1)} %get-tuple-element.16._.table), custom_call_target="tpu_custom_call" | custom-call | tf_op jit(solution)/shard_map/place/pallas_call | solution.py:635
  12.2 2.4 %collective-permute-start.2 = (f32[36,16,128]{2,1,0:T(8,128)S(1)}, f32[36,16,128]{2,1,0:T(8,128)S(1)}, u32[]{:S(2)}, u32[]{:S(2)}) collective-permute-start(f32[36,16,128]{2,1,0:T(8,128)S(1)} %get-tuple-element.17.to_a), channel_id=1, source_target_pairs={{0,4},{4,0},{8,12},{12,8},{16,20},{20,16},{24,28},{28,24},{32,36},... | collective-permute-start | bytes 884744 | tf_op jit(solution)/shard_map/ppermute | solution.py:643
  14.6 4.1 %collective-permute-start.3 = (f32[36,16,128]{2,1,0:T(8,128)S(1)}, f32[36,16,128]{2,1,0:T(8,128)S(1)}, u32[]{:S(2)}, u32[]{:S(2)}) collective-permute-start(f32[36,16,128]{2,1,0:T(8,128)S(1)} %get-tuple-element.18.to_b), channel_id=1, source_target_pairs={{4,8},{8,4},{12,16},{16,12},{20,24},{24,20},{28,32},{32,28},{36,40... | collective-permute-start | bytes 884744 | tf_op jit(solution)/shard_map/ppermute | solution.py:644
  18.7 3.4 %collective-permute-start.6 = (f32[36,16,128]{2,1,0:T(8,128)S(1)}, f32[36,16,128]{2,1,0:T(8,128)S(1)}, u32[]{:S(2)}, u32[]{:S(2)}) collective-permute-start(f32[36,16,128]{2,1,0:T(8,128)S(1)} %get-tuple-element.19.to_sub.state), channel_id=1, source_target_pairs={{0,3},{1,2},{2,1},{3,0},{4,7},{5,6},{6,5},{7,4},{8,11},{9,10},{10,... | collective-permute-start | bytes 884744 | tf_op jit(solution)/shard_map/ppermute | solution.py:646
  22.1 3.0 %collective-permute-start.5 = (f32[36,16,128]{2,1,0:T(8,128)S(1)}, f32[36,16,128]{2,1,0:T(8,128)S(1)}, u32[]{:S(2)}, u32[]{:S(2)}) collective-permute-start(f32[36,16,128]{2,1,0:T(8,128)S(1)} %get-tuple-element.19.to_sub.state), channel_id=1, source_target_pairs={{0,2},{1,3},{2,0},{3,1},{4,6},{5,7},{6,4},{7,5},{8,10},{9,11},{10,... | collective-permute-start | bytes 884744 | tf_op jit(solution)/shard_map/ppermute | solution.py:646
  25.1 3.4 %collective-permute-start.4 = (f32[36,16,128]{2,1,0:T(8,128)S(1)}, f32[36,16,128]{2,1,0:T(8,128)S(1)}, u32[]{:S(2)}, u32[]{:S(2)}) collective-permute-start(f32[36,16,128]{2,1,0:T(8,128)S(1)} %get-tuple-element.19.to_sub.state), channel_id=1, source_target_pairs={{0,1},{1,0},{2,3},{3,2},{4,5},{5,4},{6,7},{7,6},{8,9},{9,8},{10,11... | collective-permute-start | bytes 884744 | tf_op jit(solution)/shard_map/ppermute | solution.py:646
  28.5 0.0 collective-permute-done.2.from_a
  28.5 0.0 collective-permute-done.3.from_b
  28.5 18.7 %slab_pairs.1 = (f32[384,128]{1,0:T(8,128)S(1)}, f32[48,48,128]{2,1,0:T(8,128)S(1)}) custom-call(f32[36,16,128]{2,1,0:T(8,128)S(1)} %get-tuple-element.17.to_a, f32[36,16,128]{2,1,0:T(8,128)S(1)} %get-tuple-element.18.to_b, f32[36,16,128]{2,1,0:T(8,128)S(1)} %get-tuple-element.19.to_sub.state, f32[36,16,128]{2,1,0:T(8,128)S(1)} %collective-permute-done.2.from_a, ...), custom_call_target="tpu_custom_call" | custom-call | flops 90000000 | bytes 400000 | tf_op jit(solution)/shard_map/slab_pairs/pallas_call | solution.py:661
  47.2 0.0 collective-permute-done.6.rest_2_
  47.2 0.0 collective-permute-done.5.rest_1_
  47.2 0.0 collective-permute-done.4.rest_0_
  47.2 6.7 %sub_pairs.1 = (f32[3,4096]{1,0:T(4,128)}, f32[3,4096]{1,0:T(4,128)}, f32[6,4096]{1,0:T(8,128)}) custom-call(f32[384,128]{1,0:T(8,128)S(1)} %get-tuple-element.21.before, f32[48,48,128]{2,1,0:T(8,128)S(1)} %get-tuple-element.22.tiles, f32[36,16,128]{2,1,0:T(8,128)S(1)} %get-tuple-element.19.to_sub.state, f32[33,16,128]{2,1,0:T(8,128)S(1)} %copy-done, ...), custom_call_target="tpu_custom_call" | custom-call | tf_op jit(solution)/shard_map/sub_pairs/pallas_call | solution.py:677
Async XLA Ops:
  3.3 5.9 %collective-permute-start = (f32[4,16,128]{2,1,0:T(8,128)}, f32[4,16,128]{2,1,0:T(8,128)S(1)}, u32[]{:S(2)}, u32[]{:S(2)}) collective-permute-start(f32[4,16,128]{2,1,0:T(8,128)} %get-tuple-element.14), channel_id=1, source_target_pairs={{0,4},{4,0},{8,12},{12,8},{16,20},{20,16},{24,28},{28,24},{32,36},... | collective-permute-start | bytes 98312 | tf_op jit(solution)/shard_map/ppermute | solution.py:621
  5.3 5.4 %collective-permute-start.1 = (f32[4,16,128]{2,1,0:T(8,128)}, f32[4,16,128]{2,1,0:T(8,128)S(1)}, u32[]{:S(2)}, u32[]{:S(2)}) collective-permute-start(f32[4,16,128]{2,1,0:T(8,128)} %get-tuple-element.15), channel_id=1, source_target_pairs={{4,8},{8,4},{12,16},{16,12},{20,24},{24,20},{28,32},{32,28},{36,40... | collective-permute-start | bytes 98312 | tf_op jit(solution)/shard_map/ppermute | solution.py:622
  7.7 1.0 %copy-start = (f32[33,16,128]{2,1,0:T(8,128)S(1)}, f32[33,16,128]{2,1,0:T(8,128)}, u32[]{:S(2)}) copy-start(f32[33,16,128]{2,1,0:T(8,128)} %get-tuple-element.13.state.extra) | copy-start | bytes 811012
  12.2 16.3 %collective-permute-start.2 = (f32[36,16,128]{2,1,0:T(8,128)S(1)}, f32[36,16,128]{2,1,0:T(8,128)S(1)}, u32[]{:S(2)}, u32[]{:S(2)}) collective-permute-start(f32[36,16,128]{2,1,0:T(8,128)S(1)} %get-tuple-element.17.to_a), channel_id=1, source_target_pairs={{0,4},{4,0},{8,12},{12,8},{16,20},{20,16},{24,28},{28,24},{32,36},... | collective-permute-start | bytes 884744 | tf_op jit(solution)/shard_map/ppermute | solution.py:643
  14.6 13.9 %collective-permute-start.3 = (f32[36,16,128]{2,1,0:T(8,128)S(1)}, f32[36,16,128]{2,1,0:T(8,128)S(1)}, u32[]{:S(2)}, u32[]{:S(2)}) collective-permute-start(f32[36,16,128]{2,1,0:T(8,128)S(1)} %get-tuple-element.18.to_b), channel_id=1, source_target_pairs={{4,8},{8,4},{12,16},{16,12},{20,24},{24,20},{28,32},{32,28},{36,40... | collective-permute-start | bytes 884744 | tf_op jit(solution)/shard_map/ppermute | solution.py:644
  18.7 28.5 %collective-permute-start.6 = (f32[36,16,128]{2,1,0:T(8,128)S(1)}, f32[36,16,128]{2,1,0:T(8,128)S(1)}, u32[]{:S(2)}, u32[]{:S(2)}) collective-permute-start(f32[36,16,128]{2,1,0:T(8,128)S(1)} %get-tuple-element.19.to_sub.state), channel_id=1, source_target_pairs={{0,3},{1,2},{2,1},{3,0},{4,7},{5,6},{6,5},{7,4},{8,11},{9,10},{10,... | collective-permute-start | bytes 884744 | tf_op jit(solution)/shard_map/ppermute | solution.py:646
  22.1 25.1 %collective-permute-start.5 = (f32[36,16,128]{2,1,0:T(8,128)S(1)}, f32[36,16,128]{2,1,0:T(8,128)S(1)}, u32[]{:S(2)}, u32[]{:S(2)}) collective-permute-start(f32[36,16,128]{2,1,0:T(8,128)S(1)} %get-tuple-element.19.to_sub.state), channel_id=1, source_target_pairs={{0,2},{1,3},{2,0},{3,1},{4,6},{5,7},{6,4},{7,5},{8,10},{9,11},{10,... | collective-permute-start | bytes 884744 | tf_op jit(solution)/shard_map/ppermute | solution.py:646
  25.1 22.1 %collective-permute-start.4 = (f32[36,16,128]{2,1,0:T(8,128)S(1)}, f32[36,16,128]{2,1,0:T(8,128)S(1)}, u32[]{:S(2)}, u32[]{:S(2)}) collective-permute-start(f32[36,16,128]{2,1,0:T(8,128)S(1)} %get-tuple-element.19.to_sub.state), channel_id=1, source_target_pairs={{0,1},{1,0},{2,3},{3,2},{4,5},{5,4},{6,7},{7,6},{8,9},{9,8},{10,11... | collective-permute-start | bytes 884744 | tf_op jit(solution)/shard_map/ppermute | solution.py:646

commit v6 on v5

--- a/solution.py
+++ b/solution.py
@@ -19,7 +19,7 @@
 FEATS = 16
 MATS = 5
 WIDE_ROWS = (0, 1, 2, 9, 10, 11)
-GROUP = 4
+GROUP = 3
 CHOICES = 2
 GHOST_TILES = 4
 
@@ -219,20 +219,23 @@
         spread[:, block * LANES : (block + 1) * LANES] = jnp.where(hot, 1.0, 0.0).astype(bf16)
 
 
-def pair_scalars(near, far, far_mirror, spread, coefs):
+def pair_columns(near, far_mirror, spread, wide):
     moving = six(far_mirror[0:ROWS], (0, 1, 2, 0, 1, 0))
     turning = six(far_mirror[ROWS:], (0, 1, 2, 0, 1, 0))
-    columns = lax.dot_general(
+    wide[...] = lax.dot_general(
         six(near, (0, 0, 0, 1, 1, 2)),
         jnp.concatenate([spread[...], moving, turning], axis=1),
         (((0,), (0,)), ((), ())),
         preferred_element_type=f32,
     )
+
+
+def pair_scalars(far, wide, coefs):
     far_rows = [far[row : row + 1, :] for row in WIDE_ROWS]
     step = 16
     for start in range(0, LANES, step):
         col = [
-            columns[start : start + step, block * LANES : (block + 1) * LANES] for block in range(8)
+            wide[start : start + step, block * LANES : (block + 1) * LANES] for block in range(8)
         ]
         offset = [far_rows[row] - col[row] for row in range(3)]
         along, twist = col[6], col[7]
@@ -336,17 +339,31 @@
     return force + torque
 
 
-def run_pairs(count, todo, coefs, load, scalars, add):
-    def some_pairs(index, carry):
-        items = [load(index * GROUP + lane) for lane in range(GROUP)]
-        for lane in range(GROUP + 1):
-            if lane < GROUP:
-                scalars(items[lane], coefs[lane])
-            if lane > 0:
-                add(items[lane - 1], coefs[lane - 1])
+def run_pairs(count, buffers, load, columns, scalars, add):
+    wides, coefs = buffers[:GROUP], buffers[GROUP:]
+    groups = jnp.maximum((count + GROUP - 1) // GROUP, 1)
+
+    def items(group):
+        return [load(group * GROUP + lane) for lane in range(GROUP)]
+
+    for item, wide in zip(items(0), wides):
+        columns(item, wide)
+    for item, later, wide, coef in zip(items(0), items(1), wides, coefs):
+        scalars(item, wide, coef)
+        columns(later, wide)
+
+    def step(group, carry):
+        for item, following, later, wide, coef in zip(
+            items(group), items(group + 1), items(group + 2), wides, coefs
+        ):
+            add(item, coef)
+            scalars(following, wide, coef)
+            columns(later, wide)
         return carry
 
-    lax.fori_loop(0, (count + GROUP - 1) // GROUP, some_pairs, 0)
+    lax.fori_loop(0, groups - 1, step, 0)
+    for item, coef in zip(items(groups - 1), coefs):
+        add(item, coef)
 
 
 def within(shift, size):
@@ -388,7 +405,7 @@
     return ends
 
 
-def far_pairs(messages, ends, tiles, sums, spread, picked, todo, coefs):
+def far_pairs(messages, ends, tiles, sums, spread, picked, todo, buffers):
     spare = tiles.shape[0] - 1
     count = ends[-1]
     for number, message in enumerate(messages):
@@ -398,21 +415,23 @@
             return carry
 
         lax.fori_loop(ends[number], ends[number + 1], pick, 0)
-    for extra in range(GROUP):
+    for extra in range(2 * GROUP):
         todo[count + extra] = spare * 64
         picked[count + extra] = tiles[spare, 0:ROWS]
 
     def load(index):
         return todo[index] // 64, picked[index]
 
-    def scalars(item, coef):
-        mine, near = item
-        pair_scalars(near, tiles[mine, 0:ROWS], tiles[mine, ROWS:], spread, coef)
+    def columns(item, wide):
+        pair_columns(item[1], tiles[item[0], ROWS:], spread, wide)
+
+    def scalars(item, wide, coef):
+        pair_scalars(tiles[item[0], 0:ROWS], wide, coef)
 
     def add(item, coef):
         add_back(item[0], features(item[1]), sums, coef)
 
-    run_pairs(count, todo, coefs, load, scalars, add)
+    run_pairs(count, buffers, load, columns, scalars, add)
 
 
 def early_kernel(state, table, feats):
@@ -427,7 +446,7 @@
     to_a, to_b, to_sub, from_a, from_b, table, early_feats, totals, tiles, feats, far_todo, new, sums, *rest
 ):
     spread, picked, codes, heard, todo, sem = rest[:6]
-    coefs = rest[6:]
+    buffers = rest[6:]
     own_tiles = to_sub.shape[0]
     size = GHOST_TILES
     blocks = own_tiles - size
@@ -479,34 +498,36 @@
         return carry
 
     lax.fori_loop(0, news, enter_new, 0)
-    for extra in range(GROUP):
+    for extra in range(2 * GROUP):
         todo[count + extra] = spare * 64 + spare
 
     def load(index):
         return todo[index] // 64, todo[index] % 64
 
-    def scalars(item, coef):
-        first, second = item
-        pair_scalars(tiles[first, 0:ROWS], tiles[second, 0:ROWS], tiles[second, ROWS:], spread, coef)
+    def columns(item, wide):
+        pair_columns(tiles[item[0], 0:ROWS], tiles[item[1], ROWS:], spread, wide)
+
+    def scalars(item, wide, coef):
+        pair_scalars(tiles[item[1], 0:ROWS], wide, coef)
 
     def add(item, coef):
         first, second = item
         add_own(first, feats[second], sums, coef)
         add_back(second, feats[first], sums, coef)
 
-    run_pairs(count, todo, coefs, load, scalars, add)
-    far_pairs([from_a, from_b], ends, tiles, sums, spread, picked, far_todo, coefs)
+    run_pairs(count, buffers, load, columns, scalars, add)
+    far_pairs([from_a, from_b], ends, tiles, sums, spread, picked, far_todo, buffers)
     for group in range(tiles.shape[0] // 8):
         for row, value in enumerate(finish(group, sums, tiles)):
             totals[pl.ds(group * 64 + row, 8, stride=8), :] = value
 
 
 def sub_kernel(before, tiles, state, extra, *rest):
-    messages = rest[: -11 - GROUP]
+    messages = rest[: -11 - 2 * GROUP]
     force, torque, kicked, totals, sums, spread, picked, codes, heard, todo, sem = rest[
-        -11 - GROUP : -GROUP
+        -11 - 2 * GROUP : -2 * GROUP
     ]
-    coefs = rest[-GROUP:]
+    buffers = rest[-2 * GROUP :]
     size = GHOST_TILES
     blocks = state.shape[0] - size
     copy = hear([state, *messages], blocks, codes, heard, sem)
@@ -520,7 +541,7 @@
         for number in range(len(messages))
     ]
     ends = list_all(messages, places, heard, todo)
-    far_pairs(messages, ends, tiles, sums, spread, picked, todo, coefs)
+    far_pairs(messages, ends, tiles, sums, spread, picked, todo, buffers)
     for group in range(tiles.shape[0] // 8):
         for row, value in enumerate(finish(group, sums, tiles)):
             part = pl.ds(group * 64 + row, 8, stride=8)
@@ -646,8 +667,10 @@
         lax.ppermute(to_sub, "sub", [(i, i ^ d) for i in range(subs)]) for d in range(1, subs)
     ]
 
+    wides = [pltpu.VMEM((LANES, (len(WIDE_ROWS) + 2) * LANES), f32)] * GROUP
+
     def work(messages):
-        room = choices * blocks * (1 + messages) + GROUP
+        room = choices * blocks * (1 + messages) + 2 * GROUP
         return [
             pltpu.VMEM((tiles * MATS * FEATS, LANES), f32),
             pltpu.VMEM((6 * ROWS, len(WIDE_ROWS) * LANES), bf16),
@@ -656,7 +679,7 @@
             pltpu.SMEM((8, LANES), jnp.int32),
             pltpu.SMEM((room,), jnp.int32),
             pltpu.SemaphoreType.DMA(()),
-        ] + [pltpu.VMEM((MATS * LANES, 2 * LANES), bf16)] * GROUP
+        ] + wides + [pltpu.VMEM((MATS * LANES, 2 * LANES), bf16)] * GROUP
 
     totals, table = pl.pallas_call(
         slab_kernel,
@@ -665,7 +688,7 @@
         out_specs=(VMEM, VMEM),
         scratch_shapes=[
             pltpu.VMEM((tiles, 3 * FEATS, LANES), bf16),
-            pltpu.SMEM((3 * choices * blocks + GROUP,), jnp.int32),
+            pltpu.SMEM((3 * choices * blocks + 2 * GROUP,), jnp.int32),
             pltpu.SMEM((blocks + 1,), jnp.int32),
         ]
         + work(2),

time: 54.2 us -> 51.3 us (0.946)
  the two profiles are of different devices: /device:TPU:202 before, /device:TPU:66 now
where the time goes in v6:
time: 51.3 us; the launch traced here: 51 us
  Pallas kernels  25 us (49%)
  starting transfers between devices  22.8 us (44%)
  waiting for transfers between devices  1.52 us (3%)
  local copies, waits for them, and re-layouts  0.95 us (2%)
  between operations  0.77 us (2%)
    pallas_call x1, Pallas kernels, body(): pl.pallas_call(slab_kernel, out_shape=(shape(tiles * 8, LANES), shape(til...  11.9 us
    ppermute x3, starting transfers between devices, body(): lax.ppermute(to_sub, 'sub', [(i, i ^ d) for i in range(subs)])  9.82 us
    pallas_call x1, Pallas kernels, body(): pl.pallas_call(sub_kernel, out_shape=(shape(3, per_dev), shape(3, per_dev...  8.42 us
    ppermute x1, starting transfers between devices, body(): from_b = lax.ppermute(to_b, 'slab', across)  4.57 us
    ppermute x1, starting transfers between devices, body(): high = lax.ppermute(swap_b, 'slab', across)  4.57 us
    pallas_call x1, Pallas kernels, body(): pl.pallas_call(pack_kernel, out_shape=(shape(blocks + 1, ROWS, LANES), sh...  2.69 us
    ppermute x1, starting transfers between devices, body(): from_a = lax.ppermute(to_a, 'slab', inside)  1.92 us
    ppermute x1, starting transfers between devices, body(): low = lax.ppermute(swap_a, 'slab', inside)  1.92 us
  transfers between devices with their start and end apart: 7, of which 1 were waited for; matrix products, arithmetic and copies ran while one was open for 0% of the time, Pallas kernels for 24%

profile of v6, /device:TPU:66, one launch (start us, length us, event | category | flops | bytes accessed | tf_op | source)
XLA Modules:
  0.0 51.0 jit_solution(9442343283894003974)
XLA Ops:
  0.6 2.7 %pack.1 = (f32[33,16,128]{2,1,0:T(8,128)}, f32[4,16,128]{2,1,0:T(8,128)}, f32[4,16,128]{2,1,0:T(8,128)}) custom-call(s32[32]{0:T(128)} %refs_0_.1, f32[3,4096]{1,0:T(4,128)} %refs_1_.1, f32[6,4096]{1,0:T(8,128)} %refs_2_.1, f32[32,128]{1,0:T(8,128)} %bitcast.4, f32[32,128]{1,0:T(8,128)} %bitcast.5, s32[3,512]{1,0:T(4,128)} %refs_5_.1, s32[2,32]{1,0:T(2,128)} %refs_6_.1, ...), custom_call_target="tpu_custom_call" | custom-call | tf_op jit(solution)/shard_map/pack/pallas_call | solution.py:607
  3.3 1.9 %collective-permute-start = (f32[4,16,128]{2,1,0:T(8,128)}, f32[4,16,128]{2,1,0:T(8,128)S(1)}, u32[]{:S(2)}, u32[]{:S(2)}) collective-permute-start(f32[4,16,128]{2,1,0:T(8,128)} %get-tuple-element.14), channel_id=1, source_target_pairs={{0,4},{4,0},{8,12},{12,8},{16,20},{20,16},{24,28},{28,24},{32,36},... | collective-permute-start | bytes 98312 | tf_op jit(solution)/shard_map/ppermute | solution.py:642
  5.3 4.6 %collective-permute-start.1 = (f32[4,16,128]{2,1,0:T(8,128)}, f32[4,16,128]{2,1,0:T(8,128)S(1)}, u32[]{:S(2)}, u32[]{:S(2)}) collective-permute-start(f32[4,16,128]{2,1,0:T(8,128)} %get-tuple-element.15), channel_id=1, source_target_pairs={{4,8},{8,4},{12,16},{16,12},{20,24},{24,20},{28,32},{32,28},{36,40... | collective-permute-start | bytes 98312 | tf_op jit(solution)/shard_map/ppermute | solution.py:643
  9.8 0.0 copy-start
  9.8 0.9 %copy-done = f32[33,16,128]{2,1,0:T(8,128)S(1)} copy-done((f32[33,16,128]{2,1,0:T(8,128)S(1)}, f32[33,16,128]{2,1,0:T(8,128)}, u32[]{:S(2)}) %copy-start) | copy-done | bytes 270360
  10.8 0.5 early.1
  11.3 0.0 collective-permute-done.low
  11.3 1.5 %collective-permute-done.1.high = f32[4,16,128]{2,1,0:T(8,128)S(1)} collective-permute-done((f32[4,16,128]{2,1,0:T(8,128)}, f32[4,16,128]{2,1,0:T(8,128)S(1)}, u32[]{:S(2)}, u32[]{:S(2)}) %collective-permute-start.1) | collective-permute-done | bytes 32800 | tf_op jit(solution)/shard_map/ppermute | solution.py:643
  12.8 1.5 %place.1 = (f32[36,16,128]{2,1,0:T(8,128)S(1)}, f32[36,16,128]{2,1,0:T(8,128)S(1)}, f32[36,16,128]{2,1,0:T(8,128)S(1)}) custom-call(f32[33,16,128]{2,1,0:T(8,128)S(1)} %copy-done, f32[4,16,128]{2,1,0:T(8,128)S(1)} %collective-permute-done.low, f32[4,16,128]{2,1,0:T(8,128)S(1)} %collective-permute-done.1.high, f32[32,48,128]{2,1,0:T(8,128)S(1)} %get-tuple-element.16._.table), custom_call_target="tpu_custom_call" | custom-call | tf_op jit(solution)/shard_map/place/pallas_call | solution.py:656
  14.3 1.9 %collective-permute-start.2 = (f32[36,16,128]{2,1,0:T(8,128)S(1)}, f32[36,16,128]{2,1,0:T(8,128)S(1)}, u32[]{:S(2)}, u32[]{:S(2)}) collective-permute-start(f32[36,16,128]{2,1,0:T(8,128)S(1)} %get-tuple-element.17.to_a), channel_id=1, source_target_pairs={{0,4},{4,0},{8,12},{12,8},{16,20},{20,16},{24,28},{28,24},{32,36},... | collective-permute-start | bytes 884744 | tf_op jit(solution)/shard_map/ppermute | solution.py:664
  16.2 4.6 %collective-permute-start.3 = (f32[36,16,128]{2,1,0:T(8,128)S(1)}, f32[36,16,128]{2,1,0:T(8,128)S(1)}, u32[]{:S(2)}, u32[]{:S(2)}) collective-permute-start(f32[36,16,128]{2,1,0:T(8,128)S(1)} %get-tuple-element.18.to_b), channel_id=1, source_target_pairs={{4,8},{8,4},{12,16},{16,12},{20,24},{24,20},{28,32},{32,28},{36,40... | collective-permute-start | bytes 884744 | tf_op jit(solution)/shard_map/ppermute | solution.py:665
  20.8 3.4 %collective-permute-start.6 = (f32[36,16,128]{2,1,0:T(8,128)S(1)}, f32[36,16,128]{2,1,0:T(8,128)S(1)}, u32[]{:S(2)}, u32[]{:S(2)}) collective-permute-start(f32[36,16,128]{2,1,0:T(8,128)S(1)} %get-tuple-element.19.to_sub.state), channel_id=1, source_target_pairs={{0,3},{1,2},{2,1},{3,0},{4,7},{5,6},{6,5},{7,4},{8,11},{9,10},{10,... | collective-permute-start | bytes 884744 | tf_op jit(solution)/shard_map/ppermute | solution.py:667
  24.2 3.0 %collective-permute-start.5 = (f32[36,16,128]{2,1,0:T(8,128)S(1)}, f32[36,16,128]{2,1,0:T(8,128)S(1)}, u32[]{:S(2)}, u32[]{:S(2)}) collective-permute-start(f32[36,16,128]{2,1,0:T(8,128)S(1)} %get-tuple-element.19.to_sub.state), channel_id=1, source_target_pairs={{0,2},{1,3},{2,0},{3,1},{4,6},{5,7},{6,4},{7,5},{8,10},{9,11},{10,... | collective-permute-start | bytes 884744 | tf_op jit(solution)/shard_map/ppermute | solution.py:667
  27.2 3.4 %collective-permute-start.4 = (f32[36,16,128]{2,1,0:T(8,128)S(1)}, f32[36,16,128]{2,1,0:T(8,128)S(1)}, u32[]{:S(2)}, u32[]{:S(2)}) collective-permute-start(f32[36,16,128]{2,1,0:T(8,128)S(1)} %get-tuple-element.19.to_sub.state), channel_id=1, source_target_pairs={{0,1},{1,0},{2,3},{3,2},{4,5},{5,4},{6,7},{7,6},{8,9},{9,8},{10,11... | collective-permute-start | bytes 884744 | tf_op jit(solution)/shard_map/ppermute | solution.py:667
  30.6 0.0 collective-permute-done.2.from_a
  30.6 0.0 collective-permute-done.3.from_b
  30.6 11.9 %slab_pairs.1 = (f32[384,128]{1,0:T(8,128)S(1)}, f32[48,48,128]{2,1,0:T(8,128)S(1)}) custom-call(f32[36,16,128]{2,1,0:T(8,128)S(1)} %get-tuple-element.17.to_a, f32[36,16,128]{2,1,0:T(8,128)S(1)} %get-tuple-element.18.to_b, f32[36,16,128]{2,1,0:T(8,128)S(1)} %get-tuple-element.19.to_sub.state, f32[36,16,128]{2,1,0:T(8,128)S(1)} %collective-permute-done.2.from_a, ...), custom_call_target="tpu_custom_call" | custom-call | flops 90000000 | bytes 400000 | tf_op jit(solution)/shard_map/slab_pairs/pallas_call | solution.py:684
  42.6 0.0 collective-permute-done.6.rest_2_
  42.6 0.0 collective-permute-done.5.rest_1_
  42.6 0.0 collective-permute-done.4.rest_0_
  42.6 8.4 %sub_pairs.1 = (f32[3,4096]{1,0:T(4,128)}, f32[3,4096]{1,0:T(4,128)}, f32[6,4096]{1,0:T(8,128)}) custom-call(f32[384,128]{1,0:T(8,128)S(1)} %get-tuple-element.21.before, f32[48,48,128]{2,1,0:T(8,128)S(1)} %get-tuple-element.22.tiles, f32[36,16,128]{2,1,0:T(8,128)S(1)} %get-tuple-element.19.to_sub.state, f32[33,16,128]{2,1,0:T(8,128)S(1)} %copy-done, ...), custom_call_target="tpu_custom_call" | custom-call | tf_op jit(solution)/shard_map/sub_pairs/pallas_call | solution.py:700
Async XLA Ops:
  3.3 8.0 %collective-permute-start = (f32[4,16,128]{2,1,0:T(8,128)}, f32[4,16,128]{2,1,0:T(8,128)S(1)}, u32[]{:S(2)}, u32[]{:S(2)}) collective-permute-start(f32[4,16,128]{2,1,0:T(8,128)} %get-tuple-element.14), channel_id=1, source_target_pairs={{0,4},{4,0},{8,12},{12,8},{16,20},{20,16},{24,28},{28,24},{32,36},... | collective-permute-start | bytes 98312 | tf_op jit(solution)/shard_map/ppermute | solution.py:642
  5.3 7.6 %collective-permute-start.1 = (f32[4,16,128]{2,1,0:T(8,128)}, f32[4,16,128]{2,1,0:T(8,128)S(1)}, u32[]{:S(2)}, u32[]{:S(2)}) collective-permute-start(f32[4,16,128]{2,1,0:T(8,128)} %get-tuple-element.15), channel_id=1, source_target_pairs={{4,8},{8,4},{12,16},{16,12},{20,24},{24,20},{28,32},{32,28},{36,40... | collective-permute-start | bytes 98312 | tf_op jit(solution)/shard_map/ppermute | solution.py:643
  9.8 1.0 %copy-start = (f32[33,16,128]{2,1,0:T(8,128)S(1)}, f32[33,16,128]{2,1,0:T(8,128)}, u32[]{:S(2)}) copy-start(f32[33,16,128]{2,1,0:T(8,128)} %get-tuple-element.13.state.extra) | copy-start | bytes 811012
  14.3 16.4 %collective-permute-start.2 = (f32[36,16,128]{2,1,0:T(8,128)S(1)}, f32[36,16,128]{2,1,0:T(8,128)S(1)}, u32[]{:S(2)}, u32[]{:S(2)}) collective-permute-start(f32[36,16,128]{2,1,0:T(8,128)S(1)} %get-tuple-element.17.to_a), channel_id=1, source_target_pairs={{0,4},{4,0},{8,12},{12,8},{16,20},{20,16},{24,28},{28,24},{32,36},... | collective-permute-start | bytes 884744 | tf_op jit(solution)/shard_map/ppermute | solution.py:664
  16.2 14.4 %collective-permute-start.3 = (f32[36,16,128]{2,1,0:T(8,128)S(1)}, f32[36,16,128]{2,1,0:T(8,128)S(1)}, u32[]{:S(2)}, u32[]{:S(2)}) collective-permute-start(f32[36,16,128]{2,1,0:T(8,128)S(1)} %get-tuple-element.18.to_b), channel_id=1, source_target_pairs={{4,8},{8,4},{12,16},{16,12},{20,24},{24,20},{28,32},{32,28},{36,40... | collective-permute-start | bytes 884744 | tf_op jit(solution)/shard_map/ppermute | solution.py:665
  20.8 21.8 %collective-permute-start.6 = (f32[36,16,128]{2,1,0:T(8,128)S(1)}, f32[36,16,128]{2,1,0:T(8,128)S(1)}, u32[]{:S(2)}, u32[]{:S(2)}) collective-permute-start(f32[36,16,128]{2,1,0:T(8,128)S(1)} %get-tuple-element.19.to_sub.state), channel_id=1, source_target_pairs={{0,3},{1,2},{2,1},{3,0},{4,7},{5,6},{6,5},{7,4},{8,11},{9,10},{10,... | collective-permute-start | bytes 884744 | tf_op jit(solution)/shard_map/ppermute | solution.py:667
  24.2 18.4 %collective-permute-start.5 = (f32[36,16,128]{2,1,0:T(8,128)S(1)}, f32[36,16,128]{2,1,0:T(8,128)S(1)}, u32[]{:S(2)}, u32[]{:S(2)}) collective-permute-start(f32[36,16,128]{2,1,0:T(8,128)S(1)} %get-tuple-element.19.to_sub.state), channel_id=1, source_target_pairs={{0,2},{1,3},{2,0},{3,1},{4,6},{5,7},{6,4},{7,5},{8,10},{9,11},{10,... | collective-permute-start | bytes 884744 | tf_op jit(solution)/shard_map/ppermute | solution.py:667
  27.2 15.4 %collective-permute-start.4 = (f32[36,16,128]{2,1,0:T(8,128)S(1)}, f32[36,16,128]{2,1,0:T(8,128)S(1)}, u32[]{:S(2)}, u32[]{:S(2)}) collective-permute-start(f32[36,16,128]{2,1,0:T(8,128)S(1)} %get-tuple-element.19.to_sub.state), channel_id=1, source_target_pairs={{0,1},{1,0},{2,3},{3,2},{4,5},{5,4},{6,7},{7,6},{8,9},{9,8},{10,11... | collective-permute-start | bytes 884744 | tf_op jit(solution)/shard_map/ppermute | solution.py:667

commit v7 on v6

--- a/solution.py
+++ b/solution.py
@@ -20,6 +20,7 @@
 MATS = 5
 WIDE_ROWS = (0, 1, 2, 9, 10, 11)
 GROUP = 3
+LEAN = 12
 CHOICES = 2
 GHOST_TILES = 4
 
@@ -54,19 +55,20 @@
 
 
 def pack_kernel(*refs):
-    sources, (state, swap_a, swap_b), (moving, sems) = refs[:9], refs[9:12], refs[-2:]
-    goal, place, speed, size, wet, rows, partners, live, goals = refs[12:-2]
+    sources, (state, swap_a, swap_b) = refs[:9], refs[9:12]
+    moving, leave_a, leave_b, sems = refs[-4:]
+    goal, place, speed, size, wet, rows, partners, live, goals = refs[12:-4]
     copies = [
         pltpu.make_async_copy(source, target, sems.at[index])
-        for index, (source, target) in enumerate(zip(sources, refs[12:-2]))
+        for index, (source, target) in enumerate(zip(sources, refs[12:-4]))
     ]
     for copy in copies:
         copy.start()
     here = lax.axis_index("slab")
     _, slab_a, slab_b = partners_of(here)
     blocks = state.shape[0] - 1
-    swap_a[...] = jnp.zeros_like(swap_a)
-    swap_b[...] = jnp.zeros_like(swap_b)
+    leave_a[...] = jnp.zeros_like(leave_a)
+    leave_b[...] = jnp.zeros_like(leave_b)
     for copy in copies:
         copy.wait()
     count_a = jnp.int32(0)
@@ -79,24 +81,18 @@
         moving[block, 9:10, :] = size[block : block + 1, :]
         moving[block, 10:11, :] = wet[block : block + 1, :]
         moving[block, 11:16, :] = jnp.full((5, LANES), (target + 1).astype(f32), f32)
-        slab = target // blocks
+        slab = lax.div(target, blocks)
         goes_a = slab == slab_a
         goes_b = slab == slab_b
 
-        @pl.when(slab == here)
-        def _():
-            state[target % blocks] = moving[block]
-
-        @pl.when(goes_a)
-        def _():
-            swap_a[count_a] = moving[block]
-
-        @pl.when(goes_b)
-        def _():
-            swap_b[count_b] = moving[block]
-
+        tile = moving[block]
+        state[jnp.where(slab == here, lax.rem(target, blocks), blocks)] = tile
+        leave_a[jnp.where(goes_a, count_a, CAP)] = tile
+        leave_b[jnp.where(goes_b, count_b, CAP)] = tile
         count_a = jnp.minimum(count_a + goes_a.astype(jnp.int32), CAP - 1)
         count_b = jnp.minimum(count_b + goes_b.astype(jnp.int32), CAP - 1)
+    swap_a[...] = leave_a[0:CAP]
+    swap_b[...] = leave_b[0:CAP]
     state[blocks] = jnp.zeros((ROWS, LANES), f32)
     tiles = rows.shape[1] // LANES
     for which in range(3):
@@ -120,7 +116,7 @@
     return row.astype(jnp.int32)
 
 
-def place_kernel(state, low, high, _, to_a, to_b, to_sub):
+def place_kernel(state, low, high, _, to_a, to_b, to_sub, lean):
     here = lax.axis_index("slab")
     odd, _, _ = partners_of(here)
     blocks = state.shape[0] - 1
@@ -136,6 +132,7 @@
         to_sub[slot] = current
         to_a[slot] = current
         to_b[slot] = current
+        lean[slot * LEAN : (slot + 1) * LEAN, :] = current[0:LEAN]
 
     flat = to_sub[0:blocks].reshape(blocks * ROWS, LANES)
     left = jnp.concatenate(split(flat, 3), axis=1)
@@ -150,7 +147,11 @@
             for block in range(blocks):
                 total = jnp.where(source == block, picked[block * ROWS : (block + 1) * ROWS], total)
             message[blocks + tile] = total
+            if which == 2:
+                start = (blocks + tile) * LEAN
+                lean[start : start + LEAN, :] = total[0:LEAN]
         message[blocks, 11:14, :] = extra[12:15, :]
+    lean[(blocks + size) * LEAN :, :] = extra[8:16, :]
 
 
 def cross(first, second):
@@ -370,8 +371,8 @@
     return shift.astype(jnp.uint32) < jnp.uint32(size)
 
 
-def list_far(count, message, heard, number, theirs, ours, ghost, blocks, todo):
-    size = message.shape[0] - blocks
+def list_far(count, heard, number, theirs, ours, ghost, blocks, todo):
+    size = GHOST_TILES
     for tile in range(blocks):
         for which in range(CHOICES):
             shift = heard[which, tile] - theirs
@@ -385,22 +386,19 @@
     return count
 
 
-def hear(messages, blocks, codes, heard, sem):
-    for number, message in enumerate(messages):
-        codes[number * CHOICES : (number + 1) * CHOICES, :] = message[
-            blocks, 11 : 11 + CHOICES, :
-        ].astype(jnp.int32)
+def hear(rows, codes, heard, sem):
+    for number, pair in enumerate(rows):
+        codes[number * CHOICES : (number + 1) * CHOICES, :] = pair.astype(jnp.int32)
     copy = pltpu.make_async_copy(codes, heard, sem)
     copy.start()
     return copy
 
 
-def list_all(messages, places, heard, todo):
-    blocks = messages[0].shape[0] - GHOST_TILES
+def list_all(places, blocks, heard, todo):
     count = jnp.int32(0)
     ends = [count]
-    for number, (message, (theirs, ours, ghost)) in enumerate(zip(messages, places)):
-        count = list_far(count, message, heard, number, theirs, ours, ghost, blocks, todo)
+    for number, (theirs, ours, ghost) in enumerate(places):
+        count = list_far(count, heard, number, theirs, ours, ghost, blocks, todo)
         ends.append(count)
     return ends
 
@@ -411,7 +409,12 @@
     for number, message in enumerate(messages):
 
         def pick(index, carry, message=message):
-            picked[index] = scale(message[todo[index] % 64])
+            slot = lax.rem(todo[index], 64)
+            if len(message.shape) == 3:
+                tile = message[slot]
+            else:
+                tile = message[pl.ds(slot * LEAN, LEAN), :]
+            picked[index] = scale(tile)
             return carry
 
         lax.fori_loop(ends[number], ends[number + 1], pick, 0)
@@ -451,7 +454,8 @@
     size = GHOST_TILES
     blocks = own_tiles - size
     codes[7:8, :] = to_sub[blocks, 13:14, :].astype(jnp.int32)
-    copy = hear([to_sub, from_a, from_b], blocks, codes, heard, sem)
+    rows = [message[blocks, 11:13, :] for message in (to_sub, from_a, from_b)]
+    copy = hear(rows, codes, heard, sem)
     spare = tiles.shape[0] - 1
 
     def enter(slot, tile):
@@ -475,7 +479,7 @@
     odd, _, _ = partners_of(lax.axis_index("slab"))
     low, high = blocks + odd * size, blocks + (1 - odd) * size
     places = [(high, low, own_tiles), (low, high, own_tiles + size)]
-    ends = list_all([from_a, from_b], places, heard, far_todo)
+    ends = list_all(places, blocks, heard, far_todo)
     news = jnp.int32(0)
     for slot in range(blocks):
         new[news] = slot
@@ -530,17 +534,19 @@
     buffers = rest[-2 * GROUP :]
     size = GHOST_TILES
     blocks = state.shape[0] - size
-    copy = hear([state, *messages], blocks, codes, heard, sem)
+    last = (blocks + size) * LEAN + 4
+    rows = [state[blocks, 11:13, :]] + [message[last : last + 2, :] for message in messages]
+    copy = hear(rows, codes, heard, sem)
     fill_spread(spread)
     copy.wait()
     sums[...] = jnp.zeros_like(sums)
     sub = lax.axis_index("sub")
     ours = blocks + (2 + sub) * size
     places = [
-        (blocks + (2 + lax.bitwise_xor(sub, number + 1)) * size, ours, blocks)
+        (blocks + (2 + lax.bitwise_xor(sub, len(messages) - number)) * size, ours, blocks)
         for number in range(len(messages))
     ]
-    ends = list_all(messages, places, heard, todo)
+    ends = list_all(places, blocks, heard, todo)
     far_pairs(messages, ends, tiles, sums, spread, picked, todo, buffers)
     for group in range(tiles.shape[0] // 8):
         for row, value in enumerate(finish(group, sums, tiles)):
@@ -624,6 +630,8 @@
             pltpu.VMEM((1, blocks), jnp.int32),
             pltpu.VMEM((1, blocks), jnp.int32),
             pltpu.VMEM((blocks, ROWS, LANES), f32),
+            pltpu.VMEM((CAP + 1, ROWS, LANES), f32),
+            pltpu.VMEM((CAP + 1, ROWS, LANES), f32),
             pltpu.SemaphoreType.DMA((9,)),
         ],
         compiler_params=pltpu.CompilerParams(vmem_limit_bytes=60 * 1024 * 1024),
@@ -653,18 +661,20 @@
         cost_estimate=pl.CostEstimate(flops=4000000, bytes_accessed=1000000, transcendentals=0),
         name="early",
     )(state)
-    to_a, to_b, to_sub = pl.pallas_call(
+    to_a, to_b, to_sub, lean = pl.pallas_call(
         place_kernel,
-        out_shape=(shape(blocks + size, ROWS, LANES),) * 3,
+        out_shape=(shape(blocks + size, ROWS, LANES),) * 3
+        + (shape((blocks + size) * LEAN + 8, LANES),),
         in_specs=[VMEM] * 3 + [pl.BlockSpec(memory_space=pl.ANY)],
-        out_specs=(VMEM,) * 3,
+        out_specs=(VMEM,) * 4,
         compiler_params=PARAMS,
         name="place",
     )(state, low, high, early[0])
     from_a = lax.ppermute(to_a, "slab", inside)
     from_b = lax.ppermute(to_b, "slab", across)
     from_sub = [
-        lax.ppermute(to_sub, "sub", [(i, i ^ d) for i in range(subs)]) for d in range(1, subs)
+        lax.ppermute(lean, "sub", [(i, i ^ d) for i in range(subs)])
+        for d in reversed(range(1, subs))
     ]
 
     wides = [pltpu.VMEM((LANES, (len(WIDE_ROWS) + 2) * LANES), f32)] * GROUP

time: 51.3 us -> 51.9 us (1.012)
  the two profiles are of different devices: /device:TPU:66 before, /device:TPU:8 now
where the time goes in v7:
time: 51.9 us; the launch traced here: 51.6 us
  starting transfers between devices  25 us (48%)
  Pallas kernels  24.4 us (47%)
  local copies, waits for them, and re-layouts  0.95 us (2%)
  between operations  0.77 us (1%)
    pallas_call x1, Pallas kernels, body(): pl.pallas_call(slab_kernel, out_shape=(shape(tiles * 8, LANES), shape(til...  13.3 us
    ppermute x3, starting transfers between devices, body(): lax.ppermute(lean, 'sub', [(i, i ^ d) for i in range(subs)])  9.82 us
    ppermute x1, starting transfers between devices, body(): high = lax.ppermute(swap_b, 'slab', across)  7.83 us
    pallas_call x1, Pallas kernels, body(): pl.pallas_call(sub_kernel, out_shape=(shape(3, per_dev), shape(3, per_dev...  7.04 us
    ppermute x1, starting transfers between devices, body(): from_b = lax.ppermute(to_b, 'slab', across)  3.55 us
    pallas_call x1, Pallas kernels, body(): pl.pallas_call(pack_kernel, out_shape=(shape(blocks + 1, ROWS, LANES), sh...  2.17 us
    ppermute x1, starting transfers between devices, body(): from_a = lax.ppermute(to_a, 'slab', inside)  1.92 us
    ppermute x1, starting transfers between devices, body(): low = lax.ppermute(swap_a, 'slab', inside)  1.92 us
  transfers between devices with their start and end apart: 7, of which 1 were waited for; matrix products, arithmetic and copies ran while one was open for 0% of the time, Pallas kernels for 27%

profile of v7, /device:TPU:8, one launch (start us, length us, event | category | flops | bytes accessed | tf_op | source)
XLA Modules:
  0.0 51.6 jit_solution(7215000236922054045)
XLA Ops:
  0.6 2.2 %pack.1 = (f32[33,16,128]{2,1,0:T(8,128)}, f32[4,16,128]{2,1,0:T(8,128)}, f32[4,16,128]{2,1,0:T(8,128)}) custom-call(s32[32]{0:T(128)} %refs_0_.1, f32[3,4096]{1,0:T(4,128)} %refs_1_.1, f32[6,4096]{1,0:T(8,128)} %refs_2_.1, f32[32,128]{1,0:T(8,128)} %bitcast.4, f32[32,128]{1,0:T(8,128)} %bitcast.5, s32[3,512]{1,0:T(4,128)} %refs_5_.1, s32[2,32]{1,0:T(2,128)} %refs_6_.1, ...), custom_call_target="tpu_custom_call" | custom-call | tf_op jit(solution)/shard_map/pack/pallas_call | solution.py:613
  2.8 1.9 %collective-permute-start = (f32[4,16,128]{2,1,0:T(8,128)}, f32[4,16,128]{2,1,0:T(8,128)S(1)}, u32[]{:S(2)}, u32[]{:S(2)}) collective-permute-start(f32[4,16,128]{2,1,0:T(8,128)} %get-tuple-element.15), channel_id=1, source_target_pairs={{0,4},{4,0},{8,12},{12,8},{16,20},{20,16},{24,28},{28,24},{32,36},... | collective-permute-start | bytes 98312 | tf_op jit(solution)/shard_map/ppermute | solution.py:650
  4.7 7.8 %collective-permute-start.1 = (f32[4,16,128]{2,1,0:T(8,128)}, f32[4,16,128]{2,1,0:T(8,128)S(1)}, u32[]{:S(2)}, u32[]{:S(2)}) collective-permute-start(f32[4,16,128]{2,1,0:T(8,128)} %get-tuple-element.16), channel_id=1, source_target_pairs={{4,8},{8,4},{12,16},{16,12},{20,24},{24,20},{28,32},{32,28},{36,40... | collective-permute-start | bytes 98312 | tf_op jit(solution)/shard_map/ppermute | solution.py:651
  12.6 0.0 copy-start
  12.6 0.9 %copy-done = f32[33,16,128]{2,1,0:T(8,128)S(1)} copy-done((f32[33,16,128]{2,1,0:T(8,128)S(1)}, f32[33,16,128]{2,1,0:T(8,128)}, u32[]{:S(2)}) %copy-start) | copy-done | bytes 270360
  13.5 0.5 early.1
  14.0 0.0 collective-permute-done.low
  14.0 0.4 collective-permute-done.1.high
  14.5 1.5 %place.1 = (f32[36,16,128]{2,1,0:T(8,128)S(1)}, f32[36,16,128]{2,1,0:T(8,128)S(1)}, f32[36,16,128]{2,1,0:T(8,128)S(1)}, f32[440,128]{1,0:T(8,128)S(1)}) custom-call(f32[33,16,128]{2,1,0:T(8,128)S(1)} %copy-done, f32[4,16,128]{2,1,0:T(8,128)S(1)} %collective-permute-done.low, f32[4,16,128]{2,1,0:T(8,128)S(1)} %collective-permute-done.1.high, ...), custom_call_target="tpu_custom_call" | custom-call | tf_op jit(solution)/shard_map/place/pallas_call | solution.py:664
  15.9 1.9 %collective-permute-start.2 = (f32[36,16,128]{2,1,0:T(8,128)S(1)}, f32[36,16,128]{2,1,0:T(8,128)S(1)}, u32[]{:S(2)}, u32[]{:S(2)}) collective-permute-start(f32[36,16,128]{2,1,0:T(8,128)S(1)} %get-tuple-element.18.to_a), channel_id=1, source_target_pairs={{0,4},{4,0},{8,12},{12,8},{16,20},{20,16},{24,28},{28,24},{32,36},... | collective-permute-start | bytes 884744 | tf_op jit(solution)/shard_map/ppermute | solution.py:673
  17.9 3.5 %collective-permute-start.3 = (f32[36,16,128]{2,1,0:T(8,128)S(1)}, f32[36,16,128]{2,1,0:T(8,128)S(1)}, u32[]{:S(2)}, u32[]{:S(2)}) collective-permute-start(f32[36,16,128]{2,1,0:T(8,128)S(1)} %get-tuple-element.19.to_b), channel_id=1, source_target_pairs={{4,8},{8,4},{12,16},{16,12},{20,24},{24,20},{28,32},{32,28},{36,40... | collective-permute-start | bytes 884744 | tf_op jit(solution)/shard_map/ppermute | solution.py:674
  21.4 1.9 %collective-permute-start.4 = (f32[440,128]{1,0:T(8,128)S(1)}, f32[440,128]{1,0:T(8,128)S(1)}, u32[]{:S(2)}, u32[]{:S(2)}) collective-permute-start(f32[440,128]{1,0:T(8,128)S(1)} %get-tuple-element.24), channel_id=1, source_target_pairs={{0,3},{1,2},{2,1},{3,0},{4,7},{5,6},{6,5},{7,4},{8,11},{9,10},{10,... | collective-permute-start | bytes 675848 | tf_op jit(solution)/shard_map/ppermute | solution.py:676
  23.3 1.9 %collective-permute-start.5 = (f32[440,128]{1,0:T(8,128)S(1)}, f32[440,128]{1,0:T(8,128)S(1)}, u32[]{:S(2)}, u32[]{:S(2)}) collective-permute-start(f32[440,128]{1,0:T(8,128)S(1)} %get-tuple-element.24), channel_id=1, source_target_pairs={{0,2},{1,3},{2,0},{3,1},{4,6},{5,7},{6,4},{7,5},{8,10},{9,11},{10,... | collective-permute-start | bytes 675848 | tf_op jit(solution)/shard_map/ppermute | solution.py:676
  25.3 6.0 %collective-permute-start.6 = (f32[440,128]{1,0:T(8,128)S(1)}, f32[440,128]{1,0:T(8,128)S(1)}, u32[]{:S(2)}, u32[]{:S(2)}) collective-permute-start(f32[440,128]{1,0:T(8,128)S(1)} %get-tuple-element.24), channel_id=1, source_target_pairs={{0,1},{1,0},{2,3},{3,2},{4,5},{5,4},{6,7},{7,6},{8,9},{9,8},{10,11... | collective-permute-start | bytes 675848 | tf_op jit(solution)/shard_map/ppermute | solution.py:676
  31.3 0.0 collective-permute-done.2.from_a
  31.3 0.0 collective-permute-done.3.from_b
  31.3 13.3 %slab_pairs.1 = (f32[384,128]{1,0:T(8,128)S(1)}, f32[48,48,128]{2,1,0:T(8,128)S(1)}) custom-call(f32[36,16,128]{2,1,0:T(8,128)S(1)} %get-tuple-element.18.to_a, f32[36,16,128]{2,1,0:T(8,128)S(1)} %get-tuple-element.19.to_b, f32[36,16,128]{2,1,0:T(8,128)S(1)} %get-tuple-element.20.to_sub.state, f32[36,16,128]{2,1,0:T(8,128)S(1)} %collective-permute-done.2.from_a, ...), custom_call_target="tpu_custom_call" | custom-call | flops 90000000 | bytes 400000 | tf_op jit(solution)/shard_map/slab_pairs/pallas_call | solution.py:694
  44.6 0.0 collective-permute-done.4.rest_0_
  44.6 0.0 collective-permute-done.5.rest_1_
  44.6 0.0 collective-permute-done.6.rest_2_
  44.6 7.0 %sub_pairs.1 = (f32[3,4096]{1,0:T(4,128)}, f32[3,4096]{1,0:T(4,128)}, f32[6,4096]{1,0:T(8,128)}) custom-call(f32[384,128]{1,0:T(8,128)S(1)} %get-tuple-element.22.before, f32[48,48,128]{2,1,0:T(8,128)S(1)} %get-tuple-element.23.tiles, f32[36,16,128]{2,1,0:T(8,128)S(1)} %get-tuple-element.20.to_sub.state, f32[33,16,128]{2,1,0:T(8,128)S(1)} %copy-done, ...), custom_call_target="tpu_custom_call" | custom-call | tf_op jit(solution)/shard_map/sub_pairs/pallas_call | solution.py:710
Async XLA Ops:
  2.8 11.2 %collective-permute-start = (f32[4,16,128]{2,1,0:T(8,128)}, f32[4,16,128]{2,1,0:T(8,128)S(1)}, u32[]{:S(2)}, u32[]{:S(2)}) collective-permute-start(f32[4,16,128]{2,1,0:T(8,128)} %get-tuple-element.15), channel_id=1, source_target_pairs={{0,4},{4,0},{8,12},{12,8},{16,20},{20,16},{24,28},{28,24},{32,36},... | collective-permute-start | bytes 98312 | tf_op jit(solution)/shard_map/ppermute | solution.py:650
  4.7 9.7 %collective-permute-start.1 = (f32[4,16,128]{2,1,0:T(8,128)}, f32[4,16,128]{2,1,0:T(8,128)S(1)}, u32[]{:S(2)}, u32[]{:S(2)}) collective-permute-start(f32[4,16,128]{2,1,0:T(8,128)} %get-tuple-element.16), channel_id=1, source_target_pairs={{4,8},{8,4},{12,16},{16,12},{20,24},{24,20},{28,32},{32,28},{36,40... | collective-permute-start | bytes 98312 | tf_op jit(solution)/shard_map/ppermute | solution.py:651
  12.6 1.0 %copy-start = (f32[33,16,128]{2,1,0:T(8,128)S(1)}, f32[33,16,128]{2,1,0:T(8,128)}, u32[]{:S(2)}) copy-start(f32[33,16,128]{2,1,0:T(8,128)} %get-tuple-element.14.state.extra) | copy-start | bytes 811012
  15.9 15.3 %collective-permute-start.2 = (f32[36,16,128]{2,1,0:T(8,128)S(1)}, f32[36,16,128]{2,1,0:T(8,128)S(1)}, u32[]{:S(2)}, u32[]{:S(2)}) collective-permute-start(f32[36,16,128]{2,1,0:T(8,128)S(1)} %get-tuple-element.18.to_a), channel_id=1, source_target_pairs={{0,4},{4,0},{8,12},{12,8},{16,20},{20,16},{24,28},{28,24},{32,36},... | collective-permute-start | bytes 884744 | tf_op jit(solution)/shard_map/ppermute | solution.py:673
  17.9 13.4 %collective-permute-start.3 = (f32[36,16,128]{2,1,0:T(8,128)S(1)}, f32[36,16,128]{2,1,0:T(8,128)S(1)}, u32[]{:S(2)}, u32[]{:S(2)}) collective-permute-start(f32[36,16,128]{2,1,0:T(8,128)S(1)} %get-tuple-element.19.to_b), channel_id=1, source_target_pairs={{4,8},{8,4},{12,16},{16,12},{20,24},{24,20},{28,32},{32,28},{36,40... | collective-permute-start | bytes 884744 | tf_op jit(solution)/shard_map/ppermute | solution.py:674
  21.4 23.1 %collective-permute-start.4 = (f32[440,128]{1,0:T(8,128)S(1)}, f32[440,128]{1,0:T(8,128)S(1)}, u32[]{:S(2)}, u32[]{:S(2)}) collective-permute-start(f32[440,128]{1,0:T(8,128)S(1)} %get-tuple-element.24), channel_id=1, source_target_pairs={{0,3},{1,2},{2,1},{3,0},{4,7},{5,6},{6,5},{7,4},{8,11},{9,10},{10,... | collective-permute-start | bytes 675848 | tf_op jit(solution)/shard_map/ppermute | solution.py:676
  23.3 21.2 %collective-permute-start.5 = (f32[440,128]{1,0:T(8,128)S(1)}, f32[440,128]{1,0:T(8,128)S(1)}, u32[]{:S(2)}, u32[]{:S(2)}) collective-permute-start(f32[440,128]{1,0:T(8,128)S(1)} %get-tuple-element.24), channel_id=1, source_target_pairs={{0,2},{1,3},{2,0},{3,1},{4,6},{5,7},{6,4},{7,5},{8,10},{9,11},{10,... | collective-permute-start | bytes 675848 | tf_op jit(solution)/shard_map/ppermute | solution.py:676
  25.3 19.3 %collective-permute-start.6 = (f32[440,128]{1,0:T(8,128)S(1)}, f32[440,128]{1,0:T(8,128)S(1)}, u32[]{:S(2)}, u32[]{:S(2)}) collective-permute-start(f32[440,128]{1,0:T(8,128)S(1)} %get-tuple-element.24), channel_id=1, source_target_pairs={{0,1},{1,0},{2,3},{3,2},{4,5},{5,4},{6,7},{7,6},{8,9},{9,8},{10,11... | collective-permute-start | bytes 675848 | tf_op jit(solution)/shard_map/ppermute | solution.py:676

commit v8 on v7

--- a/solution.py
+++ b/solution.py
@@ -669,7 +669,7 @@
         out_specs=(VMEM,) * 4,
         compiler_params=PARAMS,
         name="place",
-    )(state, low, high, early[0])
+    )(state, high, low, early[0])
     from_a = lax.ppermute(to_a, "slab", inside)
     from_b = lax.ppermute(to_b, "slab", across)
     from_sub = [

time: 51.9 us -> 50 us (0.963)
  the two profiles are of different devices: /device:TPU:8 before, /device:TPU:249 now
where the time goes in v8:
time: 50 us; the launch traced here: 50.1 us
  Pallas kernels  25.2 us (50%)
  starting transfers between devices  22.8 us (46%)
  local copies, waits for them, and re-layouts  0.95 us (2%)
  between operations  0.76 us (2%)
    pallas_call x1, Pallas kernels, body(): pl.pallas_call(slab_kernel, out_shape=(shape(tiles * 8, LANES), shape(til...  13.4 us
    ppermute x3, starting transfers between devices, body(): lax.ppermute(lean, 'sub', [(i, i ^ d) for i in range(subs)])  8.98 us
    pallas_call x1, Pallas kernels, body(): pl.pallas_call(sub_kernel, out_shape=(shape(3, per_dev), shape(3, per_dev...  7.72 us
    ppermute x1, starting transfers between devices, body(): high = lax.ppermute(swap_b, 'slab', across)  4.98 us
    ppermute x1, starting transfers between devices, body(): from_b = lax.ppermute(to_b, 'slab', across)  4.86 us
    pallas_call x1, Pallas kernels, body(): pl.pallas_call(pack_kernel, out_shape=(shape(blocks + 1, ROWS, LANES), sh...  2.17 us
    ppermute x1, starting transfers between devices, body(): from_a = lax.ppermute(to_a, 'slab', inside)  2.03 us
    ppermute x1, starting transfers between devices, body(): low = lax.ppermute(swap_a, 'slab', inside)  1.92 us
  transfers between devices with their start and end apart: 7, of which 1 were waited for; matrix products, arithmetic and copies ran while one was open for 0% of the time, Pallas kernels for 28%

profile of v8, /device:TPU:249, one launch (start us, length us, event | category | flops | bytes accessed | tf_op | source)
XLA Modules:
  0.0 50.1 jit_solution(14334722509478886735)
XLA Ops:
  0.6 2.2 %pack.1 = (f32[33,16,128]{2,1,0:T(8,128)}, f32[4,16,128]{2,1,0:T(8,128)}, f32[4,16,128]{2,1,0:T(8,128)}) custom-call(s32[32]{0:T(128)} %refs_0_.1, f32[3,4096]{1,0:T(4,128)} %refs_1_.1, f32[6,4096]{1,0:T(8,128)} %refs_2_.1, f32[32,128]{1,0:T(8,128)} %bitcast.4, f32[32,128]{1,0:T(8,128)} %bitcast.5, s32[3,512]{1,0:T(4,128)} %refs_5_.1, s32[2,32]{1,0:T(2,128)} %refs_6_.1, ...), custom_call_target="tpu_custom_call" | custom-call | tf_op jit(solution)/shard_map/pack/pallas_call | solution.py:613
  2.8 5.0 %collective-permute-start = (f32[4,16,128]{2,1,0:T(8,128)}, f32[4,16,128]{2,1,0:T(8,128)S(1)}, u32[]{:S(2)}, u32[]{:S(2)}) collective-permute-start(f32[4,16,128]{2,1,0:T(8,128)} %get-tuple-element.15), channel_id=1, source_target_pairs={{4,8},{8,4},{12,16},{16,12},{20,24},{24,20},{28,32},{32,28},{36,40... | collective-permute-start | bytes 98312 | tf_op jit(solution)/shard_map/ppermute | solution.py:651
  7.8 1.9 %collective-permute-start.1 = (f32[4,16,128]{2,1,0:T(8,128)}, f32[4,16,128]{2,1,0:T(8,128)S(1)}, u32[]{:S(2)}, u32[]{:S(2)}) collective-permute-start(f32[4,16,128]{2,1,0:T(8,128)} %get-tuple-element.16), channel_id=1, source_target_pairs={{0,4},{4,0},{8,12},{12,8},{16,20},{20,16},{24,28},{28,24},{32,36},... | collective-permute-start | bytes 98312 | tf_op jit(solution)/shard_map/ppermute | solution.py:650
  9.7 0.0 copy-start
  9.7 0.9 %copy-done = f32[33,16,128]{2,1,0:T(8,128)S(1)} copy-done((f32[33,16,128]{2,1,0:T(8,128)S(1)}, f32[33,16,128]{2,1,0:T(8,128)}, u32[]{:S(2)}) %copy-start) | copy-done | bytes 270360
  10.7 0.5 %early.1 = (f32[32,48,128]{2,1,0:T(8,128)S(1)}, bf16[32,48,128]{2,1,0:T(8,128)(2,1)S(1)}) custom-call(f32[33,16,128]{2,1,0:T(8,128)S(1)} %copy-done), custom_call_target="tpu_custom_call" | custom-call | flops 4000000 | bytes 1000000 | tf_op jit(solution)/shard_map/early/pallas_call | solution.py:652
  11.2 0.4 collective-permute-done.low
  11.6 0.0 collective-permute-done.1.high
  11.6 1.5 %place.1 = (f32[36,16,128]{2,1,0:T(8,128)S(1)}, f32[36,16,128]{2,1,0:T(8,128)S(1)}, f32[36,16,128]{2,1,0:T(8,128)S(1)}, f32[440,128]{1,0:T(8,128)S(1)}) custom-call(f32[33,16,128]{2,1,0:T(8,128)S(1)} %copy-done, f32[4,16,128]{2,1,0:T(8,128)S(1)} %collective-permute-done.low, f32[4,16,128]{2,1,0:T(8,128)S(1)} %collective-permute-done.1.high, ...), custom_call_target="tpu_custom_call" | custom-call | tf_op jit(solution)/shard_map/place/pallas_call | solution.py:664
  13.0 2.0 %collective-permute-start.2 = (f32[36,16,128]{2,1,0:T(8,128)S(1)}, f32[36,16,128]{2,1,0:T(8,128)S(1)}, u32[]{:S(2)}, u32[]{:S(2)}) collective-permute-start(f32[36,16,128]{2,1,0:T(8,128)S(1)} %get-tuple-element.18.to_a), channel_id=1, source_target_pairs={{0,4},{4,0},{8,12},{12,8},{16,20},{20,16},{24,28},{28,24},{32,36},... | collective-permute-start | bytes 884744 | tf_op jit(solution)/shard_map/ppermute | solution.py:673
  15.1 4.9 %collective-permute-start.3 = (f32[36,16,128]{2,1,0:T(8,128)S(1)}, f32[36,16,128]{2,1,0:T(8,128)S(1)}, u32[]{:S(2)}, u32[]{:S(2)}) collective-permute-start(f32[36,16,128]{2,1,0:T(8,128)S(1)} %get-tuple-element.19.to_b), channel_id=1, source_target_pairs={{4,8},{8,4},{12,16},{16,12},{20,24},{24,20},{28,32},{32,28},{36,40... | collective-permute-start | bytes 884744 | tf_op jit(solution)/shard_map/ppermute | solution.py:674
  20.0 4.4 %collective-permute-start.4 = (f32[440,128]{1,0:T(8,128)S(1)}, f32[440,128]{1,0:T(8,128)S(1)}, u32[]{:S(2)}, u32[]{:S(2)}) collective-permute-start(f32[440,128]{1,0:T(8,128)S(1)} %get-tuple-element.24), channel_id=1, source_target_pairs={{0,3},{1,2},{2,1},{3,0},{4,7},{5,6},{6,5},{7,4},{8,11},{9,10},{10,... | collective-permute-start | bytes 675848 | tf_op jit(solution)/shard_map/ppermute | solution.py:676
  24.3 2.4 %collective-permute-start.5 = (f32[440,128]{1,0:T(8,128)S(1)}, f32[440,128]{1,0:T(8,128)S(1)}, u32[]{:S(2)}, u32[]{:S(2)}) collective-permute-start(f32[440,128]{1,0:T(8,128)S(1)} %get-tuple-element.24), channel_id=1, source_target_pairs={{0,2},{1,3},{2,0},{3,1},{4,6},{5,7},{6,4},{7,5},{8,10},{9,11},{10,... | collective-permute-start | bytes 675848 | tf_op jit(solution)/shard_map/ppermute | solution.py:676
  26.8 2.2 %collective-permute-start.6 = (f32[440,128]{1,0:T(8,128)S(1)}, f32[440,128]{1,0:T(8,128)S(1)}, u32[]{:S(2)}, u32[]{:S(2)}) collective-permute-start(f32[440,128]{1,0:T(8,128)S(1)} %get-tuple-element.24), channel_id=1, source_target_pairs={{0,1},{1,0},{2,3},{3,2},{4,5},{5,4},{6,7},{7,6},{8,9},{9,8},{10,11... | collective-permute-start | bytes 675848 | tf_op jit(solution)/shard_map/ppermute | solution.py:676
  29.0 0.0 collective-permute-done.2.from_a
  29.0 0.0 collective-permute-done.3.from_b
  29.0 13.4 %slab_pairs.1 = (f32[384,128]{1,0:T(8,128)S(1)}, f32[48,48,128]{2,1,0:T(8,128)S(1)}) custom-call(f32[36,16,128]{2,1,0:T(8,128)S(1)} %get-tuple-element.18.to_a, f32[36,16,128]{2,1,0:T(8,128)S(1)} %get-tuple-element.19.to_b, f32[36,16,128]{2,1,0:T(8,128)S(1)} %get-tuple-element.20.to_sub.state, f32[36,16,128]{2,1,0:T(8,128)S(1)} %collective-permute-done.2.from_a, ...), custom_call_target="tpu_custom_call" | custom-call | flops 90000000 | bytes 400000 | tf_op jit(solution)/shard_map/slab_pairs/pallas_call | solution.py:694
  42.4 0.0 collective-permute-done.4.rest_0_
  42.4 0.0 collective-permute-done.5.rest_1_
  42.4 0.0 collective-permute-done.6.rest_2_
  42.4 7.7 %sub_pairs.1 = (f32[3,4096]{1,0:T(4,128)}, f32[3,4096]{1,0:T(4,128)}, f32[6,4096]{1,0:T(8,128)}) custom-call(f32[384,128]{1,0:T(8,128)S(1)} %get-tuple-element.22.before, f32[48,48,128]{2,1,0:T(8,128)S(1)} %get-tuple-element.23.tiles, f32[36,16,128]{2,1,0:T(8,128)S(1)} %get-tuple-element.20.to_sub.state, f32[33,16,128]{2,1,0:T(8,128)S(1)} %copy-done, ...), custom_call_target="tpu_custom_call" | custom-call | tf_op jit(solution)/shard_map/sub_pairs/pallas_call | solution.py:710
Async XLA Ops:
  2.8 8.8 %collective-permute-start = (f32[4,16,128]{2,1,0:T(8,128)}, f32[4,16,128]{2,1,0:T(8,128)S(1)}, u32[]{:S(2)}, u32[]{:S(2)}) collective-permute-start(f32[4,16,128]{2,1,0:T(8,128)} %get-tuple-element.15), channel_id=1, source_target_pairs={{4,8},{8,4},{12,16},{16,12},{20,24},{24,20},{28,32},{32,28},{36,40... | collective-permute-start | bytes 98312 | tf_op jit(solution)/shard_map/ppermute | solution.py:651
  7.8 3.8 %collective-permute-start.1 = (f32[4,16,128]{2,1,0:T(8,128)}, f32[4,16,128]{2,1,0:T(8,128)S(1)}, u32[]{:S(2)}, u32[]{:S(2)}) collective-permute-start(f32[4,16,128]{2,1,0:T(8,128)} %get-tuple-element.16), channel_id=1, source_target_pairs={{0,4},{4,0},{8,12},{12,8},{16,20},{20,16},{24,28},{28,24},{32,36},... | collective-permute-start | bytes 98312 | tf_op jit(solution)/shard_map/ppermute | solution.py:650
  9.7 1.0 %copy-start = (f32[33,16,128]{2,1,0:T(8,128)S(1)}, f32[33,16,128]{2,1,0:T(8,128)}, u32[]{:S(2)}) copy-start(f32[33,16,128]{2,1,0:T(8,128)} %get-tuple-element.14.state.extra) | copy-start | bytes 811012
  13.0 15.9 %collective-permute-start.2 = (f32[36,16,128]{2,1,0:T(8,128)S(1)}, f32[36,16,128]{2,1,0:T(8,128)S(1)}, u32[]{:S(2)}, u32[]{:S(2)}) collective-permute-start(f32[36,16,128]{2,1,0:T(8,128)S(1)} %get-tuple-element.18.to_a), channel_id=1, source_target_pairs={{0,4},{4,0},{8,12},{12,8},{16,20},{20,16},{24,28},{28,24},{32,36},... | collective-permute-start | bytes 884744 | tf_op jit(solution)/shard_map/ppermute | solution.py:673
  15.1 13.9 %collective-permute-start.3 = (f32[36,16,128]{2,1,0:T(8,128)S(1)}, f32[36,16,128]{2,1,0:T(8,128)S(1)}, u32[]{:S(2)}, u32[]{:S(2)}) collective-permute-start(f32[36,16,128]{2,1,0:T(8,128)S(1)} %get-tuple-element.19.to_b), channel_id=1, source_target_pairs={{4,8},{8,4},{12,16},{16,12},{20,24},{24,20},{28,32},{32,28},{36,40... | collective-permute-start | bytes 884744 | tf_op jit(solution)/shard_map/ppermute | solution.py:674
  20.0 22.4 %collective-permute-start.4 = (f32[440,128]{1,0:T(8,128)S(1)}, f32[440,128]{1,0:T(8,128)S(1)}, u32[]{:S(2)}, u32[]{:S(2)}) collective-permute-start(f32[440,128]{1,0:T(8,128)S(1)} %get-tuple-element.24), channel_id=1, source_target_pairs={{0,3},{1,2},{2,1},{3,0},{4,7},{5,6},{6,5},{7,4},{8,11},{9,10},{10,... | collective-permute-start | bytes 675848 | tf_op jit(solution)/shard_map/ppermute | solution.py:676
  24.3 18.0 %collective-permute-start.5 = (f32[440,128]{1,0:T(8,128)S(1)}, f32[440,128]{1,0:T(8,128)S(1)}, u32[]{:S(2)}, u32[]{:S(2)}) collective-permute-start(f32[440,128]{1,0:T(8,128)S(1)} %get-tuple-element.24), channel_id=1, source_target_pairs={{0,2},{1,3},{2,0},{3,1},{4,6},{5,7},{6,4},{7,5},{8,10},{9,11},{10,... | collective-permute-start | bytes 675848 | tf_op jit(solution)/shard_map/ppermute | solution.py:676
  26.8 15.6 %collective-permute-start.6 = (f32[440,128]{1,0:T(8,128)S(1)}, f32[440,128]{1,0:T(8,128)S(1)}, u32[]{:S(2)}, u32[]{:S(2)}) collective-permute-start(f32[440,128]{1,0:T(8,128)S(1)} %get-tuple-element.24), channel_id=1, source_target_pairs={{0,1},{1,0},{2,3},{3,2},{4,5},{5,4},{6,7},{7,6},{8,9},{9,8},{10,11... | collective-permute-start | bytes 675848 | tf_op jit(solution)/shard_map/ppermute | solution.py:676
